TPU v7x, 256 devices: a whole 4x4x8 slice. The times are simulated.
256 devices in a mesh: tile: 128 (over x_hi, y, z, core), member: 2 (over x_lo).
Axes of the slice: x: 4 (x_hi: 2, x_lo: 2; x = x_hi * 2 + x_lo), y: 4, z: 8, core: 2. Of those that a mesh axis runs over, the one named last changes fastest.
Arguments:
- states: bfloat16 [2, 128, 32, 32, 128], P('member', 'tile'), may hold values from -6 to 6
- cotangent: bfloat16 [2, 128, 32, 32, 128], P('member', 'tile'), may hold values from -6 to 6
- seam_codes: int32 [128, 4], replicated, may hold values from 0 to 7
- corner_codes: int32 [128, 4], replicated, may hold values from 0 to 4
- dw_kernel: float32 [2, 7, 7, 128], replicated, may hold values from -0.875 to 0.875
- dw_bias: float32 [2, 128], replicated, may hold values from -3 to 3
- norm_gain: float32 [2, 128], replicated, may hold values from 0.5 to 1.5
- norm_bias: float32 [2, 128], replicated, may hold values from -3 to 3
- up_weight: bfloat16 [2, 128, 512], replicated, may hold values from -0.5 to 0.5
- up_bias: float32 [2, 512], replicated, may hold values from -3 to 3
- down_weight: bfloat16 [2, 512, 128], replicated, may hold values from -0.25 to 0.25
- down_bias: float32 [2, 128], replicated, may hold values from -3 to 3
- layer_scale: float32 [2, 128], replicated, may hold values from 0.3 to 1
Outputs:
- out_states: bfloat16 [2, 128, 32, 32, 128], P('member', 'tile')
- input_grad: bfloat16 [2, 128, 32, 32, 128], P('member', 'tile')
- kernel_grad: float32 [2, 7, 7, 128], replicated
- conv_bias_grad: float32 [2, 128], replicated
- gain_grad: float32 [2, 128], replicated
- offset_grad: float32 [2, 128], replicated
- up_weight_grad: float32 [2, 128, 512], replicated
- up_bias_grad: float32 [2, 512], replicated
- down_weight_grad: float32 [2, 512, 128], replicated
- down_bias_grad: float32 [2, 128], replicated
- scale_grad: float32 [2, 128], replicated
Inputs may be any that keep to these rules, and one draw needn't show every extreme that they name: Tile t takes the strip of its neighbour in edge direction d from the neighbour's edge seam_codes[t, d] mod 4 (0 north, 1 south, 2 west, 3 east), reversed along the edge when the code is 4 or more. `corner_codes`: codes 0 to 3 name the neighbour's corner block (north-west, north-east, south-west, south-east) that fills tile t's corner slot d; 4 marks a corner where three faces meet, filled with zeros.
All inputs are finite; a program needn't handle non-finite values.
Results may differ from a plain program's by a relative error of at most 0.008.
Values may be sent and summed in bfloat16 or wider, within the bound.
No kernel may reach another device: no remote copies, remote signals or barrier semaphores. Data moves between devices by JAX's collectives and lax.ppermute only.
A program may use at most 128 MiB of HBM per device.

v0:
```python
import math

import jax
import jax.numpy as jnp
from jax import lax
from jax.sharding import PartitionSpec as P

ROW = 4
BLOCKS = 2


EPSILON = 1e-06
GELU_C = 0.7978845608028654
GELU_A = 0.044715


def passed_along(value, axis, steps):
    count = lax.axis_size(axis)
    pairs = [(source, (source + steps) % count) for source in range(count)]
    return lax.ppermute(value, axis, pairs)


def gelu_value(values):
    inner = GELU_C * (values + GELU_A * values * values * values)
    return 0.5 * values * (1.0 + jnp.tanh(inner))


def gelu_slope(values):
    inner = GELU_C * (values + GELU_A * values * values * values)
    tangent = jnp.tanh(inner)
    return 0.5 * (1.0 + tangent) + 0.5 * values * (1.0 - tangent * tangent) * GELU_C * (
        1.0 + 3.0 * GELU_A * values * values
    )


def edge_offsets():
    return (-ROW, ROW, -1, 1)


def corner_offsets():
    return (-ROW - 1, -ROW + 1, ROW - 1, ROW + 1)


def edge_strips(tile_field):
    north = tile_field[0:3]
    south = tile_field[-3:][::-1]
    west = jnp.transpose(tile_field[:, 0:3], (1, 0, 2))
    east = jnp.transpose(tile_field[:, -3:][:, ::-1], (1, 0, 2))
    return jnp.stack([north, south, west, east])


def corner_blocks(tile_field):
    return jnp.stack(
        [tile_field[0:3, 0:3], tile_field[0:3, -3:], tile_field[-3:, 0:3], tile_field[-3:, -3:]]
    )


def orient(strip_data, seam_code):
    return jnp.where(seam_code >= 4, strip_data[:, ::-1], strip_data)


def select_edge(edge_set, seam_code):
    chosen = lax.dynamic_index_in_dim(edge_set, seam_code % 4, 0, keepdims=False)
    return orient(chosen, seam_code)


def select_corner(block_set, corner_code):
    chosen = lax.dynamic_index_in_dim(block_set, jnp.minimum(corner_code, 3), 0, keepdims=False)
    return jnp.where(corner_code < 4, chosen, jnp.zeros_like(chosen))


def assemble(tile_field, edges, corners):
    top = jnp.concatenate([corners[0], edges[0][::-1], corners[1]], axis=1)
    middle = jnp.concatenate(
        [jnp.transpose(edges[2][::-1], (1, 0, 2)), tile_field, jnp.transpose(edges[3], (1, 0, 2))],
        axis=1,
    )
    bottom = jnp.concatenate([corners[2], edges[1], corners[3]], axis=1)
    return jnp.concatenate([top, middle, bottom], axis=0)


def split_rims(grad_pad):
    north = grad_pad[0:3, 3:-3][::-1]
    south = grad_pad[-3:, 3:-3]
    west = jnp.transpose(grad_pad[3:-3, 0:3], (1, 0, 2))[::-1]
    east = jnp.transpose(grad_pad[3:-3, -3:], (1, 0, 2))
    corners = [grad_pad[0:3, 0:3], grad_pad[0:3, -3:], grad_pad[-3:, 0:3], grad_pad[-3:, -3:]]
    return ([north, south, west, east], corners, grad_pad[3:-3, 3:-3])


def embed_rims(interior, edge_sum, corner_sum):
    size = interior.shape[0]
    result = interior
    result = result.at[0:3].add(edge_sum[0])
    result = result.at[size - 3 :].add(edge_sum[1][::-1])
    result = result.at[:, 0:3].add(jnp.transpose(edge_sum[2], (1, 0, 2)))
    result = result.at[:, size - 3 :].add(jnp.transpose(edge_sum[3], (1, 0, 2))[:, ::-1])
    result = result.at[0:3, 0:3].add(corner_sum[0])
    result = result.at[0:3, size - 3 :].add(corner_sum[1])
    result = result.at[size - 3 :, 0:3].add(corner_sum[2])
    result = result.at[size - 3 :, size - 3 :].add(corner_sum[3])
    return result


def depthwise(padded, kernel, bias):
    size = padded.shape[0] - 6
    wide = padded.astype(jnp.float32)
    total = jnp.zeros((size, size, padded.shape[2]), jnp.float32) + bias
    for row_tap in range(7):
        for col_tap in range(7):
            total = (
                total
                + wide[row_tap : row_tap + size, col_tap : col_tap + size]
                * kernel[row_tap, col_tap]
            )
    return total


def contract_rows(left, right):
    return lax.dot_general(
        left, right, (((0,), (0,)), ((), ())), preferred_element_type=jnp.float32
    )


def contract_cols(left, right):
    return lax.dot_general(
        left, right, (((1,), (1,)), ((), ())), preferred_element_type=jnp.float32
    )


def block_forward(padded, params):
    kernel, conv_bias, gain, offset_bias, up_w, up_b, down_w, down_b, scale = params
    size = padded.shape[0] - 6
    width = padded.shape[2]
    conv = depthwise(padded, kernel, conv_bias).reshape(size * size, width)
    centred = conv - jnp.mean(conv, axis=1, keepdims=True)
    inv_std = lax.rsqrt(jnp.mean(centred * centred, axis=1, keepdims=True) + EPSILON)
    standard = centred * inv_std
    normed = (standard * gain + offset_bias).astype(jnp.bfloat16)
    pre_act = jnp.dot(normed, up_w, preferred_element_type=jnp.float32) + up_b
    activated = gelu_value(pre_act).astype(jnp.bfloat16)
    branch = jnp.dot(activated, down_w, preferred_element_type=jnp.float32) + down_b
    residual_in = padded[3:-3, 3:-3].reshape(size * size, width).astype(jnp.float32)
    output = (residual_in + scale * branch).astype(jnp.bfloat16).reshape(size, size, width)
    return (output, (standard, inv_std, normed, pre_act, activated, branch))


def block_backward(padded, saved, upstream, params):
    kernel, conv_bias, gain, offset_bias, up_w, up_b, down_w, down_b, scale = params
    standard, inv_std, normed, pre_act, activated, branch = saved
    size = padded.shape[0] - 6
    width = padded.shape[2]
    scale_grad = jnp.sum(upstream * branch, axis=0)
    scaled = upstream * scale
    down_b_grad = jnp.sum(scaled, axis=0)
    scaled_b = scaled.astype(jnp.bfloat16)
    down_w_grad = contract_rows(activated, scaled_b)
    act_grad = contract_cols(scaled_b, down_w)
    pre_grad = act_grad * gelu_slope(pre_act)
    up_b_grad = jnp.sum(pre_grad, axis=0)
    pre_grad_b = pre_grad.astype(jnp.bfloat16)
    up_w_grad = contract_rows(normed, pre_grad_b)
    normed_grad = contract_cols(pre_grad_b, up_w)
    gain_grad = jnp.sum(normed_grad * standard, axis=0)
    offset_grad = jnp.sum(normed_grad, axis=0)
    std_grad = normed_grad * gain
    conv_grad = inv_std * (
        std_grad
        - jnp.mean(std_grad, axis=1, keepdims=True)
        - standard * jnp.mean(std_grad * standard, axis=1, keepdims=True)
    )
    conv_bias_grad = jnp.sum(conv_grad, axis=0)
    conv_field = conv_grad.reshape(size, size, width)
    wide = padded.astype(jnp.float32)
    kernel_rows = []
    for row_tap in range(7):
        kernel_cols = []
        for col_tap in range(7):
            kernel_cols.append(
                jnp.sum(
                    wide[row_tap : row_tap + size, col_tap : col_tap + size] * conv_field,
                    axis=(0, 1),
                )
            )
        kernel_rows.append(jnp.stack(kernel_cols))
    kernel_grad = jnp.stack(kernel_rows)
    grown = jnp.pad(conv_field, ((6, 6), (6, 6), (0, 0)))
    pad_grad = jnp.zeros((size + 6, size + 6, width), jnp.float32)
    for row_tap in range(7):
        for col_tap in range(7):
            pad_grad = (
                pad_grad
                + grown[6 - row_tap : 12 - row_tap + size, 6 - col_tap : 12 - col_tap + size]
                * kernel[row_tap, col_tap]
            )
    grads = (
        kernel_grad,
        conv_bias_grad,
        gain_grad,
        offset_grad,
        up_w_grad,
        up_b_grad,
        down_w_grad,
        down_b_grad,
        scale_grad,
    )
    return (pad_grad, grads)


def gather_halo(tile_field, seam_codes, corner_codes, here):
    edge_set = edge_strips(tile_field)
    block_set = corner_blocks(tile_field)
    edges = []
    corners = []
    for facing in range(4):
        offset = edge_offsets()[facing]
        arrived = passed_along(edge_set, "tile", -offset)
        edges.append(select_edge(arrived, seam_codes[here, facing]))
    for facing in range(4):
        offset = corner_offsets()[facing]
        arrived = passed_along(block_set, "tile", -offset)
        corners.append(select_corner(arrived, corner_codes[here, facing]))
    return assemble(tile_field, edges, corners)


def return_rims(pad_grad, seam_codes, corner_codes, here, tile_count):
    edges, corners, interior = split_rims(pad_grad)
    size = interior.shape[0]
    width = interior.shape[2]
    slots = jnp.arange(4, dtype=jnp.int32)
    edge_sum = jnp.zeros((4, 3, size, width), jnp.float32)
    corner_sum = jnp.zeros((4, 3, 3, width), jnp.float32)
    for facing in range(4):
        offset = edge_offsets()[facing]
        sent = orient(edges[facing], seam_codes[here, facing])
        arrived = passed_along(sent.astype(jnp.bfloat16), "tile", offset).astype(sent.dtype)
        source_code = seam_codes[(here - offset) % tile_count, facing]
        chosen = (slots == source_code % 4).astype(jnp.float32)
        edge_sum = edge_sum + chosen[:, None, None, None] * arrived[None]
    for facing in range(4):
        offset = corner_offsets()[facing]
        live = corner_codes[here, facing] < 4
        sent = jnp.where(live, corners[facing], jnp.zeros_like(corners[facing]))
        arrived = passed_along(sent, "tile", offset)
        source_code = corner_codes[(here - offset) % tile_count, facing]
        chosen = (slots == source_code).astype(jnp.float32)
        corner_sum = corner_sum + chosen[:, None, None, None] * arrived[None]
    return embed_rims(interior, edge_sum, corner_sum)


def body(
    states,
    cotangent,
    seam_codes,
    corner_codes,
    dw_kernel,
    dw_bias,
    norm_gain,
    norm_bias,
    up_weight,
    up_bias,
    down_weight,
    down_bias,
    layer_scale,
):
    tile_count = lax.axis_size("tile")
    member_count = lax.axis_size("member")
    here = lax.axis_index("tile")
    stacks = (
        dw_kernel,
        dw_bias,
        norm_gain,
        norm_bias,
        up_weight,
        up_bias,
        down_weight,
        down_bias,
        layer_scale,
    )
    current = states[0, 0]
    size = current.shape[0]
    width = current.shape[2]
    saved_blocks = []
    for block in range(BLOCKS):
        params = tuple((item[block] for item in stacks))
        padded = gather_halo(current, seam_codes, corner_codes, here)
        current, saved = block_forward(padded, params)
        saved_blocks.append((padded, saved))
    upstream = cotangent[0, 0].astype(jnp.float32).reshape(size * size, width)
    collected = [None] * BLOCKS
    for block in reversed(range(BLOCKS)):
        params = tuple((item[block] for item in stacks))
        padded, saved = saved_blocks[block]
        pad_grad, grads = block_backward(padded, saved, upstream, params)
        collected[block] = grads
        returned = return_rims(pad_grad, seam_codes, corner_codes, here, tile_count)
        upstream = upstream + returned.reshape(size * size, width)
    stacked = [jnp.stack([collected[block][kind] for block in range(BLOCKS)]) for kind in range(9)]
    stacked = lax.psum(
        (
            stacked[0],
            stacked[1],
            stacked[2],
            stacked[3],
            stacked[4],
            stacked[5],
            stacked[6],
            stacked[7],
            stacked[8],
        ),
        ("tile", "member"),
    )
    factor = 1.0 / math.sqrt(tile_count * member_count * size * size)
    final = [item * factor for item in stacked]
    grad_field = upstream.reshape(size, size, width).astype(jnp.bfloat16)
    return (
        current[None, None],
        grad_field[None, None],
        final[0],
        final[1],
        final[2],
        final[3],
        final[4],
        final[5],
        final[6],
        final[7],
        final[8],
    )


def solution(mesh):
    in_specs = (
        P("member", "tile", None, None, None),
        P("member", "tile", None, None, None),
        P(),
        P(),
        P(),
        P(),
        P(),
        P(),
        P(),
        P(),
        P(),
        P(),
        P(),
    )
    out_specs = (
        P("member", "tile", None, None, None),
        P("member", "tile", None, None, None),
        P(),
        P(),
        P(),
        P(),
        P(),
        P(),
        P(),
        P(),
        P(),
    )
    return jax.shard_map(body, mesh=mesh, in_specs=in_specs, out_specs=out_specs, check_vma=False)
```

profile of v0, /device:TPU:2, one launch (start us, length us, event | category | flops | bytes accessed | tf_op | source)
XLA Modules:
  0.0 606.4 jit_solution(115761085560191962)
XLA Ops:
  8.3 10.3 %collective-permute-start.7 = (bf16[4,3,3,128]{3,1,2,0:T(4,128)(2,1)S(1)}, bf16[4,3,3,128]{3,1,2,0:T(4,128)(2,1)S(1)}, u32[]{:S(2)}, u32[]{:S(2)}) collective-permute-start(bf16[4,3,3,128]{3,1,2,0:T(4,128)(2,1)S(1)} %pad_maximum_fusion.7), channel_id=1, source_target_pairs={{0,246},{2,248},{4,250},{6,252},{8,254},{10,0},{12,2},{14,4},{16,6... | collective-permute-start | bytes 27656 | tf_op jit(solution)/shard_map/ppermute | solution.py:20
  21.6 9.0 %collective-permute-start.6 = (bf16[4,3,32,128]{3,2,1,0:T(8,128)(2,1)S(1)}, bf16[4,3,32,128]{3,2,1,0:T(8,128)(2,1)S(1)}, u32[]{:S(2)}, u32[]{:S(2)}) collective-permute-start(bf16[4,3,32,128]{3,2,1,0:T(8,128)(2,1)S(1)} %pad_maximum_fusion.3), channel_id=1, source_target_pairs={{0,248},{2,250},{4,252},{6,254},{8,0},{10,2},{12,4},{14,6},{16,8},... | collective-permute-start | bytes 294920 | tf_op jit(solution)/shard_map/ppermute | solution.py:20
  30.6 1.7 constant_dynamic-slice_fusion.2
  55.3 2.2 fusion.207
  76.4 7.6 %collective-permute-done.3 = bf16[4,3,32,128]{3,2,1,0:T(8,128)(2,1)S(1)} collective-permute-done((bf16[4,3,32,128]{3,2,1,0:T(8,128)(2,1)S(1)}, bf16[4,3,32,128]{3,2,1,0:T(8,128)(2,1)S(1)}, u32[]{:S(2)}, u32[]{:S(2)}) %collective-permute-start.3) | collective-permute-done | bytes 98336 | tf_op jit(solution)/shard_map/ppermute | solution.py:20
  84.1 4.2 collective-permute-done.1
  88.6 4.4 fusion.273
  94.9 2.9 multiply_convert_fusion.1
  101.8 1.7 collective-permute-start.10
  103.5 4.7 collective-permute-start.8
  109.6 4.3 collective-permute-start.14
  115.0 2.6 collective-permute-start.9
  117.6 2.7 collective-permute-done.14
  120.4 1.7 collective-permute-done.12
  122.2 2.7 collective-permute-done.11
  125.0 4.0 collective-permute-done.9
  129.3 17.3 %fusion.272 = (f32[32,32]{1,0:T(8,128)S(1)}, f32[32,32,128]{2,1,0:T(8,128)S(1)}) fusion(f32[128]{0:T(128)S(1)} %get-tuple-element.444, f32[38,38,128]{2,1,0:T(8,128)S(1)} %maximum_convert_fusion.1, f32[128]{0:T(128)S(1)} %get-tuple-element.445, f32[128]{0:T(128)S(1)} %get-tuple-element.446, f32[128]{0:T(128)S(1)} %get-tuple-element.447, ...), kind=kLoop, calls=%fused_computation.789 | loop fusion | flops 12975104 | bytes 26244096 | tf_op jit(solution)/shard_map/reduce_sum | solution.py:136
  148.6 1.8 multiply_convert_fusion
  150.5 2.1 fusion.281
  152.6 1.9 multiply_reduce_fusion.1
  154.6 2.7 fusion.271
  161.8 6.8 %fusion.105 = f32[38,38,128]{2,0,1:T(8,128)S(1)} fusion(f32[32,32,128]{2,0,1:T(8,128)S(1)} %copy.343, f32[128]{0:T(128)S(1)} %get-tuple-element.444, f32[128]{0:T(128)S(1)} %get-tuple-element.445, f32[128]{0:T(128)S(1)} %get-tuple-element.446, f32[128]{0:T(128)S(1)} %get-tuple-element.447, f32[128]{0:T(128)S(1)} %get-tuple-element.448, ...), kind=kLoop, calls=%fused_computation.215 | loop fusion | flops 17928704 | bytes 1288704 | tf_op jit(solution)/shard_map/add | solution.py:192
  169.7 2.2 convolution_bitcast_fusion.2
  172.0 2.9 collective-permute-start.22
  174.9 5.5 collective-permute-start.21
  180.6 4.7 collective-permute-start.18
  189.3 6.7 %collective-permute-start.16 = (bf16[3,32,128]{2,0,1:T(4,128)(2,1)S(1)}, bf16[3,32,128]{2,0,1:T(4,128)(2,1)S(1)}, u32[]{:S(2)}, u32[]{:S(2)}) collective-permute-start(bf16[3,32,128]{2,0,1:T(4,128)(2,1)S(1)} %select_convert_fusion.1), channel_id=1, source_target_pairs={{0,248},{2,250},{4,252},{6,254},{8,0},{10,2},{12,4},{14,6},{16,8},... | collective-permute-start | bytes 73736 | tf_op jit(solution)/shard_map/ppermute | solution.py:20
  196.2 2.1 collective-permute-done.19
  198.4 8.3 %collective-permute-done.17 = bf16[3,32,128]{2,0,1:T(4,128)(2,1)S(1)} collective-permute-done((bf16[3,32,128]{2,0,1:T(4,128)(2,1)S(1)}, bf16[3,32,128]{2,0,1:T(4,128)(2,1)S(1)}, u32[]{:S(2)}, u32[]{:S(2)}) %collective-permute-start.17) | collective-permute-done | bytes 24608 | tf_op jit(solution)/shard_map/ppermute | solution.py:20
  211.2 1.9 add_select_fusion.1
  216.4 3.8 fusion.282
  220.2 2.3 multiply_reduce_fusion.2
  222.6 1.8 fusion.270
  225.6 1.7 multiply_reduce_fusion.70
  229.7 6.9 %fusion.202 = f32[38,38,128]{2,0,1:T(8,128)S(1)} fusion(f32[32,32,128]{2,0,1:T(8,128)S(1)} %get-tuple-element.416, f32[128]{0:T(128)S(1)} %copy-done.88, f32[128]{0:T(128)S(1)} %copy-done.90, f32[128]{0:T(128)S(1)} %copy-done.92, f32[128]{0:T(128)S(1)} %copy-done.94, f32[128]{0:T(128)S(1)} %copy-done.96, f32[128]{0:T(128)S(1)} %copy-done.98, ...), kind=kLoop, calls=%fused_computation.312 | loop fusion | flops 17928704 | bytes 1288704 | tf_op jit(solution)/shard_map/add | solution.py:192
  238.8 2.2 multiply_reduce_fusion
  249.3 74.7 %all-reduce.2 = (f32[2,7,7,128]{3,2,1,0:T(8,128)S(1)}, f32[2,128]{1,0:T(2,128)S(1)}, f32[2,128]{1,0:T(2,128)S(1)}, f32[2,128]{1,0:T(2,128)S(1)}, f32[2,512]{1,0:...) all-reduce(f32[2,7,7,128]{3,2,1,0:T(8,128)S(1)} %pad_maximum_fusion, ...), channel_id=1, replica_groups=mesh['tile'=128,'member'=2] {'tile','member'}, use_global_device_ids=true, to_apply=%region_107.108 | all-reduce | flops 14848 | bytes 118784 | tf_op jit(solution)/shard_map/psum | solution.py:299
  328.1 1.7 collective-permute-start.28
  330.8 2.8 collective-permute-start.30
  333.6 5.6 collective-permute-start.29
  340.4 2.0 collective-permute-start.26
  346.5 2.5 collective-permute-start.25
  351.2 2.5 collective-permute-done.27
  354.5 3.2 collective-permute-done.25
  358.8 1.9 add_select_fusion
  363.3 232.3 %all-reduce.6.cloned.1.call-done = (f32[2,128,512]{2,1,0:T(8,128)}, f32[2,512,128]{2,1,0:T(8,128)}) async-done(((f32[2,128,512]{2,1,0:T(8,128)}, f32[2,512,128]{2,1,0:T(8,128)}), (f32[2,128,512]{2,1,0:T(8,128)}, f32[2,512,128]{2,1,0:T(8,128)})) %all-reduce.6.cloned.1.call-update) | async-done | bytes 1048592 | tf_op jit(solution)/shard_map/psum | solution.py:299
  595.6 1.9 broadcast_multiply_fusion.1
  597.5 1.9 broadcast_multiply_fusion
  (620 shorter events, 80.4 us)
Async XLA Ops:
  7.2 588.4 %all-reduce.6.cloned.1.call-start = ((), (), s32[]{:S(2)}) async-start(), calls=%async_computation | async-start | bytes 2097152 | tf_op jit(solution)/shard_map/psum | solution.py:299
  8.3 65.6 %collective-permute-start.7 = (bf16[4,3,3,128]{3,1,2,0:T(4,128)(2,1)S(1)}, bf16[4,3,3,128]{3,1,2,0:T(4,128)(2,1)S(1)}, u32[]{:S(2)}, u32[]{:S(2)}) collective-permute-start(bf16[4,3,3,128]{3,1,2,0:T(4,128)(2,1)S(1)} %pad_maximum_fusion.7), channel_id=1, source_target_pairs={{0,246},{2,248},{4,250},{6,252},{8,254},{10,0},{12,2},{14,4},{16,6... | collective-permute-start | bytes 27656 | tf_op jit(solution)/shard_map/ppermute | solution.py:20
  18.6 55.6 %collective-permute-start.5 = (bf16[4,3,3,128]{3,1,2,0:T(4,128)(2,1)S(1)}, bf16[4,3,3,128]{3,1,2,0:T(4,128)(2,1)S(1)}, u32[]{:S(2)}, u32[]{:S(2)}) collective-permute-start(bf16[4,3,3,128]{3,1,2,0:T(4,128)(2,1)S(1)} %pad_maximum_fusion.7), channel_id=1, source_target_pairs={{0,250},{2,252},{4,254},{6,0},{8,2},{10,4},{12,6},{14,8},{16,10},{... | collective-permute-start | bytes 27656 | tf_op jit(solution)/shard_map/ppermute | solution.py:20
  19.9 54.8 %collective-permute-start.2 = (bf16[4,3,3,128]{3,1,2,0:T(4,128)(2,1)S(1)}, bf16[4,3,3,128]{3,1,2,0:T(4,128)(2,1)S(1)}, u32[]{:S(2)}, u32[]{:S(2)}) collective-permute-start(bf16[4,3,3,128]{3,1,2,0:T(4,128)(2,1)S(1)} %pad_maximum_fusion.7), channel_id=1, source_target_pairs={{0,6},{2,8},{4,10},{6,12},{8,14},{10,16},{12,18},{14,20},{16,22},{... | collective-permute-start | bytes 27656 | tf_op jit(solution)/shard_map/ppermute | solution.py:20
  20.3 55.9 %collective-permute-start = (bf16[4,3,3,128]{3,1,2,0:T(4,128)(2,1)S(1)}, bf16[4,3,3,128]{3,1,2,0:T(4,128)(2,1)S(1)}, u32[]{:S(2)}, u32[]{:S(2)}) collective-permute-start(bf16[4,3,3,128]{3,1,2,0:T(4,128)(2,1)S(1)} %pad_maximum_fusion.7), channel_id=1, source_target_pairs={{0,10},{2,12},{4,14},{6,16},{8,18},{10,20},{12,22},{14,24},{16,26}... | collective-permute-start | bytes 27656 | tf_op jit(solution)/shard_map/ppermute | solution.py:20
  21.6 54.7 %collective-permute-start.6 = (bf16[4,3,32,128]{3,2,1,0:T(8,128)(2,1)S(1)}, bf16[4,3,32,128]{3,2,1,0:T(8,128)(2,1)S(1)}, u32[]{:S(2)}, u32[]{:S(2)}) collective-permute-start(bf16[4,3,32,128]{3,2,1,0:T(8,128)(2,1)S(1)} %pad_maximum_fusion.3), channel_id=1, source_target_pairs={{0,248},{2,250},{4,252},{6,254},{8,0},{10,2},{12,4},{14,6},{16,8},... | collective-permute-start | bytes 294920 | tf_op jit(solution)/shard_map/ppermute | solution.py:20
  41.7 51.3 %copy-start.25 = (f32[128]{0:T(128)}, f32[128]{0:T(128)S(1)}, u32[]{:S(2)}) copy-start(f32[128]{0:T(128)S(1)} %get-tuple-element.530) | copy-start | bytes 1540
  41.7 51.2 %copy-start.27 = (f32[128]{0:T(128)}, f32[128]{0:T(128)S(1)}, u32[]{:S(2)}) copy-start(f32[128]{0:T(128)S(1)} %get-tuple-element.531) | copy-start | bytes 1540
  41.7 51.2 %copy-start.29 = (f32[128]{0:T(128)}, f32[128]{0:T(128)S(1)}, u32[]{:S(2)}) copy-start(f32[128]{0:T(128)S(1)} %get-tuple-element.532) | copy-start | bytes 1540
  41.8 51.2 %copy-start.31 = (f32[128]{0:T(128)}, f32[128]{0:T(128)S(1)}, u32[]{:S(2)}) copy-start(f32[128]{0:T(128)S(1)} %get-tuple-element.533) | copy-start | bytes 1540
  41.8 51.2 %copy-start.33 = (f32[128]{0:T(128)}, f32[128]{0:T(128)S(1)}, u32[]{:S(2)}) copy-start(f32[128]{0:T(128)S(1)} %get-tuple-element.534) | copy-start | bytes 1540
  41.8 51.2 %copy-start.35 = (f32[128]{0:T(128)}, f32[128]{0:T(128)S(1)}, u32[]{:S(2)}) copy-start(f32[128]{0:T(128)S(1)} %get-tuple-element.535) | copy-start | bytes 1540
  41.8 51.2 %copy-start.37 = (f32[128]{0:T(128)}, f32[128]{0:T(128)S(1)}, u32[]{:S(2)}) copy-start(f32[128]{0:T(128)S(1)} %get-tuple-element.536) | copy-start | bytes 1540
  41.8 51.2 %copy-start.39 = (f32[128]{0:T(128)}, f32[128]{0:T(128)S(1)}, u32[]{:S(2)}) copy-start(f32[128]{0:T(128)S(1)} %get-tuple-element.537) | copy-start | bytes 1540
  41.8 51.2 %copy-start.41 = (f32[128]{0:T(128)}, f32[128]{0:T(128)S(1)}, u32[]{:S(2)}) copy-start(f32[128]{0:T(128)S(1)} %get-tuple-element.538) | copy-start | bytes 1540
  41.8 51.2 %copy-start.43 = (f32[128]{0:T(128)}, f32[128]{0:T(128)S(1)}, u32[]{:S(2)}) copy-start(f32[128]{0:T(128)S(1)} %get-tuple-element.539) | copy-start | bytes 1540
  41.8 51.2 %copy-start.45 = (f32[128]{0:T(128)}, f32[128]{0:T(128)S(1)}, u32[]{:S(2)}) copy-start(f32[128]{0:T(128)S(1)} %get-tuple-element.540) | copy-start | bytes 1540
  41.9 51.2 %copy-start.47 = (f32[128]{0:T(128)}, f32[128]{0:T(128)S(1)}, u32[]{:S(2)}) copy-start(f32[128]{0:T(128)S(1)} %get-tuple-element.511) | copy-start | bytes 1540
  74.0 2.5 collective-permute-start.4
  74.2 9.8 %collective-permute-start.3 = (bf16[4,3,32,128]{3,2,1,0:T(8,128)(2,1)S(1)}, bf16[4,3,32,128]{3,2,1,0:T(8,128)(2,1)S(1)}, u32[]{:S(2)}, u32[]{:S(2)}) collective-permute-start(bf16[4,3,32,128]{3,2,1,0:T(8,128)(2,1)S(1)} %pad_maximum_fusion.3), channel_id=1, source_target_pairs={{0,2},{2,4},{4,6},{6,8},{8,10},{10,12},{12,14},{14,16},{16,18},{18... | collective-permute-start | bytes 294920 | tf_op jit(solution)/shard_map/ppermute | solution.py:20
  74.6 13.6 %collective-permute-start.1 = (bf16[4,3,32,128]{3,2,1,0:T(8,128)(2,1)S(1)}, bf16[4,3,32,128]{3,2,1,0:T(8,128)(2,1)S(1)}, u32[]{:S(2)}, u32[]{:S(2)}) collective-permute-start(bf16[4,3,32,128]{3,2,1,0:T(8,128)(2,1)S(1)} %pad_maximum_fusion.3), channel_id=1, source_target_pairs={{0,8},{2,10},{4,12},{6,14},{8,16},{10,18},{12,20},{14,22},{16,24},... | collective-permute-start | bytes 294920 | tf_op jit(solution)/shard_map/ppermute | solution.py:20
  100.1 13.8 %collective-permute-start.15 = (bf16[4,3,3,128]{3,1,2,0:T(4,128)(2,1)S(1)}, bf16[4,3,3,128]{3,1,2,0:T(4,128)(2,1)S(1)}, u32[]{:S(2)}, u32[]{:S(2)}) collective-permute-start(bf16[4,3,3,128]{3,1,2,0:T(4,128)(2,1)S(1)} %pad_maximum_fusion.8), channel_id=1, source_target_pairs={{0,246},{2,248},{4,250},{6,252},{8,254},{10,0},{12,2},{14,4},{16,6... | collective-permute-start | bytes 27656 | tf_op jit(solution)/shard_map/ppermute | solution.py:20
  101.8 12.9 %collective-permute-start.13 = (bf16[4,3,3,128]{3,1,2,0:T(4,128)(2,1)S(1)}, bf16[4,3,3,128]{3,1,2,0:T(4,128)(2,1)S(1)}, u32[]{:S(2)}, u32[]{:S(2)}) collective-permute-start(bf16[4,3,3,128]{3,1,2,0:T(4,128)(2,1)S(1)} %pad_maximum_fusion.8), channel_id=1, source_target_pairs={{0,250},{2,252},{4,254},{6,0},{8,2},{10,4},{12,6},{14,8},{16,10},{... | collective-permute-start | bytes 27656 | tf_op jit(solution)/shard_map/ppermute | solution.py:20
  101.8 13.2 %collective-permute-start.10 = (bf16[4,3,3,128]{3,1,2,0:T(4,128)(2,1)S(1)}, bf16[4,3,3,128]{3,1,2,0:T(4,128)(2,1)S(1)}, u32[]{:S(2)}, u32[]{:S(2)}) collective-permute-start(bf16[4,3,3,128]{3,1,2,0:T(4,128)(2,1)S(1)} %pad_maximum_fusion.8), channel_id=1, source_target_pairs={{0,6},{2,8},{4,10},{6,12},{8,14},{10,16},{12,18},{14,20},{16,22},{... | collective-permute-start | bytes 27656 | tf_op jit(solution)/shard_map/ppermute | solution.py:20
  103.5 14.0 %collective-permute-start.8 = (bf16[4,3,3,128]{3,1,2,0:T(4,128)(2,1)S(1)}, bf16[4,3,3,128]{3,1,2,0:T(4,128)(2,1)S(1)}, u32[]{:S(2)}, u32[]{:S(2)}) collective-permute-start(bf16[4,3,3,128]{3,1,2,0:T(4,128)(2,1)S(1)} %pad_maximum_fusion.8), channel_id=1, source_target_pairs={{0,10},{2,12},{4,14},{6,16},{8,18},{10,20},{12,22},{14,24},{16,26}... | collective-permute-start | bytes 27656 | tf_op jit(solution)/shard_map/ppermute | solution.py:20
  109.6 10.7 %collective-permute-start.14 = (bf16[4,3,32,128]{3,1,2,0:T(4,128)(2,1)S(1)}, bf16[4,3,32,128]{3,1,2,0:T(4,128)(2,1)S(1)}, u32[]{:S(2)}, u32[]{:S(2)}) collective-permute-start(bf16[4,3,32,128]{3,1,2,0:T(4,128)(2,1)S(1)} %pad_maximum_fusion.2), channel_id=1, source_target_pairs={{0,248},{2,250},{4,252},{6,254},{8,0},{10,2},{12,4},{14,6},{16,8},... | collective-permute-start | bytes 294920 | tf_op jit(solution)/shard_map/ppermute | solution.py:20
  114.0 8.1 %collective-permute-start.12 = (bf16[4,3,32,128]{3,1,2,0:T(4,128)(2,1)S(1)}, bf16[4,3,32,128]{3,1,2,0:T(4,128)(2,1)S(1)}, u32[]{:S(2)}, u32[]{:S(2)}) collective-permute-start(bf16[4,3,32,128]{3,1,2,0:T(4,128)(2,1)S(1)} %pad_maximum_fusion.2), channel_id=1, source_target_pairs={{0,254},{2,0},{4,2},{6,4},{8,6},{10,8},{12,10},{14,12},{16,14},{18... | collective-permute-start | bytes 294920 | tf_op jit(solution)/shard_map/ppermute | solution.py:20
  114.7 10.2 %collective-permute-start.11 = (bf16[4,3,32,128]{3,1,2,0:T(4,128)(2,1)S(1)}, bf16[4,3,32,128]{3,1,2,0:T(4,128)(2,1)S(1)}, u32[]{:S(2)}, u32[]{:S(2)}) collective-permute-start(bf16[4,3,32,128]{3,1,2,0:T(4,128)(2,1)S(1)} %pad_maximum_fusion.2), channel_id=1, source_target_pairs={{0,2},{2,4},{4,6},{6,8},{8,10},{10,12},{12,14},{14,16},{16,18},{18... | collective-permute-start | bytes 294920 | tf_op jit(solution)/shard_map/ppermute | solution.py:20
  115.0 14.0 %collective-permute-start.9 = (bf16[4,3,32,128]{3,1,2,0:T(4,128)(2,1)S(1)}, bf16[4,3,32,128]{3,1,2,0:T(4,128)(2,1)S(1)}, u32[]{:S(2)}, u32[]{:S(2)}) collective-permute-start(bf16[4,3,32,128]{3,1,2,0:T(4,128)(2,1)S(1)} %pad_maximum_fusion.2), channel_id=1, source_target_pairs={{0,8},{2,10},{4,12},{6,14},{8,16},{10,18},{12,20},{14,22},{16,24},... | collective-permute-start | bytes 294920 | tf_op jit(solution)/shard_map/ppermute | solution.py:20
  171.9 17.3 %collective-permute-start.20 = (f32[3,3,128]{2,0,1:T(4,128)S(1)}, f32[3,3,128]{2,0,1:T(4,128)S(1)}, u32[]{:S(2)}, u32[]{:S(2)}) collective-permute-start(f32[3,3,128]{2,0,1:T(4,128)S(1)} %get-tuple-element.405), channel_id=1, source_target_pairs={{0,246},{2,248},{4,250},{6,252},{8,254},{10,0},{12,2},{14,4},{16,6... | collective-permute-start | bytes 13832 | tf_op jit(solution)/shard_map/ppermute | solution.py:20
  172.0 17.3 %collective-permute-start.22 = (f32[3,3,128]{2,0,1:T(4,128)S(1)}, f32[3,3,128]{2,0,1:T(4,128)S(1)}, u32[]{:S(2)}, u32[]{:S(2)}) collective-permute-start(f32[3,3,128]{2,0,1:T(4,128)S(1)} %get-tuple-element.406), channel_id=1, source_target_pairs={{0,6},{2,8},{4,10},{6,12},{8,14},{10,16},{12,18},{14,20},{16,22},{... | collective-permute-start | bytes 13832 | tf_op jit(solution)/shard_map/ppermute | solution.py:20
  174.9 21.1 %collective-permute-start.21 = (f32[3,3,128]{2,0,1:T(4,128)S(1)}, f32[3,3,128]{2,0,1:T(4,128)S(1)}, u32[]{:S(2)}, u32[]{:S(2)}) collective-permute-start(f32[3,3,128]{2,0,1:T(4,128)S(1)} %get-tuple-element.407), channel_id=1, source_target_pairs={{0,250},{2,252},{4,254},{6,0},{8,2},{10,4},{12,6},{14,8},{16,10},{... | collective-permute-start | bytes 13832 | tf_op jit(solution)/shard_map/ppermute | solution.py:20
  180.5 15.6 %collective-permute-start.23 = (f32[3,3,128]{2,0,1:T(4,128)S(1)}, f32[3,3,128]{2,0,1:T(4,128)S(1)}, u32[]{:S(2)}, u32[]{:S(2)}) collective-permute-start(f32[3,3,128]{2,0,1:T(4,128)S(1)} %get-tuple-element.408), channel_id=1, source_target_pairs={{0,10},{2,12},{4,14},{6,16},{8,18},{10,20},{12,22},{14,24},{16,26}... | collective-permute-start | bytes 13832 | tf_op jit(solution)/shard_map/ppermute | solution.py:20
  180.6 17.7 %collective-permute-start.18 = (bf16[3,32,128]{2,1,0:T(8,128)(2,1)S(1)}, bf16[3,32,128]{2,1,0:T(8,128)(2,1)S(1)}, u32[]{:S(2)}, u32[]{:S(2)}) collective-permute-start(bf16[3,32,128]{2,1,0:T(8,128)(2,1)S(1)} %select_convert_fusion.5), channel_id=1, source_target_pairs={{0,254},{2,0},{4,2},{6,4},{8,6},{10,8},{12,10},{14,12},{16,14},{18... | collective-permute-start | bytes 73736 | tf_op jit(solution)/shard_map/ppermute | solution.py:20
  189.2 9.1 %collective-permute-start.19 = (bf16[3,32,128]{2,1,0:T(8,128)(2,1)S(1)}, bf16[3,32,128]{2,1,0:T(8,128)(2,1)S(1)}, u32[]{:S(2)}, u32[]{:S(2)}) collective-permute-start(bf16[3,32,128]{2,1,0:T(8,128)(2,1)S(1)} %select_convert_fusion.4), channel_id=1, source_target_pairs={{0,2},{2,4},{4,6},{6,8},{8,10},{10,12},{12,14},{14,16},{16,18},{18... | collective-permute-start | bytes 73736 | tf_op jit(solution)/shard_map/ppermute | solution.py:20
  189.3 9.0 %collective-permute-start.16 = (bf16[3,32,128]{2,0,1:T(4,128)(2,1)S(1)}, bf16[3,32,128]{2,0,1:T(4,128)(2,1)S(1)}, u32[]{:S(2)}, u32[]{:S(2)}) collective-permute-start(bf16[3,32,128]{2,0,1:T(4,128)(2,1)S(1)} %select_convert_fusion.1), channel_id=1, source_target_pairs={{0,248},{2,250},{4,252},{6,254},{8,0},{10,2},{12,4},{14,6},{16,8},... | collective-permute-start | bytes 73736 | tf_op jit(solution)/shard_map/ppermute | solution.py:20
  196.0 10.6 %collective-permute-start.17 = (bf16[3,32,128]{2,0,1:T(4,128)(2,1)S(1)}, bf16[3,32,128]{2,0,1:T(4,128)(2,1)S(1)}, u32[]{:S(2)}, u32[]{:S(2)}) collective-permute-start(bf16[3,32,128]{2,0,1:T(4,128)(2,1)S(1)} %fusion.239), channel_id=1, source_target_pairs={{0,8},{2,10},{4,12},{6,14},{8,16},{10,18},{12,20},{14,22},{16,24},... | collective-permute-start | bytes 73736 | tf_op jit(solution)/shard_map/ppermute | solution.py:20
  241.8 97.3 %copy-start.18 = (bf16[3,32,128]{2,1,0:T(8,128)(2,1)S(1)}, bf16[3,32,128]{2,1,0:T(8,128)(2,1)}, u32[]{:S(2)}) copy-start(bf16[3,32,128]{2,1,0:T(8,128)(2,1)} %get-tuple-element.404) | copy-start | bytes 73732
  241.9 100.6 %copy-start.4 = (f32[32,32,128]{2,0,1:T(8,128)S(1)}, f32[32,32,128]{2,0,1:T(8,128)}, u32[]{:S(2)}) copy-start(f32[32,32,128]{2,0,1:T(8,128)} %slice.2334) | copy-start | bytes 1572868
  242.4 101.3 %copy-start.10 = (f32[1,128,512]{2,1,0:T(8,128)S(1)}, f32[1,128,512]{2,1,0:T(8,128)}, u32[]{:S(2)}) copy-start(f32[1,128,512]{2,1,0:T(8,128)} %convolution_bitcast_fusion.2) | copy-start | bytes 786436
  328.1 16.4 %collective-permute-start.28 = (f32[3,3,128]{2,0,1:T(4,128)}, f32[3,3,128]{2,0,1:T(4,128)}, u32[]{:S(2)}, u32[]{:S(2)}) collective-permute-start(f32[3,3,128]{2,0,1:T(4,128)} %get-tuple-element.397), channel_id=1, source_target_pairs={{0,246},{2,248},{4,250},{6,252},{8,254},{10,0},{12,2},{14,4},{16,6... | collective-permute-start | bytes 13832 | tf_op jit(solution)/shard_map/ppermute | solution.py:20
  329.9 15.5 %collective-permute-start.31 = (f32[3,3,128]{2,0,1:T(4,128)}, f32[3,3,128]{2,0,1:T(4,128)}, u32[]{:S(2)}, u32[]{:S(2)}) collective-permute-start(f32[3,3,128]{2,0,1:T(4,128)} %get-tuple-element.398), channel_id=1, source_target_pairs={{0,10},{2,12},{4,14},{6,16},{8,18},{10,20},{12,22},{14,24},{16,26}... | collective-permute-start | bytes 13832 | tf_op jit(solution)/shard_map/ppermute | solution.py:20
  330.8 15.7 %collective-permute-start.30 = (f32[3,3,128]{2,0,1:T(4,128)}, f32[3,3,128]{2,0,1:T(4,128)}, u32[]{:S(2)}, u32[]{:S(2)}) collective-permute-start(f32[3,3,128]{2,0,1:T(4,128)} %get-tuple-element.399), channel_id=1, source_target_pairs={{0,6},{2,8},{4,10},{6,12},{8,14},{10,16},{12,18},{14,20},{16,22},{... | collective-permute-start | bytes 13832 | tf_op jit(solution)/shard_map/ppermute | solution.py:20
  333.6 16.1 %collective-permute-start.29 = (f32[3,3,128]{2,0,1:T(4,128)}, f32[3,3,128]{2,0,1:T(4,128)}, u32[]{:S(2)}, u32[]{:S(2)}) collective-permute-start(f32[3,3,128]{2,0,1:T(4,128)} %get-tuple-element.400), channel_id=1, source_target_pairs={{0,250},{2,252},{4,254},{6,0},{8,2},{10,4},{12,6},{14,8},{16,10},{... | collective-permute-start | bytes 13832 | tf_op jit(solution)/shard_map/ppermute | solution.py:20
  340.4 13.2 %collective-permute-start.26 = (bf16[3,32,128]{2,1,0:T(8,128)(2,1)}, bf16[3,32,128]{2,1,0:T(8,128)(2,1)}, u32[]{:S(2)}, u32[]{:S(2)}) collective-permute-start(bf16[3,32,128]{2,1,0:T(8,128)(2,1)} %select_convert_fusion.3), channel_id=1, source_target_pairs={{0,254},{2,0},{4,2},{6,4},{8,6},{10,8},{12,10},{14,12},{16,14},{18... | collective-permute-start | bytes 73736 | tf_op jit(solution)/shard_map/ppermute | solution.py:20
  344.6 9.1 %collective-permute-start.27 = (bf16[3,32,128]{2,1,0:T(8,128)(2,1)S(1)}, bf16[3,32,128]{2,1,0:T(8,128)(2,1)S(1)}, u32[]{:S(2)}, u32[]{:S(2)}) collective-permute-start(bf16[3,32,128]{2,1,0:T(8,128)(2,1)S(1)} %copy-done.21), channel_id=1, source_target_pairs={{0,2},{2,4},{4,6},{6,8},{8,10},{10,12},{12,14},{14,16},{16,18},{18... | collective-permute-start | bytes 73736 | tf_op jit(solution)/shard_map/ppermute | solution.py:20
  345.4 9.1 %collective-permute-start.24 = (bf16[3,32,128]{2,0,1:T(4,128)(2,1)S(1)}, bf16[3,32,128]{2,0,1:T(4,128)(2,1)S(1)}, u32[]{:S(2)}, u32[]{:S(2)}) collective-permute-start(bf16[3,32,128]{2,0,1:T(4,128)(2,1)S(1)} %select_convert_fusion), channel_id=1, source_target_pairs={{0,248},{2,250},{4,252},{6,254},{8,0},{10,2},{12,4},{14,6},{16,8},... | collective-permute-start | bytes 73736 | tf_op jit(solution)/shard_map/ppermute | solution.py:20
  346.5 11.1 %collective-permute-start.25 = (bf16[3,32,128]{2,0,1:T(4,128)(2,1)S(1)}, bf16[3,32,128]{2,0,1:T(4,128)(2,1)S(1)}, u32[]{:S(2)}, u32[]{:S(2)}) collective-permute-start(bf16[3,32,128]{2,0,1:T(4,128)(2,1)S(1)} %fusion.240), channel_id=1, source_target_pairs={{0,8},{2,10},{4,12},{6,14},{8,16},{10,18},{12,20},{14,22},{16,24},... | collective-permute-start | bytes 73736 | tf_op jit(solution)/shard_map/ppermute | solution.py:20
  (149 other events, 2329.4 us)
Sparse Core Ops, SparseCore 0:
  344.6 250.9 all-reduce.5
where the time goes:
time: 614 us; the launch traced here: 606 us
  waiting for transfers between devices  271 us (44%)
  other arithmetic  85.9 us (14%)
  blocking collectives  74.7 us (12%)
  starting transfers between devices  74.3 us (12%)
  between operations  40.6 us (7%)
  local copies, waits for them, and re-layouts  36.9 us (6%)
  matrix products  22.6 us (4%)
    psum x1, waiting for transfers between devices, body(): lax.psum((stacked[0], stacked[1], stacked[2], stacked[3], stacked[4], sta...  232 us
    psum x1, blocking collectives, body(): lax.psum((stacked[0], stacked[1], stacked[2], stacked[3], stacked[4], sta...  74.7 us
    ppermute x32, starting transfers between devices, passed_along(): return lax.ppermute(value, axis, pairs)  74.3 us
    ppermute x32, waiting for transfers between devices, passed_along(): return lax.ppermute(value, axis, pairs)  39 us
    reduce_sum x2, other arithmetic, block_forward(): centred = conv - jnp.mean(conv, axis=1, keepdims=True)  21.7 us
    add x2, other arithmetic, block_backward(): pad_grad + grown[6 - row_tap:12 - row_tap + size, 6 - col_tap:12 - col_ta...  13.7 us
  transfers between devices with their start and end apart: 33, of which 12 were waited for; matrix products, arithmetic and copies ran while one was open for 7% of the time, Pallas kernels for 0%

commit v1 on v0

v1 whole, which is shorter than its diff:
```python
import math

import jax
import jax.numpy as jnp
from jax import lax
from jax.experimental import pallas as pl
from jax.experimental.pallas import tpu as pltpu
from jax.sharding import Mesh, PartitionSpec as P

BF = jnp.bfloat16
F32 = jnp.float32
BLOCKS = 2
SIZE = 32
CELLS = SIZE * SIZE
WIDTH = 128
HID = 512
TAPS = 7
CHUNK = 256
PAD_ROWS = 38
PAD_COLS = 48
GROWN_COLS = 64
MESSAGE = 128
EPSILON = 1e-06
GELU_C = 0.7978845608028654
GELU_A = 0.044715
TILE_AXES = ("far", "y", "z", "core")
VMEM_LIMIT = 32 * 1024 * 1024


def kernel_params():
    return pltpu.CompilerParams(vmem_limit_bytes=VMEM_LIMIT)


def whole(count):
    return [pl.BlockSpec(memory_space=pltpu.VMEM)] * count


def onehot(condition):
    return jnp.where(condition, 1.0, 0.0).astype(BF)


def matmul(left, right, dims=((1,), (0,))):
    return lax.dot_general(left, right, (dims, ((), ())), preferred_element_type=F32)


def message_cells(seam_ref, corner_ref, here, facing, slot):
    step = (4, -4, 1, -1)[facing]
    tiles = seam_ref.shape[0]
    code = seam_ref[(here + step + tiles) % tiles, facing]
    along = slot & 31
    depth = slot >> 5
    depth = 2 - depth if facing in (0, 2) else depth
    edge = code & 3
    along = jnp.where(code >= 4, 31 - along, along)
    depth = jnp.where((edge & 1) == 1, 31 - depth, depth)
    strip = jnp.where(edge < 2, depth * SIZE + along, along * SIZE + depth)
    if facing < 2:
        return jnp.where(slot < 96, strip, -1)
    if facing == 2:
        first, second = corner_ref[(here + 5) % tiles, 0], corner_ref[(here - 3 + tiles) % tiles, 2]
    else:
        first, second = corner_ref[(here - 5 + tiles) % tiles, 3], corner_ref[(here + 3) % tiles, 1]
    at = jnp.where(slot < 112, slot - 96, slot - 112)
    code = jnp.where(slot < 112, first, second)
    row = (at * 11) >> 5
    col = at - 3 * row
    block = (row + 29 * (code >> 1)) * SIZE + col + 29 * (code & 1)
    block = jnp.where((at < 9) & (code < 4), block, -1)
    return jnp.where(slot < 96, strip, block)


def select_kernel(here_ref, seam_ref, corner_ref, field_ref, sent_ref, gather_ref):
    here = here_ref[0]
    field = field_ref[...]
    slot = lax.broadcasted_iota(jnp.int32, (MESSAGE, WIDTH), 0)
    lane = lax.broadcasted_iota(jnp.int32, (MESSAGE, WIDTH), 1)
    for facing in range(4):
        cells = message_cells(seam_ref, corner_ref, here, facing, slot)
        total = jnp.zeros((MESSAGE, WIDTH), F32)
        for part in range(CELLS // WIDTH):
            chosen = onehot(cells == lane + part * WIDTH)
            gather_ref[facing * MESSAGE : (facing + 1) * MESSAGE, part * WIDTH : (part + 1) * WIDTH] = chosen
            total = total + matmul(chosen, field[part * WIDTH : (part + 1) * WIDTH])
        sent_ref[facing] = total.astype(BF)


def scatter_kernel(here_ref, seam_ref, corner_ref, scatter_ref):
    here = here_ref[0]
    slot = lax.broadcasted_iota(jnp.int32, (8, MESSAGE), 1)
    cell = lax.broadcasted_iota(jnp.int32, (CELLS, MESSAGE), 0)
    for facing in range(4):
        cells = message_cells(seam_ref, corner_ref, here, facing, slot)
        scatter_ref[:, facing * MESSAGE : (facing + 1) * MESSAGE] = onehot(cell == cells[0:1])


def row_rim_slots(position):
    depth = jnp.where(position >= 96, 2, jnp.where(position >= 48, 1, 0))
    along = position - 48 * depth - 5
    slot = jnp.where(
        along < 3, 96 + 3 * depth + along, jnp.where(along < 35, 32 * depth + along - 3, 77 + 3 * depth + along)
    )
    return jnp.where((along >= 0) & (along < 38), slot, -1)


def col_rim_slots(position, first):
    depth = (position & 7) - first
    slot = 32 * depth + (position >> 3)
    return jnp.where((depth >= 0) & (depth < 3), slot, -1)


def iota(shape, dim):
    return lax.broadcasted_iota(jnp.int32, shape, dim)


def fill_padded(padded_ref, field, north, south, west, east):
    rows = (3 * PAD_COLS, MESSAGE)
    place = onehot(row_rim_slots(iota(rows, 0)) == iota(rows, 1))
    padded_ref[0:3] = matmul(place, north).reshape(3, PAD_COLS, WIDTH)
    padded_ref[35:38] = matmul(place, south).reshape(3, PAD_COLS, WIDTH)
    cols = (SIZE * 8, MESSAGE)
    place = onehot(col_rim_slots(iota(cols, 0), 5) == iota(cols, 1))
    padded_ref[3:35, 0:8] = matmul(place, west).reshape(SIZE, 8, WIDTH)
    place = onehot(col_rim_slots(iota(cols, 0), 0) == iota(cols, 1))
    padded_ref[3:35, 40:48] = matmul(place, east).reshape(SIZE, 8, WIDTH)
    padded_ref[3:35, 8:40] = field.astype(F32).reshape(SIZE, SIZE, WIDTH)


def tap(kernel_ref, row_tap, col_tap):
    return kernel_ref[row_tap * TAPS + col_tap : row_tap * TAPS + col_tap + 1, :]


def convolve(source_ref, first_col, kernel_ref, flipped, start, out_ref):
    def group(index, carry):
        totals = [jnp.broadcast_to(start, (SIZE, WIDTH)) for _ in range(4)]
        for col_tap in range(TAPS):
            for row in range(4 + TAPS - 1):
                values = source_ref[index * 4 + row, first_col + col_tap : first_col + col_tap + SIZE, :]
                for out in range(max(0, row - TAPS + 1), min(4, row + 1)):
                    a, e = row - out, col_tap
                    if flipped:
                        a, e = TAPS - 1 - a, TAPS - 1 - e
                    totals[out] = totals[out] + values * tap(kernel_ref, a, e)
        for out in range(4):
            out_ref[pl.ds(pl.multiple_of(index * 128 + out * SIZE, SIZE), SIZE), :] = totals[out]
        return carry

    lax.fori_loop(0, SIZE // 4, group, 0)


def kernel_sums(padded_ref, grown_ref, sums_ref):
    sums_ref[...] = jnp.zeros_like(sums_ref)

    def group(index, carry):
        grads = [grown_ref[index * 4 + 3 + row, 16:48, :] for row in range(4)]
        for col_tap in range(TAPS):
            totals = [jnp.zeros((8, WIDTH), F32) for _ in range(TAPS)]
            for row in range(4 + TAPS - 1):
                values = padded_ref[index * 4 + row, 5 + col_tap : 5 + col_tap + SIZE, :]
                for out in range(max(0, row - TAPS + 1), min(4, row + 1)):
                    product = values * grads[out]
                    totals[row - out] = totals[row - out] + (
                        (product[0:8] + product[8:16]) + (product[16:24] + product[24:32])
                    )
            for row_tap in range(TAPS):
                at = 8 * (row_tap * TAPS + col_tap)
                sums_ref[at : at + 8, :] += totals[row_tap]
        return carry

    lax.fori_loop(0, SIZE // 4, group, 0)


def row_rim(grown_ref, kernel_ref, top):
    rows = []
    for depth in range(3):
        total = jnp.zeros((PAD_COLS, WIDTH), F32)
        for row_tap in range(TAPS):
            source = depth - row_tap if top else 35 + depth - row_tap
            if 0 <= source < SIZE:
                for col_tap in range(TAPS):
                    at = 11 - col_tap
                    total = total + grown_ref[source + 3, at : at + PAD_COLS, :] * tap(kernel_ref, row_tap, col_tap)
        rows.append(total)
    return jnp.concatenate(rows, axis=0)


def col_rim(grown_ref, kernel_ref, left, out_ref):
    def group(index, carry):
        totals = [jnp.zeros((8, WIDTH), F32) for _ in range(8)]
        for col_tap in range(3) if left else range(4, TAPS):
            at = 11 - col_tap if left else 51 - col_tap
            for row in range(8 + TAPS - 1):
                values = grown_ref[index * 8 + row, at : at + 8, :]
                for out in range(max(0, row - TAPS + 1), min(8, row + 1)):
                    totals[out] = totals[out] + values * tap(kernel_ref, TAPS - 1 - (row - out), col_tap)
        for out in range(8):
            out_ref[pl.ds(pl.multiple_of(index * 64 + out * 8, 8), 8), :] = totals[out]
        return carry

    lax.fori_loop(0, SIZE // 8, group, 0)


def send_rims(grown_ref, kernel_ref, rim_ref, sent_ref):
    rows = (MESSAGE, 3 * PAD_COLS)
    place = onehot(row_rim_slots(iota(rows, 1)) == iota(rows, 0))
    for facing in range(2):
        sent_ref[facing] = matmul(place, row_rim(grown_ref, kernel_ref, facing == 0).astype(BF)).astype(BF)
    cols = (MESSAGE, SIZE * 8)
    for facing in range(2, 4):
        col_rim(grown_ref, kernel_ref, facing == 2, rim_ref)
        place = onehot(col_rim_slots(iota(cols, 1), 5 if facing == 2 else 0) == iota(cols, 0))
        sent_ref[facing] = matmul(place, rim_ref[...].astype(BF)).astype(BF)


def normalised(conv):
    centred = conv - jnp.mean(conv, axis=1, keepdims=True)
    inv_std = lax.rsqrt(jnp.mean(centred * centred, axis=1, keepdims=True) + EPSILON)
    return centred * inv_std, inv_std


def forward_chunk(conv, field, rows, up_w, up_b, down_w):
    gain, offset, down_b, scale = rows
    standard, _ = normalised(conv)
    normed = (standard * gain + offset).astype(BF)
    pre = matmul(normed, up_w) + up_b
    tangent = jnp.tanh(pre * (GELU_C + (GELU_C * GELU_A) * pre * pre))
    activated = (0.5 * pre * (1.0 + tangent)).astype(BF)
    branch = matmul(activated, down_w) + down_b
    return (field.astype(F32) + scale * branch).astype(BF)


def first_kernel(
    field_ref, north_ref, south_ref, west_ref, east_ref, gather_ref, kernel_ref, bias_ref, gain_ref, offset_ref,
    up_ref, up_b_ref, down_ref, down_b_ref, scale_ref,
    out_ref, conv_ref, padded_ref, sent_ref,
):
    fill_padded(padded_ref, field_ref[...], north_ref[...], south_ref[...], west_ref[...], east_ref[...])
    convolve(padded_ref, 5, kernel_ref.at[0], False, bias_ref[0:1, :], conv_ref)
    rows = (gain_ref[0:1, :], offset_ref[0:1, :], down_b_ref[0:1, :], scale_ref[0:1, :])

    def chunk(index, carry):
        here = pl.ds(pl.multiple_of(index * CHUNK, CHUNK), CHUNK)
        out_ref[here, :] = forward_chunk(
            conv_ref[here, :], field_ref[here, :], rows, up_ref[0], up_b_ref[0:1, :], down_ref[0]
        )
        return carry

    lax.fori_loop(0, CELLS // CHUNK, chunk, 0)
    sent = matmul(gather_ref[...], out_ref[...]).astype(BF)
    for facing in range(4):
        sent_ref[facing] = sent[facing * MESSAGE : (facing + 1) * MESSAGE]


def backward_chunk(block, here, conv, upstream, refs, field, out_ref):
    (gain_ref, offset_ref, up_ref, up_b_ref, down_ref, down_b_ref, scale_ref, up_sum, down_sum, vector_sum, up_b_sum) = refs
    at = slice(block, block + 1)
    gain, scale = gain_ref[at, :], scale_ref[at, :]
    standard, inv_std = normalised(conv)
    normed = (standard * gain + offset_ref[at, :]).astype(BF)
    pre = matmul(normed, up_ref[block]) + up_b_ref[at, :]
    square = pre * pre
    tangent = jnp.tanh(pre * (GELU_C + (GELU_C * GELU_A) * square))
    half = 0.5 + 0.5 * tangent
    activated = (pre * half).astype(BF)
    slope = half + pre * (0.5 - 0.5 * tangent * tangent) * (GELU_C + (3.0 * GELU_C * GELU_A) * square)
    branch = matmul(activated, down_ref[block]) + down_b_ref[at, :]
    if out_ref is not None:
        out_ref[here, :] = (field.astype(F32) + scale * branch).astype(BF)
    scaled = upstream * scale
    scaled_b = scaled.astype(BF)
    down_sum[...] += matmul(scaled_b, activated, ((0,), (0,)))
    pre_grad = matmul(scaled_b, down_ref[block], ((1,), (1,))) * slope
    up_b_sum[...] += jnp.sum(pre_grad, axis=0, keepdims=True)
    pre_grad_b = pre_grad.astype(BF)
    up_sum[...] += matmul(normed, pre_grad_b, ((0,), (0,)))
    normed_grad = matmul(pre_grad_b, up_ref[block], ((1,), (1,)))
    std_grad = normed_grad * gain
    conv_grad = inv_std * (
        std_grad
        - jnp.mean(std_grad, axis=1, keepdims=True)
        - standard * jnp.mean(std_grad * standard, axis=1, keepdims=True)
    )
    for row, values in enumerate((conv_grad, normed_grad * standard, normed_grad, scaled, upstream * branch)):
        vector_sum[row : row + 1, :] += jnp.sum(values, axis=0, keepdims=True)
    return conv_grad


def backward_block(block, conv_ref, upstream_of, refs, field_ref, out_ref, grown_ref):
    for ref in refs[7:]:
        ref[...] = jnp.zeros_like(ref)
    grown_ref[0:3] = jnp.zeros((3, GROWN_COLS, WIDTH), F32)
    grown_ref[35:38] = jnp.zeros((3, GROWN_COLS, WIDTH), F32)
    grown_ref[3:35, 0:16] = jnp.zeros((SIZE, 16, WIDTH), F32)
    grown_ref[3:35, 48:64] = jnp.zeros((SIZE, 16, WIDTH), F32)
    tall = CHUNK // SIZE

    def chunk(index, carry):
        here = pl.ds(pl.multiple_of(index * CHUNK, CHUNK), CHUNK)
        field = None if field_ref is None else field_ref[here, :]
        grad = backward_chunk(block, here, conv_ref[here, :], upstream_of(here), refs, field, out_ref)
        grown_ref[pl.ds(3 + index * tall, tall), 16:48, :] = grad.reshape(tall, SIZE, WIDTH)
        return carry

    lax.fori_loop(0, CELLS // CHUNK, chunk, 0)


def pack_sums(refs, weights_ref, vectors_ref):
    up_sum, down_sum, vector_sum, up_b_sum = refs[7:]
    for part in range(HID // WIDTH):
        lanes = slice(part * WIDTH, (part + 1) * WIDTH)
        weights_ref[part * WIDTH : (part + 1) * WIDTH, :] = up_sum[:, lanes].astype(BF)
        weights_ref[HID + part * WIDTH : HID + (part + 1) * WIDTH, :] = down_sum[:, lanes].astype(BF)
        vector_sum[8 + part : 9 + part, :] = up_b_sum[:, lanes]
    vectors_ref[...] = vector_sum[...].astype(BF)


def second_kernel(
    field_ref, north_ref, south_ref, west_ref, east_ref, cotangent_ref, kernel_ref, bias_ref, gain_ref, offset_ref,
    up_ref, up_b_ref, down_ref, down_b_ref, scale_ref,
    out_ref, padded_ref, grown_ref, sent_ref, weights_ref, vectors_ref,
    conv_ref, up_sum, down_sum, vector_sum, up_b_sum, rim_ref,
):
    fill_padded(padded_ref, field_ref[...], north_ref[...], south_ref[...], west_ref[...], east_ref[...])
    convolve(padded_ref, 5, kernel_ref.at[1], False, bias_ref[1:2, :], conv_ref)
    refs = (gain_ref, offset_ref, up_ref, up_b_ref, down_ref, down_b_ref, scale_ref, up_sum, down_sum, vector_sum, up_b_sum)
    backward_block(
        1, conv_ref, lambda here: cotangent_ref[here, :].astype(F32), refs, field_ref, out_ref, grown_ref
    )
    send_rims(grown_ref, kernel_ref.at[1], rim_ref, sent_ref)
    pack_sums(refs, weights_ref, vectors_ref)


def third_kernel(
    conv_ref, cotangent_ref, inner_ref, first_ref, second_ref, third_ref, fourth_ref, scatter_ref, kernel_ref, gain_ref,
    offset_ref, up_ref, up_b_ref, down_ref, down_b_ref, scale_ref,
    upstream_ref, grown_ref, sent_ref, weights_ref, vectors_ref,
    up_sum, down_sum, vector_sum, up_b_sum, rim_ref,
):
    returned = jnp.concatenate([first_ref[...], second_ref[...], third_ref[...], fourth_ref[...]], axis=0)
    upstream_ref[...] = cotangent_ref[...].astype(F32) + inner_ref[...] + matmul(scatter_ref[...], returned)
    refs = (gain_ref, offset_ref, up_ref, up_b_ref, down_ref, down_b_ref, scale_ref, up_sum, down_sum, vector_sum, up_b_sum)
    backward_block(0, conv_ref, lambda here: upstream_ref[here, :], refs, None, None, grown_ref)
    send_rims(grown_ref, kernel_ref.at[0], rim_ref, sent_ref)
    pack_sums(refs, weights_ref, vectors_ref)


def last_kernel(upstream_ref, inner_ref, first_ref, second_ref, third_ref, fourth_ref, scatter_ref, out_ref):
    returned = jnp.concatenate([first_ref[...], second_ref[...], third_ref[...], fourth_ref[...]], axis=0)
    out_ref[...] = (upstream_ref[...] + inner_ref[...] + matmul(scatter_ref[...], returned)).astype(BF)


def make_inner_kernel(block):
    def inner_kernel(grown_ref, kernel_ref, inner_ref):
        convolve(grown_ref, 13, kernel_ref.at[block], True, jnp.zeros((1, WIDTH), F32), inner_ref)

    return inner_kernel


def taps_kernel(padded_ref, grown_ref, taps_ref, sums_ref):
    kernel_sums(padded_ref, grown_ref, sums_ref)
    taps_ref[...] = jnp.sum(sums_ref[...].reshape(64, 8, WIDTH), axis=1).astype(BF)


def passed_along(value, steps):
    count = lax.axis_size(TILE_AXES)
    return lax.ppermute(value, TILE_AXES, [(source, (source + steps) % count) for source in range(count)])


def give_halo(sent):
    west = passed_along(sent[2], 1)
    east = passed_along(sent[3], -1)
    north = passed_along(jnp.concatenate([sent[0, :96], west[96:112], east[112:]]), 4)
    south = passed_along(jnp.concatenate([sent[1, :96], west[112:], east[96:112]]), -4)
    return north, south, west, east


def give_back(sent):
    first = passed_along(sent[0], -4)
    second = passed_along(sent[1], 4)
    third = passed_along(jnp.concatenate([sent[2, :96], first[96:112], second[96:112]]), -1)
    fourth = passed_along(jnp.concatenate([sent[3, :96], second[112:], first[112:]]), 1)
    return first, second, third, fourth


REDUCED_ROWS = 2304


def swapped(value, axis):
    return lax.ppermute(value, axis, [(0, 1), (1, 0)])


def halved(value, axis):
    mine = lax.axis_index(axis)
    parts = value.reshape(2, value.shape[0] // 2, WIDTH)
    kept = lax.dynamic_index_in_dim(parts, mine, 0, keepdims=False)
    given = lax.dynamic_index_in_dim(parts, 1 - mine, 0, keepdims=False)
    return (kept.astype(F32) + swapped(given, axis).astype(F32)).astype(BF)


def joined(value, axis):
    other = swapped(value, axis)
    return jnp.where(
        lax.axis_index(axis) == 0, jnp.concatenate([value, other]), jnp.concatenate([other, value])
    )


def summed_apart(value, axes):
    count = lax.axis_size(axes)
    parts = lax.all_to_all(value, axes, 0, 0, tiled=True).reshape(count, -1, WIDTH)
    return jnp.sum(parts.astype(F32), axis=0).astype(BF)


def gathered(value, axes):
    count = lax.axis_size(axes)
    copies = jnp.broadcast_to(value[None], (count,) + value.shape).reshape(-1, WIDTH)
    return lax.all_to_all(copies, axes, 0, 0, tiled=True)


def summed_everywhere(value):
    value = halved(value, "core")
    value = summed_apart(value, ("far", "y", "z"))
    value = (value.astype(F32) + swapped(value, "member").astype(F32)).astype(BF)
    value = gathered(value, ("far", "y", "z"))
    return joined(value, "core")


def make_unpack_kernel(factor):
    def unpack_kernel(sum_ref, taps, conv_b, gain, offset, up, up_b, down, down_b, scale):
        for block in range(BLOCKS):
            base = block * 2 * HID
            for part in range(HID // WIDTH):
                rows = slice(base + part * WIDTH, base + (part + 1) * WIDTH)
                up[block, :, part * WIDTH : (part + 1) * WIDTH] = sum_ref[rows, :].astype(F32) * factor
                rows = slice(base + HID + part * WIDTH, base + HID + (part + 1) * WIDTH)
                down[block, part * WIDTH : (part + 1) * WIDTH, :] = (sum_ref[rows, :].astype(F32) * factor).T
            base = 4 * HID + 16 * block
            vectors = sum_ref[base : base + 16, :].astype(F32) * factor
            for row, ref in enumerate((conv_b, gain, offset, down_b, scale)):
                ref[block : block + 1, :] = vectors[row : row + 1]
            for part in range(HID // WIDTH):
                up_b[block : block + 1, part * WIDTH : (part + 1) * WIDTH] = vectors[8 + part : 9 + part]
            base = 4 * HID + 32 + 64 * block
            kernel_sum = sum_ref[base : base + 64, :].astype(F32) * factor
            for row_tap in range(TAPS):
                taps[block, row_tap] = kernel_sum[row_tap * TAPS : (row_tap + 1) * TAPS]

    return unpack_kernel


def shaped(*shapes):
    return [jax.ShapeDtypeStruct(shape, dtype) for shape, dtype in shapes]


def call(kernel, shapes, inputs, scratch=(), scalars=0, cost=None):
    specs = [pl.BlockSpec(memory_space=pltpu.SMEM)] * scalars + whole(len(inputs) - scalars)
    return pl.pallas_call(
        kernel,
        out_shape=shaped(*shapes),
        in_specs=specs,
        out_specs=whole(len(shapes)),
        scratch_shapes=list(scratch),
        compiler_params=kernel_params(),
        cost_estimate=cost,
    )(*inputs)


def body(
    states, cotangent, seam_codes, corner_codes, dw_kernel, dw_bias, norm_gain, norm_bias, up_weight, up_bias,
    down_weight, down_bias, layer_scale,
):
    count = lax.axis_size(TILE_AXES) * lax.axis_size("member")
    here = lax.axis_index(TILE_AXES).astype(jnp.int32).reshape(1)
    field = states.reshape(CELLS, WIDTH)
    upstream = cotangent.reshape(CELLS, WIDTH)
    taps = dw_kernel.reshape(BLOCKS, TAPS * TAPS, WIDTH)
    message = ((4, MESSAGE, WIDTH), BF)
    padded_shape = ((PAD_ROWS, PAD_COLS, WIDTH), F32)
    grown_shape = ((PAD_ROWS, GROWN_COLS, WIDTH), F32)
    cells = (CELLS, WIDTH)
    sums = [
        pltpu.VMEM((WIDTH, HID), F32),
        pltpu.VMEM((WIDTH, HID), F32),
        pltpu.VMEM((16, WIDTH), F32),
        pltpu.VMEM((1, HID), F32),
        pltpu.VMEM((SIZE * 8, WIDTH), F32),
    ]
    vpu = pl.CostEstimate(flops=2 * 49 * CELLS * WIDTH, bytes_accessed=3 << 20, transcendentals=0)

    sent, gather = call(
        select_kernel, [message, ((4 * MESSAGE, CELLS), BF)], [here, seam_codes, corner_codes, field], scalars=3
    )
    halo = give_halo(sent)
    (scatter,) = call(
        scatter_kernel, [((CELLS, 4 * MESSAGE), BF)], [here, seam_codes, corner_codes], scalars=3
    )
    vectors = (norm_gain, norm_bias, up_weight, up_bias, down_weight, down_bias, layer_scale)
    middle, conv, padded_0, sent = call(
        first_kernel,
        [(cells, BF), (cells, F32), padded_shape, message],
        [field, *halo, gather, taps, dw_bias, *vectors],
    )
    halo = give_halo(sent)
    out, padded_1, grown_1, sent, weights_1, vectors_1 = call(
        second_kernel,
        [(cells, BF), padded_shape, grown_shape, message, ((2 * HID, WIDTH), BF), ((16, WIDTH), BF)],
        [middle, *halo, upstream, taps, dw_bias, *vectors],
        [pltpu.VMEM(cells, F32), *sums],
    )
    returned = give_back(sent)
    (inner_1,) = call(make_inner_kernel(1), [(cells, F32)], [grown_1, taps], cost=vpu)
    tap_scratch = [pltpu.VMEM((64 * 8, WIDTH), F32)]
    (taps_1,) = call(taps_kernel, [((64, WIDTH), BF)], [padded_1, grown_1], tap_scratch, cost=vpu)
    upstream_0, grown_0, sent, weights_0, vectors_0 = call(
        third_kernel,
        [(cells, F32), grown_shape, message, ((2 * HID, WIDTH), BF), ((16, WIDTH), BF)],
        [conv, upstream, inner_1, *returned, scatter, taps, *vectors],
        sums,
    )
    returned = give_back(sent)
    (inner_0,) = call(make_inner_kernel(0), [(cells, F32)], [grown_0, taps], cost=vpu)
    (taps_0,) = call(taps_kernel, [((64, WIDTH), BF)], [padded_0, grown_0], tap_scratch, cost=vpu)
    (grad_field,) = call(last_kernel, [(cells, BF)], [upstream_0, inner_0, *returned, scatter])
    blank = jnp.zeros((REDUCED_ROWS - 4 * HID - 160, WIDTH), BF)
    total = summed_everywhere(
        jnp.concatenate([weights_0, weights_1, vectors_0, vectors_1, taps_0, taps_1, blank])
    )
    row, wide = ((BLOCKS, WIDTH), F32), ((BLOCKS, HID), F32)
    grads = call(
        make_unpack_kernel(1.0 / math.sqrt(count * CELLS)),
        [
            ((BLOCKS, TAPS, TAPS, WIDTH), F32), row, row, row, ((BLOCKS, WIDTH, HID), F32), wide,
            ((BLOCKS, HID, WIDTH), F32), row, row,
        ],
        [total],
    )
    shape = states.shape
    return (out.reshape(shape), grad_field.reshape(shape), *grads)


def solution(mesh):
    split = Mesh(mesh.devices.reshape(2, 4, 8, 2, 2), (*TILE_AXES, "member"))
    field = P("member", TILE_AXES, None, None, None)
    return jax.shard_map(
        body,
        mesh=split,
        in_specs=(field, field) + (P(),) * 11,
        out_specs=(field, field) + (P(),) * 9,
        check_vma=False,
    )
```

time: 614 us -> 180 us (0.29); the launches traced: 606 us -> 179 us
  waiting for transfers between devices: 271 us -> 26.7 us
  other arithmetic: 85.9 us -> 3.69 us
  blocking collectives: 74.7 us -> 26.5 us
  Pallas kernels: 0 us -> 39.9 us
  between operations: 40.6 us -> 1.13 us
  matrix products: 22.6 us -> 0 us
  local copies, waits for them, and re-layouts: 36.9 us -> 14.6 us
  starting transfers between devices: 74.3 us -> 66.6 us
    psum x1 -> x0, waiting for transfers between devices: 232 us -> none  [body(): lax.psum((stacked[0], stacked[1], stacked[2], stacked[3], stacked[4], sta...]
    psum x1 -> x0, blocking collectives: 74.7 us -> none  [body(): lax.psum((stacked[0], stacked[1], stacked[2], stacked[3], stacked[4], sta...]
    pallas_call x0 -> x11, Pallas kernels: none -> 39.9 us  [call(): pl.pallas_call(kernel, out_shape=shaped(*shapes), in_specs=specs, out_spe...]
    reduce_sum x14 -> x1, other arithmetic: 39.4 us -> 0.09 us  [summed_apart(): return jnp.sum(parts.astype(F32), axis=0).astype(BF)]
    all_to_all x0 -> x1, blocking collectives: none -> 26.5 us  [summed_apart(): lax.all_to_all(value, axes, 0, 0, tiled=True).reshape(count, -1, WIDTH)]
    dot_general x12 -> x0, matrix products: 22.6 us -> none  [the longest x4 10.2 us: contract_cols(): lax.dot_general(left, right, (((1,), (1,)), ((), ())), preferred_element_...]
    add x17 -> x0, other arithmetic: 15.8 us -> none  [the longest x2 13.7 us: block_backward(): pad_grad + grown[6 - row_tap:12 - row_tap + size, 6 - col_tap:12 - col_ta...]
    ppermute x32 -> x19, starting transfers between devices: 74.3 us -> 61.1 us  [the longest x16 59.5 us: passed_along(): lax.ppermute(value, TILE_AXES, [(source, (source + steps) % count) for so...]
  transfers between devices with their start and end apart: 33 -> 20, of which waited for: 12 -> 12; matrix products, arithmetic and copies ran while one was open for 7% -> 1% of each run, Pallas kernels for 0% -> 7%
where the time goes in v1:
time: 180 us; the launch traced here: 179 us
  starting transfers between devices  66.6 us (37%)
  Pallas kernels  39.9 us (22%)
  waiting for transfers between devices  26.7 us (15%)
  blocking collectives  26.5 us (15%)
  local copies, waits for them, and re-layouts  14.6 us (8%)
  other arithmetic  3.69 us (2%)
    ppermute x16, starting transfers between devices, passed_along(): lax.ppermute(value, TILE_AXES, [(source, (source + steps) % count) for so...  59.5 us
    pallas_call x11, Pallas kernels, call(): pl.pallas_call(kernel, out_shape=shaped(*shapes), in_specs=specs, out_spe...  39.9 us
    all_to_all x1, blocking collectives, summed_apart(): lax.all_to_all(value, axes, 0, 0, tiled=True).reshape(count, -1, WIDTH)  26.5 us
    ppermute x16, waiting for transfers between devices, passed_along(): lax.ppermute(value, TILE_AXES, [(source, (source + steps) % count) for so...  22.3 us
    unnamed x69, local copies, waits for them, and re-layouts  10.2 us
    all_to_all x1, starting transfers between devices, gathered(): return lax.all_to_all(copies, axes, 0, 0, tiled=True)  5.45 us
    ppermute x3, waiting for transfers between devices, swapped(): return lax.ppermute(value, axis, [(0, 1), (1, 0)])  3.91 us
  transfers between devices with their start and end apart: 20, of which 12 were waited for; matrix products, arithmetic and copies ran while one was open for 1% of the time, Pallas kernels for 7%

profile of v1, /device:TPU:2, one launch (start us, length us, event | category | flops | bytes accessed | tf_op | source)
XLA Modules:
  0.0 179.0 jit_solution(4311070238022202389)
XLA Ops:
  0.7 0.8 copy.30.seam_ref
  1.5 0.8 copy.31.corner_ref
  2.3 0.9 copy-done.2
  3.3 3.3 %shard_map.212 = (bf16[4,128,128]{2,1,0:T(8,128)(2,1)S(1)}, bf16[512,1024]{1,0:T(8,128)(2,1)S(1)}) custom-call(s32[1]{0:T(128)} %bitcast.1.here_ref, s32[128,4]{1,0:T(8,128)S(1)} %copy.30.seam_ref, s32[128,4]{1,0:T(8,128)S(1)} %copy.31.corner_ref, bf16[1024,128]{1,0:T(8,128)(2,1)S(1)} %bitcast.44), custom_call_target="tpu_custom_call" | custom-call | tf_op jit(solution)/shard_map/pallas_call | solution.py:455
  6.7 9.4 %collective-permute-start.1 = (bf16[128,128]{1,0:T(8,128)(2,1)S(1)}, bf16[128,128]{1,0:T(8,128)(2,1)S(1)}, u32[]{:S(2)}, u32[]{:S(2)}) collective-permute-start(bf16[128,128]{1,0:T(8,128)(2,1)S(1)} %get-tuple-element.100), channel_id=1, source_target_pairs={{0,254},{2,0},{4,2},{6,4},{8,6},{10,8},{12,10},{14,12},{16,14},{18... | collective-permute-start | bytes 98312 | tf_op jit(solution)/shard_map/ppermute | solution.py:365
  16.1 1.5 collective-permute-done.west_ref
  17.7 8.6 %collective-permute-start.3 = (bf16[128,128]{1,0:T(8,128)(2,1)S(1)}, bf16[128,128]{1,0:T(8,128)(2,1)S(1)}, u32[]{:S(2)}, u32[]{:S(2)}) collective-permute-start(bf16[128,128]{1,0:T(8,128)(2,1)S(1)} %pad_maximum_fusion.1), channel_id=1, source_target_pairs={{0,248},{2,250},{4,252},{6,254},{8,0},{10,2},{12,4},{14,6},{16,8},... | collective-permute-start | bytes 98312 | tf_op jit(solution)/shard_map/ppermute | solution.py:365
  26.3 0.8 copy.32.kernel_ref
  27.1 1.1 collective-permute-done.2.north_ref
  28.2 0.7 copy-done.16
  28.9 0.7 copy-done.18
  30.3 0.7 copy-done.22
  32.4 5.9 %shard_map.213 = (bf16[1024,128]{1,0:T(8,128)(2,1)S(1)}, f32[1024,128]{1,0:T(8,128)S(1)}, f32[38,48,128]{2,1,0:T(8,128)S(1)}, bf16[4,128,128]{2,1,0:T(8,128)(2,1)S(1)}) custom-call(bf16[1024,128]{1,0:T(8,128)(2,1)S(1)} %bitcast.45, bf16[128,128]{1,0:T(8,128)(2,1)S(1)} %collective-permute-done.2.north_ref, ...), custom_call_target="tpu_custom_call" | custom-call | tf_op jit(solution)/shard_map/pallas_call | solution.py:455
  38.3 1.0 copy-done.4
  39.4 7.4 %collective-permute-start.5 = (bf16[128,128]{1,0:T(8,128)(2,1)S(1)}, bf16[128,128]{1,0:T(8,128)(2,1)S(1)}, u32[]{:S(2)}, u32[]{:S(2)}) collective-permute-start(bf16[128,128]{1,0:T(8,128)(2,1)S(1)} %get-tuple-element.96), channel_id=1, source_target_pairs={{0,254},{2,0},{4,2},{6,4},{8,6},{10,8},{12,10},{14,12},{16,14},{18... | collective-permute-start | bytes 98312 | tf_op jit(solution)/shard_map/ppermute | solution.py:365
  46.8 1.6 collective-permute-done.4.west_ref
  48.5 8.6 %collective-permute-start.7 = (bf16[128,128]{1,0:T(8,128)(2,1)S(1)}, bf16[128,128]{1,0:T(8,128)(2,1)S(1)}, u32[]{:S(2)}, u32[]{:S(2)}) collective-permute-start(bf16[128,128]{1,0:T(8,128)(2,1)S(1)} %pad_maximum_fusion.3), channel_id=1, source_target_pairs={{0,248},{2,250},{4,252},{6,254},{8,0},{10,2},{12,4},{14,6},{16,8},... | collective-permute-start | bytes 98312 | tf_op jit(solution)/shard_map/ppermute | solution.py:365
  57.2 1.9 %collective-permute-done.6.north_ref = bf16[128,128]{1,0:T(8,128)(2,1)S(1)} collective-permute-done((bf16[128,128]{1,0:T(8,128)(2,1)S(1)}, bf16[128,128]{1,0:T(8,128)(2,1)S(1)}, u32[]{:S(2)}, u32[]{:S(2)}) %collective-permute-start.6) | collective-permute-done | bytes 32800 | tf_op jit(solution)/shard_map/ppermute | solution.py:365
  59.1 9.0 %shard_map.214 = (bf16[1024,128]{1,0:T(8,128)(2,1)}, f32[38,48,128]{2,1,0:T(8,128)S(1)}, f32[38,64,128]{2,1,0:T(8,128)S(1)}, bf16[4,128,128]{2,1,0:T(8,128)(2,1)...) custom-call(bf16[1024,128]{1,0:T(8,128)(2,1)S(1)} %get-tuple-element.39.field_ref, ...), custom_call_target="tpu_custom_call" | custom-call | tf_op jit(solution)/shard_map/pallas_call | solution.py:455
  68.1 0.9 copy-done.6
  69.1 8.7 %collective-permute-start.8 = (bf16[128,128]{1,0:T(8,128)(2,1)S(1)}, bf16[128,128]{1,0:T(8,128)(2,1)S(1)}, u32[]{:S(2)}, u32[]{:S(2)}) collective-permute-start(bf16[128,128]{1,0:T(8,128)(2,1)S(1)} %get-tuple-element.92), channel_id=1, source_target_pairs={{0,248},{2,250},{4,252},{6,254},{8,0},{10,2},{12,4},{14,6},{16,8},... | collective-permute-start | bytes 98312 | tf_op jit(solution)/shard_map/ppermute | solution.py:365
  77.8 1.8 %collective-permute-done.9.second_ref = bf16[128,128]{1,0:T(8,128)(2,1)S(1)} collective-permute-done((bf16[128,128]{1,0:T(8,128)(2,1)S(1)}, bf16[128,128]{1,0:T(8,128)(2,1)S(1)}, u32[]{:S(2)}, u32[]{:S(2)}) %collective-permute-start.9) | collective-permute-done | bytes 32800 | tf_op jit(solution)/shard_map/ppermute | solution.py:365
  80.3 5.3 %collective-permute-start.10 = (bf16[128,128]{1,0:T(8,128)(2,1)}, bf16[128,128]{1,0:T(8,128)(2,1)}, u32[]{:S(2)}, u32[]{:S(2)}) collective-permute-start(bf16[128,128]{1,0:T(8,128)(2,1)} %pad_maximum_fusion.4), channel_id=1, source_target_pairs={{0,254},{2,0},{4,2},{6,4},{8,6},{10,8},{12,10},{14,12},{16,14},{18... | collective-permute-start | bytes 98312 | tf_op jit(solution)/shard_map/ppermute | solution.py:365
  86.1 3.0 %shard_map.216.scatter_ref = bf16[1024,512]{1,0:T(8,128)(2,1)S(1)} custom-call(s32[1]{0:T(128)} %bitcast.1.here_ref, s32[128,4]{1,0:T(8,128)S(1)} %copy.30.seam_ref, s32[128,4]{1,0:T(8,128)S(1)} %copy.31.corner_ref), custom_call_target="tpu_custom_call" | custom-call | tf_op jit(solution)/shard_map/pallas_call | solution.py:455
  89.1 3.0 %shard_map.215.inner_ref = f32[1024,128]{1,0:T(8,128)S(1)} custom-call(f32[38,64,128]{2,1,0:T(8,128)S(1)} %get-tuple-element.43.grown_ref, f32[2,49,128]{2,1,0:T(8,128)S(1)} %copy.32.kernel_ref), custom_call_target="tpu_custom_call" | custom-call | flops 12845056 | bytes 3145728 | tf_op jit(solution)/shard_map/pallas_call | solution.py:455
  92.2 1.8 %shard_map.221 = bf16[64,128]{1,0:T(8,128)(2,1)S(1)} custom-call(f32[38,48,128]{2,1,0:T(8,128)S(1)} %copy-done.7, f32[38,64,128]{2,1,0:T(8,128)S(1)} %get-tuple-element.43.grown_ref), custom_call_target="tpu_custom_call" | custom-call | flops 12845056 | bytes 3145728 | tf_op jit(solution)/shard_map/pallas_call | solution.py:455
  94.1 1.4 collective-permute-done.11.fourth_ref
  95.5 6.6 %shard_map.217 = (f32[1024,128]{1,0:T(8,128)S(1)}, f32[38,64,128]{2,1,0:T(8,128)S(1)}, bf16[4,128,128]{2,1,0:T(8,128)(2,1)S(1)}, bf16[1024,128]{1,0:T(8,128)(2,1)S(1)}, bf16[16,128]{1,0:T(8,128)(2,1)S(1)}) custom-call(f32[1024,128]{1,0:T(8,128)S(1)} %copy-done.11, bf16[1024,128]{1,0:T(8,128)(2,1)S(1)} %bitcast.47, f32[1024,128]{1,0:T(8,128)S(1)} %shard_map.215.inner_ref, ...), custom_call_target="tpu_custom_call" | custom-call | tf_op jit(solution)/shard_map/pallas_call | solution.py:455
  102.2 1.9 %shard_map.220 = bf16[64,128]{1,0:T(8,128)(2,1)S(1)} custom-call(f32[38,48,128]{2,1,0:T(8,128)S(1)} %copy-done.5, f32[38,64,128]{2,1,0:T(8,128)S(1)} %get-tuple-element.46.grown_ref), custom_call_target="tpu_custom_call" | custom-call | flops 12845056 | bytes 3145728 | tf_op jit(solution)/shard_map/pallas_call | solution.py:455
  104.2 0.8 copy-done.28
  105.2 1.7 collective-permute-done.16
  106.9 1.1 fusion
  108.0 0.8 all_to_all.12
  108.8 26.5 %all_to_all.18 = bf16[64,18,128]{2,1,0:T(8,128)(2,1)S(1)} all-to-all(bf16[64,18,128]{2,1,0:T(8,128)(2,1)} %all_to_all.12), channel_id=1, replica_groups=mesh['far'=2,'y'=4,'z'=8,'core'=2,'member'=2] {'far','y','z'}, dimensions={0} | all-to-all | bytes 589824 | tf_op jit(solution)/shard_map/all_to_all | solution.py:408
  135.5 1.5 collective-permute-start.17
  137.0 2.2 %collective-permute-done.17 = bf16[18,128]{1,0:T(8,128)(2,1)S(1)} collective-permute-done((bf16[18,128]{1,0:T(8,128)(2,1)S(1)}, bf16[18,128]{1,0:T(8,128)(2,1)S(1)}, u32[]{:S(2)}, u32[]{:S(2)}) %collective-permute-start.17) | collective-permute-done | bytes 4640 | tf_op jit(solution)/shard_map/ppermute | solution.py:388
  139.2 0.8 broadcast_in_dim.10
  140.0 5.5 %all-to-all-start.1 = ((bf16[64,18,128]{2,1,0:T(8,128)(2,1)}), bf16[64,18,128]{2,1,0:T(8,128)(2,1)}, u32[]{:S(2)}, u32[]{:S(2)}) async-start(bf16[64,18,128]{2,1,0:T(8,128)(2,1)} %broadcast_in_dim.10), calls=%async_computation.1 | async-start | bytes 786432 | tf_op jit(solution)/shard_map/all_to_all | solution.py:415
  145.4 2.4 %collective-permute-start.13 = (bf16[128,128]{1,0:T(8,128)(2,1)S(1)}, bf16[128,128]{1,0:T(8,128)(2,1)S(1)}, u32[]{:S(2)}, u32[]{:S(2)}) collective-permute-start(bf16[128,128]{1,0:T(8,128)(2,1)S(1)} %get-tuple-element.87), channel_id=1, source_target_pairs={{0,8},{2,10},{4,12},{6,14},{8,16},{10,18},{12,20},{14,22},{16,24},... | collective-permute-start | bytes 98312 | tf_op jit(solution)/shard_map/ppermute | solution.py:365
  147.8 6.3 %collective-permute-start.12 = (bf16[128,128]{1,0:T(8,128)(2,1)S(1)}, bf16[128,128]{1,0:T(8,128)(2,1)S(1)}, u32[]{:S(2)}, u32[]{:S(2)}) collective-permute-start(bf16[128,128]{1,0:T(8,128)(2,1)S(1)} %get-tuple-element.88), channel_id=1, source_target_pairs={{0,248},{2,250},{4,252},{6,254},{8,0},{10,2},{12,4},{14,6},{16,8},... | collective-permute-start | bytes 98312 | tf_op jit(solution)/shard_map/ppermute | solution.py:365
  154.2 6.8 %collective-permute-done.13.second_ref = bf16[128,128]{1,0:T(8,128)(2,1)S(1)} collective-permute-done((bf16[128,128]{1,0:T(8,128)(2,1)S(1)}, bf16[128,128]{1,0:T(8,128)(2,1)S(1)}, u32[]{:S(2)}, u32[]{:S(2)}) %collective-permute-start.13) | collective-permute-done | bytes 32800 | tf_op jit(solution)/shard_map/ppermute | solution.py:365
  161.5 1.8 %all_to_all.15 = bf16[1152,128]{1,0:T(8,128)(2,1)} reshape(bf16[64,18,128]{2,1,0:T(8,128)(2,1)} %all-to-all-done.1) | data formatting | bytes 589824 | tf_op jit(solution)/shard_map/all_to_all | solution.py:415
  163.3 2.5 %collective-permute-start.14 = (bf16[128,128]{1,0:T(8,128)(2,1)S(1)}, bf16[128,128]{1,0:T(8,128)(2,1)S(1)}, u32[]{:S(2)}, u32[]{:S(2)}) collective-permute-start(bf16[128,128]{1,0:T(8,128)(2,1)S(1)} %pad_maximum_fusion.6), channel_id=1, source_target_pairs={{0,254},{2,0},{4,2},{6,4},{8,6},{10,8},{12,10},{14,12},{16,14},{18... | collective-permute-start | bytes 98312 | tf_op jit(solution)/shard_map/ppermute | solution.py:365
  165.8 3.0 %shard_map.218.inner_ref = f32[1024,128]{1,0:T(8,128)S(1)} custom-call(f32[38,64,128]{2,1,0:T(8,128)S(1)} %get-tuple-element.46.grown_ref, f32[2,49,128]{2,1,0:T(8,128)S(1)} %copy.32.kernel_ref), custom_call_target="tpu_custom_call" | custom-call | flops 12845056 | bytes 3145728 | tf_op jit(solution)/shard_map/pallas_call | solution.py:455
  168.8 6.1 %collective-permute-done.15.fourth_ref = bf16[128,128]{1,0:T(8,128)(2,1)S(1)} collective-permute-done((bf16[128,128]{1,0:T(8,128)(2,1)S(1)}, bf16[128,128]{1,0:T(8,128)(2,1)S(1)}, u32[]{:S(2)}, u32[]{:S(2)}) %collective-permute-start.15) | collective-permute-done | bytes 32800 | tf_op jit(solution)/shard_map/ppermute | solution.py:365
  174.9 1.1 shard_map.219
  176.0 1.2 maximum_select_fusion.sum_ref
  177.2 1.2 shard_map.222
  (107 shorter events, 5.3 us)
Async XLA Ops:
  0.6 27.6 %copy-start.1 = (bf16[2,512,128]{2,1,0:T(8,128)(2,1)S(1)}, bf16[2,512,128]{2,1,0:T(8,128)(2,1)}, u32[]{:S(2)}) copy-start(bf16[2,512,128]{2,1,0:T(8,128)(2,1)} %down_ref.5) | copy-start | bytes 786436
  0.7 27.6 %copy-start = (bf16[2,128,512]{2,1,0:T(8,128)(2,1)S(1)}, bf16[2,128,512]{2,1,0:T(8,128)(2,1)}, u32[]{:S(2)}) copy-start(bf16[2,128,512]{2,1,0:T(8,128)(2,1)} %up_ref.5) | copy-start | bytes 786436
  2.3 1.0 copy-start.2
  6.6 11.0 %collective-permute-start = (bf16[128,128]{1,0:T(8,128)(2,1)S(1)}, bf16[128,128]{1,0:T(8,128)(2,1)S(1)}, u32[]{:S(2)}, u32[]{:S(2)}) collective-permute-start(bf16[128,128]{1,0:T(8,128)(2,1)S(1)} %get-tuple-element.99), channel_id=1, source_target_pairs={{0,2},{2,4},{4,6},{6,8},{8,10},{10,12},{12,14},{14,16},{16,18},{18... | collective-permute-start | bytes 98312 | tf_op jit(solution)/shard_map/ppermute | solution.py:365
  6.7 11.0 %collective-permute-start.1 = (bf16[128,128]{1,0:T(8,128)(2,1)S(1)}, bf16[128,128]{1,0:T(8,128)(2,1)S(1)}, u32[]{:S(2)}, u32[]{:S(2)}) collective-permute-start(bf16[128,128]{1,0:T(8,128)(2,1)S(1)} %get-tuple-element.100), channel_id=1, source_target_pairs={{0,254},{2,0},{4,2},{6,4},{8,6},{10,8},{12,10},{14,12},{16,14},{18... | collective-permute-start | bytes 98312 | tf_op jit(solution)/shard_map/ppermute | solution.py:365
  17.7 10.5 %collective-permute-start.2 = (bf16[128,128]{1,0:T(8,128)(2,1)S(1)}, bf16[128,128]{1,0:T(8,128)(2,1)S(1)}, u32[]{:S(2)}, u32[]{:S(2)}) collective-permute-start(bf16[128,128]{1,0:T(8,128)(2,1)S(1)} %pad_maximum_fusion), channel_id=1, source_target_pairs={{0,8},{2,10},{4,12},{6,14},{8,16},{10,18},{12,20},{14,22},{16,24},... | collective-permute-start | bytes 98312 | tf_op jit(solution)/shard_map/ppermute | solution.py:365
  17.7 10.5 %collective-permute-start.3 = (bf16[128,128]{1,0:T(8,128)(2,1)S(1)}, bf16[128,128]{1,0:T(8,128)(2,1)S(1)}, u32[]{:S(2)}, u32[]{:S(2)}) collective-permute-start(bf16[128,128]{1,0:T(8,128)(2,1)S(1)} %pad_maximum_fusion.1), channel_id=1, source_target_pairs={{0,248},{2,250},{4,252},{6,254},{8,0},{10,2},{12,4},{14,6},{16,8},... | collective-permute-start | bytes 98312 | tf_op jit(solution)/shard_map/ppermute | solution.py:365
  28.2 0.7 copy-start.16
  28.9 0.7 copy-start.18
  29.6 0.7 copy-start.20
  30.3 0.7 copy-start.22
  32.3 26.7 %copy-start.3 = (bf16[1,1,32,32,128]{4,3,2,1,0:T(8,128)(2,1)S(1)}, bf16[1,1,32,32,128]{4,3,2,1,0:T(8,128)(2,1)}, u32[]{:S(2)}) copy-start(bf16[1,1,32,32,128]{4,3,2,1,0:T(8,128)(2,1)} %param.14) | copy-start | bytes 786436
  32.3 26.7 %copy-start.17 = (f32[2,512]{1,0:T(2,128)S(1)}, f32[2,512]{1,0:T(2,128)}, u32[]{:S(2)}) copy-start(f32[2,512]{1,0:T(2,128)} %up_b_ref.5) | copy-start | bytes 12292
  32.3 26.7 %copy-start.19 = (f32[2,128]{1,0:T(2,128)S(1)}, f32[2,128]{1,0:T(2,128)}, u32[]{:S(2)}) copy-start(f32[2,128]{1,0:T(2,128)} %gain_ref.5) | copy-start | bytes 3076
  32.3 26.7 %copy-start.21 = (f32[2,128]{1,0:T(2,128)S(1)}, f32[2,128]{1,0:T(2,128)}, u32[]{:S(2)}) copy-start(f32[2,128]{1,0:T(2,128)} %offset_ref.5) | copy-start | bytes 3076
  32.3 26.7 %copy-start.23 = (f32[2,128]{1,0:T(2,128)S(1)}, f32[2,128]{1,0:T(2,128)}, u32[]{:S(2)}) copy-start(f32[2,128]{1,0:T(2,128)} %down_b_ref.5) | copy-start | bytes 3076
  32.3 26.7 %copy-start.25 = (f32[2,128]{1,0:T(2,128)S(1)}, f32[2,128]{1,0:T(2,128)}, u32[]{:S(2)}) copy-start(f32[2,128]{1,0:T(2,128)} %scale_ref.5) | copy-start | bytes 3076
  32.4 26.7 %copy-start.27 = (f32[2,128]{1,0:T(2,128)S(1)}, f32[2,128]{1,0:T(2,128)}, u32[]{:S(2)}) copy-start(f32[2,128]{1,0:T(2,128)} %bias_ref.3) | copy-start | bytes 3076
  38.3 1.0 copy-start.4
  39.3 46.8 %copy-start.10 = (f32[1024,128]{1,0:T(8,128)}, f32[1024,128]{1,0:T(8,128)S(1)}, u32[]{:S(2)}) copy-start(f32[1024,128]{1,0:T(8,128)S(1)} %get-tuple-element.42.conv_ref) | copy-start | bytes 1572868
  39.3 9.1 %collective-permute-start.4 = (bf16[128,128]{1,0:T(8,128)(2,1)S(1)}, bf16[128,128]{1,0:T(8,128)(2,1)S(1)}, u32[]{:S(2)}, u32[]{:S(2)}) collective-permute-start(bf16[128,128]{1,0:T(8,128)(2,1)S(1)} %get-tuple-element.95), channel_id=1, source_target_pairs={{0,2},{2,4},{4,6},{6,8},{8,10},{10,12},{12,14},{14,16},{16,18},{18... | collective-permute-start | bytes 98312 | tf_op jit(solution)/shard_map/ppermute | solution.py:365
  39.4 9.0 %collective-permute-start.5 = (bf16[128,128]{1,0:T(8,128)(2,1)S(1)}, bf16[128,128]{1,0:T(8,128)(2,1)S(1)}, u32[]{:S(2)}, u32[]{:S(2)}) collective-permute-start(bf16[128,128]{1,0:T(8,128)(2,1)S(1)} %get-tuple-element.96), channel_id=1, source_target_pairs={{0,254},{2,0},{4,2},{6,4},{8,6},{10,8},{12,10},{14,12},{16,14},{18... | collective-permute-start | bytes 98312 | tf_op jit(solution)/shard_map/ppermute | solution.py:365
  48.4 10.6 %collective-permute-start.6 = (bf16[128,128]{1,0:T(8,128)(2,1)S(1)}, bf16[128,128]{1,0:T(8,128)(2,1)S(1)}, u32[]{:S(2)}, u32[]{:S(2)}) collective-permute-start(bf16[128,128]{1,0:T(8,128)(2,1)S(1)} %pad_maximum_fusion.2), channel_id=1, source_target_pairs={{0,8},{2,10},{4,12},{6,14},{8,16},{10,18},{12,20},{14,22},{16,24},... | collective-permute-start | bytes 98312 | tf_op jit(solution)/shard_map/ppermute | solution.py:365
  48.5 10.5 %collective-permute-start.7 = (bf16[128,128]{1,0:T(8,128)(2,1)S(1)}, bf16[128,128]{1,0:T(8,128)(2,1)S(1)}, u32[]{:S(2)}, u32[]{:S(2)}) collective-permute-start(bf16[128,128]{1,0:T(8,128)(2,1)S(1)} %pad_maximum_fusion.3), channel_id=1, source_target_pairs={{0,248},{2,250},{4,252},{6,254},{8,0},{10,2},{12,4},{14,6},{16,8},... | collective-permute-start | bytes 98312 | tf_op jit(solution)/shard_map/ppermute | solution.py:365
  68.1 0.9 copy-start.6
  69.1 10.5 %collective-permute-start.9 = (bf16[128,128]{1,0:T(8,128)(2,1)S(1)}, bf16[128,128]{1,0:T(8,128)(2,1)S(1)}, u32[]{:S(2)}, u32[]{:S(2)}) collective-permute-start(bf16[128,128]{1,0:T(8,128)(2,1)S(1)} %get-tuple-element.91), channel_id=1, source_target_pairs={{0,8},{2,10},{4,12},{6,14},{8,16},{10,18},{12,20},{14,22},{16,24},... | collective-permute-start | bytes 98312 | tf_op jit(solution)/shard_map/ppermute | solution.py:365
  69.1 10.5 %collective-permute-start.8 = (bf16[128,128]{1,0:T(8,128)(2,1)S(1)}, bf16[128,128]{1,0:T(8,128)(2,1)S(1)}, u32[]{:S(2)}, u32[]{:S(2)}) collective-permute-start(bf16[128,128]{1,0:T(8,128)(2,1)S(1)} %get-tuple-element.92), channel_id=1, source_target_pairs={{0,248},{2,250},{4,252},{6,254},{8,0},{10,2},{12,4},{14,6},{16,8},... | collective-permute-start | bytes 98312 | tf_op jit(solution)/shard_map/ppermute | solution.py:365
  79.6 6.5 %copy-start.12 = (bf16[128,128]{1,0:T(8,128)(2,1)}, bf16[128,128]{1,0:T(8,128)(2,1)S(1)}, u32[]{:S(2)}) copy-start(bf16[128,128]{1,0:T(8,128)(2,1)S(1)} %collective-permute-done.9.second_ref) | copy-start | bytes 98308
  79.6 6.5 %copy-start.14 = (bf16[128,128]{1,0:T(8,128)(2,1)}, bf16[128,128]{1,0:T(8,128)(2,1)S(1)}, u32[]{:S(2)}) copy-start(bf16[128,128]{1,0:T(8,128)(2,1)S(1)} %collective-permute-done.8.first_ref) | copy-start | bytes 98308
  80.3 13.8 %collective-permute-start.10 = (bf16[128,128]{1,0:T(8,128)(2,1)}, bf16[128,128]{1,0:T(8,128)(2,1)}, u32[]{:S(2)}, u32[]{:S(2)}) collective-permute-start(bf16[128,128]{1,0:T(8,128)(2,1)} %pad_maximum_fusion.4), channel_id=1, source_target_pairs={{0,254},{2,0},{4,2},{6,4},{8,6},{10,8},{12,10},{14,12},{16,14},{18... | collective-permute-start | bytes 98312 | tf_op jit(solution)/shard_map/ppermute | solution.py:365
  86.1 9.4 %collective-permute-start.11 = (bf16[128,128]{1,0:T(8,128)(2,1)}, bf16[128,128]{1,0:T(8,128)(2,1)}, u32[]{:S(2)}, u32[]{:S(2)}) collective-permute-start(bf16[128,128]{1,0:T(8,128)(2,1)} %pad_maximum_fusion.5), channel_id=1, source_target_pairs={{0,2},{2,4},{4,6},{6,8},{8,10},{10,12},{12,14},{14,16},{16,18},{18... | collective-permute-start | bytes 98312 | tf_op jit(solution)/shard_map/ppermute | solution.py:365
  89.1 3.1 %copy-start.7 = (f32[38,48,128]{2,1,0:T(8,128)S(1)}, f32[38,48,128]{2,1,0:T(8,128)}, u32[]{:S(2)}) copy-start(f32[38,48,128]{2,1,0:T(8,128)} %copy-done.6) | copy-start | bytes 2801668
  92.2 3.3 %copy-start.11 = (f32[1024,128]{1,0:T(8,128)S(1)}, f32[1024,128]{1,0:T(8,128)}, u32[]{:S(2)}) copy-start(f32[1024,128]{1,0:T(8,128)} %copy-done.10) | copy-start | bytes 1572868
  92.2 3.3 %copy-start.13 = (bf16[128,128]{1,0:T(8,128)(2,1)S(1)}, bf16[128,128]{1,0:T(8,128)(2,1)}, u32[]{:S(2)}) copy-start(bf16[128,128]{1,0:T(8,128)(2,1)} %copy-done.12) | copy-start | bytes 98308
  92.2 3.3 %copy-start.15 = (bf16[128,128]{1,0:T(8,128)(2,1)S(1)}, bf16[128,128]{1,0:T(8,128)(2,1)}, u32[]{:S(2)}) copy-start(bf16[128,128]{1,0:T(8,128)(2,1)} %copy-done.14) | copy-start | bytes 98308
  95.5 6.7 %copy-start.5 = (f32[38,48,128]{2,1,0:T(8,128)S(1)}, f32[38,48,128]{2,1,0:T(8,128)}, u32[]{:S(2)}) copy-start(f32[38,48,128]{2,1,0:T(8,128)} %copy-done.4) | copy-start | bytes 2801668
  102.2 1.9 %copy-start.8 = (f32[1024,128]{1,0:T(8,128)}, f32[1024,128]{1,0:T(8,128)S(1)}, u32[]{:S(2)}) copy-start(f32[1024,128]{1,0:T(8,128)S(1)} %get-tuple-element.45.upstream_ref) | copy-start | bytes 1572868
  104.2 0.8 copy-start.28
  105.1 1.8 %collective-permute-start.16 = (bf16[1152,128]{1,0:T(8,128)(2,1)S(1)}, bf16[1152,128]{1,0:T(8,128)(2,1)}, u32[]{:S(2)}, u32[]{:S(2)}) collective-permute-start(bf16[1152,128]{1,0:T(8,128)(2,1)S(1)} %dynamic-slice_bitcast_fusion), channel_id=1, source_target_pairs={{0,2},{2,0},{1,3},{3,1},{4,6},{6,4},{5,7},{7,5},{8,10},{10,8},{9,1... | collective-permute-start | bytes 884744 | tf_op jit(solution)/shard_map/ppermute | solution.py:388
  135.5 3.7 %collective-permute-start.17 = (bf16[18,128]{1,0:T(8,128)(2,1)S(1)}, bf16[18,128]{1,0:T(8,128)(2,1)S(1)}, u32[]{:S(2)}, u32[]{:S(2)}) collective-permute-start(bf16[18,128]{1,0:T(8,128)(2,1)S(1)} %reduce_sum.12), channel_id=1, source_target_pairs={{0,1},{1,0},{2,3},{3,2},{4,5},{5,4},{6,7},{7,6},{8,9},{9,8},{10,11... | collective-permute-start | bytes 13832 | tf_op jit(solution)/shard_map/ppermute | solution.py:388
  140.0 21.5 %all-to-all-start.1 = ((bf16[64,18,128]{2,1,0:T(8,128)(2,1)}), bf16[64,18,128]{2,1,0:T(8,128)(2,1)}, u32[]{:S(2)}, u32[]{:S(2)}) async-start(bf16[64,18,128]{2,1,0:T(8,128)(2,1)} %broadcast_in_dim.10), calls=%async_computation.1 | async-start | bytes 786432 | tf_op jit(solution)/shard_map/all_to_all | solution.py:415
  145.4 15.5 %collective-permute-start.13 = (bf16[128,128]{1,0:T(8,128)(2,1)S(1)}, bf16[128,128]{1,0:T(8,128)(2,1)S(1)}, u32[]{:S(2)}, u32[]{:S(2)}) collective-permute-start(bf16[128,128]{1,0:T(8,128)(2,1)S(1)} %get-tuple-element.87), channel_id=1, source_target_pairs={{0,8},{2,10},{4,12},{6,14},{8,16},{10,18},{12,20},{14,22},{16,24},... | collective-permute-start | bytes 98312 | tf_op jit(solution)/shard_map/ppermute | solution.py:365
  147.8 15.5 %collective-permute-start.12 = (bf16[128,128]{1,0:T(8,128)(2,1)S(1)}, bf16[128,128]{1,0:T(8,128)(2,1)S(1)}, u32[]{:S(2)}, u32[]{:S(2)}) collective-permute-start(bf16[128,128]{1,0:T(8,128)(2,1)S(1)} %get-tuple-element.88), channel_id=1, source_target_pairs={{0,248},{2,250},{4,252},{6,254},{8,0},{10,2},{12,4},{14,6},{16,8},... | collective-permute-start | bytes 98312 | tf_op jit(solution)/shard_map/ppermute | solution.py:365
  160.9 13.9 %copy-start.9 = (f32[1024,128]{1,0:T(8,128)S(1)}, f32[1024,128]{1,0:T(8,128)}, u32[]{:S(2)}) copy-start(f32[1024,128]{1,0:T(8,128)} %copy-done.8) | copy-start | bytes 1572868
  163.3 12.7 %collective-permute-start.18 = (bf16[1152,128]{1,0:T(8,128)(2,1)}, bf16[1152,128]{1,0:T(8,128)(2,1)}, u32[]{:S(2)}, u32[]{:S(2)}) collective-permute-start(bf16[1152,128]{1,0:T(8,128)(2,1)} %all_to_all.15), channel_id=1, source_target_pairs={{0,2},{2,0},{1,3},{3,1},{4,6},{6,4},{5,7},{7,5},{8,10},{10,8},{9,1... | collective-permute-start | bytes 884744 | tf_op jit(solution)/shard_map/ppermute | solution.py:388
  163.3 5.5 %collective-permute-start.14 = (bf16[128,128]{1,0:T(8,128)(2,1)S(1)}, bf16[128,128]{1,0:T(8,128)(2,1)S(1)}, u32[]{:S(2)}, u32[]{:S(2)}) collective-permute-start(bf16[128,128]{1,0:T(8,128)(2,1)S(1)} %pad_maximum_fusion.6), channel_id=1, source_target_pairs={{0,254},{2,0},{4,2},{6,4},{8,6},{10,8},{12,10},{14,12},{16,14},{18... | collective-permute-start | bytes 98312 | tf_op jit(solution)/shard_map/ppermute | solution.py:365
  165.8 9.1 %collective-permute-start.15 = (bf16[128,128]{1,0:T(8,128)(2,1)S(1)}, bf16[128,128]{1,0:T(8,128)(2,1)S(1)}, u32[]{:S(2)}, u32[]{:S(2)}) collective-permute-start(bf16[128,128]{1,0:T(8,128)(2,1)S(1)} %pad_maximum_fusion.7), channel_id=1, source_target_pairs={{0,2},{2,4},{4,6},{6,8},{8,10},{10,12},{12,14},{14,16},{16,18},{18... | collective-permute-start | bytes 98312 | tf_op jit(solution)/shard_map/ppermute | solution.py:365
  174.9 1.1 copy-start.29
  (2 other events, 1.4 us)

commit v2 on v1

v2 whole, which is shorter than its diff:
```python
import math

import jax
import jax.numpy as jnp
from jax import lax
from jax.experimental import pallas as pl
from jax.experimental.pallas import tpu as pltpu
from jax.sharding import Mesh, PartitionSpec as P

BF = jnp.bfloat16
F32 = jnp.float32
BLOCKS = 2
SIZE = 32
CELLS = SIZE * SIZE
WIDTH = 128
HID = 512
TAPS = 7
CHUNK = 256
PAD_ROWS = 38
PAD_COLS = 48
GROWN_COLS = 64
MESSAGE = 128
TILES = 128
PARAM_ROWS = 58
EPSILON = 1e-06
GELU_C = 0.7978845608028654
GELU_A = 0.044715
TILE_AXES = ("far", "y", "z", "core")
VMEM_LIMIT = 16 * 1024 * 1024


def kernel_params():
    return pltpu.CompilerParams(vmem_limit_bytes=VMEM_LIMIT)


def whole(count):
    return [pl.BlockSpec(memory_space=pltpu.VMEM)] * count


def onehot(condition):
    return jnp.where(condition, 1.0, 0.0).astype(BF)


def matmul(left, right, dims=((1,), (0,))):
    return lax.dot_general(left, right, (dims, ((), ())), preferred_element_type=F32)


def strip_cells(code, slot, facing):
    along = slot & 31
    depth = slot >> 5
    depth = 2 - depth if facing in (0, 2) else depth
    edge = code & 3
    along = jnp.where(code >= 4, 31 - along, along)
    depth = jnp.where((edge & 1) == 1, 31 - depth, depth)
    return jnp.where(edge < 2, depth * SIZE + along, along * SIZE + depth)


def corner_cells(first, second, slot):
    at = jnp.where(slot < 112, slot - 96, slot - 112)
    code = jnp.where(slot < 112, first, second)
    row = (at * 11) >> 5
    col = at - 3 * row
    block = (row + 29 * (code >> 1)) * SIZE + col + 29 * (code & 1)
    return jnp.where((at >= 0) & (at < 9) & (code < 4), block, -1)


def side_of(here, shift):
    return (here >> shift) & 1


def slot_of_facing(here, facing):
    row_side, col_side = side_of(here, 2), side_of(here, 0)
    return (row_side, 1 - row_side, 2 + col_side, 3 - col_side)[facing]


def seam_of(codes_ref, here, facing):
    step = (4, -4, 1, -1)[facing]
    return codes_ref[facing, (here + step) & (TILES - 1)]


def corner_of(codes_ref, here, step, direction):
    return codes_ref[4 + direction, (here + step) & (TILES - 1)]


def gathered_cells(codes_ref, here, facing, slot):
    strip = strip_cells(seam_of(codes_ref, here, facing), slot, facing)
    if facing < 2:
        return jnp.where(slot < 96, strip, -1)
    if facing == 2:
        below, above = corner_of(codes_ref, here, 5, 0), corner_of(codes_ref, here, -3, 2)
        flip = side_of(here + 1, 2)
    else:
        below, above = corner_of(codes_ref, here, 3, 1), corner_of(codes_ref, here, -5, 3)
        flip = side_of(here - 1, 2)
    first, second = jnp.where(flip == 0, below, above), jnp.where(flip == 0, above, below)
    return jnp.where(slot < 96, strip, corner_cells(first, second, slot))


def scattered_cells(codes_ref, here, facing, slot):
    strip = strip_cells(seam_of(codes_ref, here, facing), slot, facing)
    if facing >= 2:
        return jnp.where(slot < 96, strip, -1)
    if facing == 0:
        right, left = corner_of(codes_ref, here, 5, 0), corner_of(codes_ref, here, 3, 1)
    else:
        right, left = corner_of(codes_ref, here, -3, 2), corner_of(codes_ref, here, -5, 3)
    flip = side_of(here, 0)
    first, second = jnp.where(flip == 0, right, left), jnp.where(flip == 0, left, right)
    return jnp.where(slot < 96, strip, corner_cells(first, second, slot))


def select_kernel(here_ref, codes_ref, field_ref, sent_ref, gather_ref, owners_ref):
    here = here_ref[0]
    slot = iota((MESSAGE, WIDTH), 0)
    lane = iota((MESSAGE, WIDTH), 1)
    for facing in range(4):
        cells = gathered_cells(codes_ref, here, facing, slot)
        for part in range(CELLS // WIDTH):
            chosen = onehot(cells == lane + part * WIDTH)
            gather_ref[facing * MESSAGE : (facing + 1) * MESSAGE, part * WIDTH : (part + 1) * WIDTH] = chosen
    send_cells(here, gather_ref[...], field_ref[...], sent_ref)
    slot = iota((8, MESSAGE), 1)
    for facing in range(4):
        owners_ref[slot_of_facing(here, facing)] = scattered_cells(codes_ref, here, facing, slot)


def send_cells(here, gather, field, sent_ref):
    sent = matmul(gather, field).astype(BF)
    for facing in range(4):
        sent_ref[slot_of_facing(here, facing)] = sent[facing * MESSAGE : (facing + 1) * MESSAGE]


def scatter_kernel(owners_ref, scatter_ref):
    cell = iota((CELLS, MESSAGE), 0)
    for slot in range(4):
        scatter_ref[:, slot * MESSAGE : (slot + 1) * MESSAGE] = onehot(cell == owners_ref[slot][0:1])


def row_rim_slots(position, strip, left=None, right=None):
    depth = jnp.where(position >= 96, 2, jnp.where(position >= 48, 1, 0))
    along = position - 48 * depth - 5
    slot = jnp.full_like(position, -1)
    if strip:
        slot = jnp.where((along >= 3) & (along < 35), 32 * depth + along - 3, slot)
    if left is not None:
        slot = jnp.where((along >= 0) & (along < 3), left + 3 * depth + along, slot)
    if right is not None:
        slot = jnp.where((along >= 35) & (along < 38), right + 3 * depth + along - 35, slot)
    return slot


def col_rim_slots(position, first):
    depth = (position & 7) - first
    slot = 32 * depth + (position >> 3)
    return jnp.where((depth >= 0) & (depth < 3), slot, -1)


def iota(shape, dim):
    return lax.broadcasted_iota(jnp.int32, shape, dim)


def fill_inside(padded_ref, here, field, by_a, by_b):
    side = side_of(here, 0)
    west, east = jnp.where(side == 0, by_b, by_a), jnp.where(side == 0, by_a, by_b)
    cols = (SIZE * 8, MESSAGE)
    place = onehot(col_rim_slots(iota(cols, 0), 5) == iota(cols, 1))
    padded_ref[3:35, 0:8] = matmul(place, west).reshape(SIZE, 8, WIDTH)
    place = onehot(col_rim_slots(iota(cols, 0), 0) == iota(cols, 1))
    padded_ref[3:35, 40:48] = matmul(place, east).reshape(SIZE, 8, WIDTH)
    padded_ref[3:35, 8:40] = field.astype(F32).reshape(SIZE, SIZE, WIDTH)


def fill_rims(padded_ref, here, by_c, by_d):
    row_side, col_side = side_of(here, 2), side_of(here, 0)
    north, south = jnp.where(row_side == 0, by_d, by_c), jnp.where(row_side == 0, by_c, by_d)
    rows = (3 * PAD_COLS, MESSAGE)
    slots = row_rim_slots(iota(rows, 0), True, 112 - 16 * col_side, 96 + 16 * col_side)
    place = onehot(slots == iota(rows, 1))
    padded_ref[0:3] = matmul(place, north).reshape(3, PAD_COLS, WIDTH)
    padded_ref[35:38] = matmul(place, south).reshape(3, PAD_COLS, WIDTH)


def tap(kernel, row_tap, col_tap):
    ref, block = kernel
    return ref[row_tap * TAPS + col_tap, block : block + 1, :]


def convolve(source_ref, first_col, kernel_ref, flipped, start, out_ref, first=0, last=SIZE // 4):
    def group(index, carry):
        totals = [jnp.broadcast_to(start, (SIZE, WIDTH)) for _ in range(4)]
        for col_tap in range(TAPS):
            for row in range(4 + TAPS - 1):
                values = source_ref[index * 4 + row, first_col + col_tap : first_col + col_tap + SIZE, :]
                for out in range(max(0, row - TAPS + 1), min(4, row + 1)):
                    a, e = row - out, col_tap
                    if flipped:
                        a, e = TAPS - 1 - a, TAPS - 1 - e
                    totals[out] = totals[out] + values * tap(kernel_ref, a, e)
        for out in range(4):
            out_ref[pl.ds(pl.multiple_of(index * 128 + out * SIZE, SIZE), SIZE), :] = totals[out]
        return carry

    lax.fori_loop(first, last, group, 0)


def kernel_sums(padded_ref, grad_ref, sums_ref):
    sums_ref[...] = jnp.zeros_like(sums_ref)

    def group(index, carry):
        grads = [
            grad_ref[pl.ds(pl.multiple_of(index * 128 + row * SIZE, SIZE), SIZE), :] for row in range(4)
        ]
        for col_tap in range(TAPS):
            totals = [jnp.zeros((8, WIDTH), F32) for _ in range(TAPS)]
            for row in range(4 + TAPS - 1):
                values = padded_ref[index * 4 + row, 5 + col_tap : 5 + col_tap + SIZE, :]
                for out in range(max(0, row - TAPS + 1), min(4, row + 1)):
                    product = values * grads[out]
                    totals[row - out] = totals[row - out] + (
                        (product[0:8] + product[8:16]) + (product[16:24] + product[24:32])
                    )
            for row_tap in range(TAPS):
                at = 8 * (row_tap * TAPS + col_tap)
                sums_ref[at : at + 8, :] += totals[row_tap]
        return carry

    lax.fori_loop(0, SIZE // 4, group, 0)


def row_rim(grown_ref, kernel_ref, top):
    rows = []
    for depth in range(3):
        total = jnp.zeros((PAD_COLS, WIDTH), F32)
        for row_tap in range(TAPS):
            source = depth - row_tap if top else 35 + depth - row_tap
            if 0 <= source < SIZE:
                for col_tap in range(TAPS):
                    at = 11 - col_tap
                    total = total + grown_ref[source + 3, at : at + PAD_COLS, :] * tap(kernel_ref, row_tap, col_tap)
        rows.append(total)
    return jnp.concatenate(rows, axis=0)


def col_rim(grown_ref, kernel_ref, left, out_ref):
    def group(index, carry):
        totals = [jnp.zeros((8, WIDTH), F32) for _ in range(8)]
        for col_tap in range(3) if left else range(4, TAPS):
            at = 11 - col_tap if left else 51 - col_tap
            for row in range(8 + TAPS - 1):
                values = grown_ref[index * 8 + row, at : at + 8, :]
                for out in range(max(0, row - TAPS + 1), min(8, row + 1)):
                    totals[out] = totals[out] + values * tap(kernel_ref, TAPS - 1 - (row - out), col_tap)
        for out in range(8):
            out_ref[pl.ds(pl.multiple_of(index * 64 + out * 8, 8), 8), :] = totals[out]
        return carry

    lax.fori_loop(0, SIZE // 8, group, 0)


def send_rims(here, grown_ref, kernel, rim_ref, sent_ref):
    rows = (MESSAGE, 3 * PAD_COLS)
    place = onehot(row_rim_slots(iota(rows, 1), True) == iota(rows, 0))
    rims = []
    for facing in range(2):
        rim = row_rim(grown_ref, kernel, facing == 0).astype(BF)
        sent_ref[(1 - side_of(here, 2), side_of(here, 2))[facing]] = matmul(place, rim).astype(BF)
        rims.append(rim)
    cols = (MESSAGE, SIZE * 8)
    for left in (True, False):
        col_rim(grown_ref, kernel, left, rim_ref)
        place = onehot(col_rim_slots(iota(cols, 1), 5 if left else 0) == iota(cols, 0))
        message = matmul(place, rim_ref[...].astype(BF))
        flip = side_of(here - 1 if left else here + 1, 2)
        for rim, base in ((rims[0], 112 - 16 * flip), (rims[1], 96 + 16 * flip)):
            slots = row_rim_slots(iota(rows, 1), False, base if left else None, None if left else base)
            message = message + matmul(onehot(slots == iota(rows, 0)), rim)
        side = side_of(here, 0)
        sent_ref[3 - side if left else 2 + side] = message.astype(BF)


def normalised(conv):
    centred = conv - jnp.mean(conv, axis=1, keepdims=True)
    inv_std = lax.rsqrt(jnp.mean(centred * centred, axis=1, keepdims=True) + EPSILON)
    return centred * inv_std, inv_std


def forward_chunk(conv, field, rows, up_w, up_b, down_w):
    gain, offset, down_b, scale = rows
    standard, _ = normalised(conv)
    normed = (standard * gain + offset).astype(BF)
    pre = matmul(normed, up_w) + up_b
    tangent = jnp.tanh(pre * (GELU_C + (GELU_C * GELU_A) * pre * pre))
    activated = (0.5 * pre * (1.0 + tangent)).astype(BF)
    branch = matmul(activated, down_w) + down_b
    return (field.astype(F32) + scale * branch).astype(BF)


def block_rows(params_ref, block):
    rows = [params_ref[row, block : block + 1, :] for row in range(TAPS * TAPS, PARAM_ROWS)]
    return (*rows[:5], jnp.concatenate(rows[5:], axis=1))


EDGE = 4 * SIZE
INSIDE = CELLS - 2 * EDGE


def first_inside_kernel(
    here_ref, field_ref, a_ref, b_ref, params_ref, up_ref, down_ref,
    out_ref, conv_ref, padded_ref, full_ref,
):
    fill_inside(padded_ref, here_ref[0], field_ref[...], a_ref[...], b_ref[...])
    bias, gain, offset, down_b, scale, up_b = block_rows(params_ref, 0)
    convolve(padded_ref, 5, (params_ref, 0), False, bias, full_ref, 1, 7)

    def chunk(index, carry):
        at = pl.ds(pl.multiple_of(index * CHUNK, CHUNK), CHUNK)
        cells = pl.ds(pl.multiple_of(EDGE + index * CHUNK, EDGE), CHUNK)
        conv = full_ref[cells, :]
        conv_ref[at, :] = conv
        out_ref[at, :] = forward_chunk(
            conv, field_ref[cells, :], (gain, offset, down_b, scale), up_ref[0], up_b, down_ref[0]
        )
        return carry

    lax.fori_loop(0, INSIDE // CHUNK, chunk, 0)


def ends(ref):
    return jnp.concatenate([ref[:EDGE, :], ref[CELLS - EDGE :, :]], axis=0)


def join_rows(ref, inside, edges):
    ref[:EDGE, :] = edges[:EDGE]
    ref[EDGE : CELLS - EDGE, :] = inside
    ref[CELLS - EDGE :, :] = edges[EDGE:]


def first_kernel(
    here_ref, field_ref, c_ref, d_ref, a_ref, b_ref, out_in_ref, gather_ref, params_ref, up_ref, down_ref,
    out_ref, conv_ref, padded_ref, sent_ref, full_ref,
):
    here = here_ref[0]
    fill_inside(padded_ref, here, field_ref[...], a_ref[...], b_ref[...])
    fill_rims(padded_ref, here, c_ref[...], d_ref[...])
    bias, gain, offset, down_b, scale, up_b = block_rows(params_ref, 0)
    for index in (0, 7):
        convolve(padded_ref, 5, (params_ref, 0), False, bias, full_ref, index, index + 1)
    conv = ends(full_ref)
    conv_ref[...] = conv
    out = forward_chunk(conv, ends(field_ref), (gain, offset, down_b, scale), up_ref[0], up_b, down_ref[0])
    join_rows(out_ref, out_in_ref[...], out)
    send_cells(here, gather_ref[...], out_ref[...], sent_ref)


def again(block, conv, refs):
    params_ref, up_ref, down_ref = refs
    _, gain, offset, down_b, _, up_b = block_rows(params_ref, block)
    standard, inv_std = normalised(conv)
    normed = (standard * gain + offset).astype(BF)
    pre = matmul(normed, up_ref[block]) + up_b
    square = pre * pre
    tangent = jnp.tanh(pre * (GELU_C + (GELU_C * GELU_A) * square))
    half = 0.5 + 0.5 * tangent
    activated = (pre * half).astype(BF)
    slope = half + pre * (0.5 - 0.5 * tangent * tangent) * (GELU_C + (3.0 * GELU_C * GELU_A) * square)
    branch = matmul(activated, down_ref[block]) + down_b
    return standard, inv_std, normed, activated, slope, branch


def backward_chunk(block, saved, upstream, refs):
    params_ref, up_ref, down_ref, up_sum, down_sum, vector_sum, up_b_sum = refs
    standard, inv_std, normed, activated, slope, branch = saved
    _, gain, _, _, scale, _ = block_rows(params_ref, block)
    scaled = upstream * scale
    scaled_b = scaled.astype(BF)
    down_sum[...] += matmul(scaled_b, activated, ((0,), (0,)))
    pre_grad = matmul(scaled_b, down_ref[block], ((1,), (1,))) * slope
    up_b_sum[...] += jnp.sum(pre_grad, axis=0, keepdims=True)
    pre_grad_b = pre_grad.astype(BF)
    up_sum[...] += matmul(normed, pre_grad_b, ((0,), (0,)))
    normed_grad = matmul(pre_grad_b, up_ref[block], ((1,), (1,)))
    std_grad = normed_grad * gain
    conv_grad = inv_std * (
        std_grad
        - jnp.mean(std_grad, axis=1, keepdims=True)
        - standard * jnp.mean(std_grad * standard, axis=1, keepdims=True)
    )
    for row, values in enumerate((conv_grad, normed_grad * standard, normed_grad, scaled, upstream * branch)):
        vector_sum[row : row + 1, :] += jnp.sum(values, axis=0, keepdims=True)
    return conv_grad


def through(block, conv, upstream, field, refs):
    saved = again(block, conv, refs[:3])
    scale = block_rows(refs[0], block)[4]
    out = (field.astype(F32) + scale * saved[5]).astype(BF)
    return backward_chunk(block, saved, upstream, refs), out


def clear(refs):
    for ref in refs:
        ref[...] = jnp.zeros_like(ref)


def fill_grown(grown_ref, grad):
    grown_ref[0:3] = jnp.zeros((3, GROWN_COLS, WIDTH), F32)
    grown_ref[35:38] = jnp.zeros((3, GROWN_COLS, WIDTH), F32)
    grown_ref[3:35, 0:16] = jnp.zeros((SIZE, 16, WIDTH), F32)
    grown_ref[3:35, 48:64] = jnp.zeros((SIZE, 16, WIDTH), F32)
    grown_ref[3:35, 16:48] = grad.reshape(SIZE, SIZE, WIDTH)


def pack_sums(refs, weights_ref, vectors_ref):
    up_sum, down_sum, vector_sum, up_b_sum = refs[3:]
    for part in range(HID // WIDTH):
        lanes = slice(part * WIDTH, (part + 1) * WIDTH)
        weights_ref[part * WIDTH : (part + 1) * WIDTH, :] = up_sum[:, lanes].astype(BF)
        weights_ref[HID + part * WIDTH : HID + (part + 1) * WIDTH, :] = down_sum[:, lanes].astype(BF)
        vector_sum[8 + part : 9 + part, :] = up_b_sum[:, lanes]
    vectors_ref[...] = vector_sum[...].astype(BF)


def second_inside_kernel(
    here_ref, field_ref, a_ref, b_ref, cotangent_ref, params_ref, up_ref, down_ref,
    out_ref, grad_ref, up_sum, down_sum, vector_sum, up_b_sum, padded_ref, conv_ref,
):
    fill_inside(padded_ref, here_ref[0], field_ref[...], a_ref[...], b_ref[...])
    convolve(padded_ref, 5, (params_ref, 1), False, block_rows(params_ref, 1)[0], conv_ref, 1, 7)
    refs = (params_ref, up_ref, down_ref, up_sum, down_sum, vector_sum, up_b_sum)
    clear(refs[3:])

    def chunk(index, carry):
        at = pl.ds(pl.multiple_of(index * CHUNK, CHUNK), CHUNK)
        cells = pl.ds(pl.multiple_of(EDGE + index * CHUNK, EDGE), CHUNK)
        grad_ref[at, :], out_ref[at, :] = through(
            1, conv_ref[cells, :], cotangent_ref[cells, :].astype(F32), field_ref[cells, :], refs
        )
        return carry

    lax.fori_loop(0, INSIDE // CHUNK, chunk, 0)


def second_kernel(
    here_ref, field_ref, c_ref, d_ref, a_ref, b_ref, grad_in_ref, up_in, down_in, vector_in, up_b_in,
    cotangent_ref, params_ref, up_ref, down_ref,
    out_ref, padded_ref, grad_ref, sent_ref, weights_ref, sums_ref,
    conv_ref, grown_ref, up_sum, down_sum, vector_sum, up_b_sum, rim_ref,
):
    here = here_ref[0]
    fill_inside(padded_ref, here, field_ref[...], a_ref[...], b_ref[...])
    fill_rims(padded_ref, here, c_ref[...], d_ref[...])
    for index in (0, 7):
        convolve(padded_ref, 5, (params_ref, 1), False, block_rows(params_ref, 1)[0], conv_ref, index, index + 1)
    refs = (params_ref, up_ref, down_ref, up_sum, down_sum, vector_sum, up_b_sum)
    for ref, start in zip(refs[3:], (up_in, down_in, vector_in, up_b_in)):
        ref[...] = start[...]
    grad, out_ref[...] = through(1, ends(conv_ref), ends(cotangent_ref).astype(F32), ends(field_ref), refs)
    join_rows(grad_ref, grad_in_ref[...], grad)
    fill_grown(grown_ref, grad_ref[...])
    send_rims(here, grown_ref, (params_ref, 1), rim_ref, sent_ref)
    pack_sums(refs, weights_ref, sums_ref)


def third_again_kernel(
    conv_ref, conv_edge_ref, params_ref, up_ref, down_ref,
    standard_ref, inv_std_ref, normed_ref, activated_ref, slope_ref, branch_ref, full_ref,
):
    join_rows(full_ref, conv_ref[...], conv_edge_ref[...])

    def chunk(index, carry):
        at = pl.ds(pl.multiple_of(index * CHUNK, CHUNK), CHUNK)
        saved = again(0, full_ref[at, :], (params_ref, up_ref, down_ref))
        standard_ref[at, :], _, normed_ref[at, :], activated_ref[at, :], slope_ref[at, :], branch_ref[at, :] = saved
        inv_std_ref[at, :] = jnp.broadcast_to(saved[1], (CHUNK, WIDTH))
        return carry

    lax.fori_loop(0, CELLS // CHUNK, chunk, 0)


def third_kernel(
    here_ref, standard_ref, inv_std_ref, normed_ref, activated_ref, slope_ref, branch_ref, cotangent_ref, inner_ref,
    c_ref, d_ref, a_ref, b_ref, scatter_ref, params_ref, up_ref, down_ref,
    upstream_ref, grad_ref, sent_ref, weights_ref, sums_ref,
    grown_ref, up_sum, down_sum, vector_sum, up_b_sum, rim_ref,
):
    returned = jnp.concatenate([c_ref[...], d_ref[...], a_ref[...], b_ref[...]], axis=0)
    upstream_ref[...] = cotangent_ref[...].astype(F32) + inner_ref[...] + matmul(scatter_ref[...], returned)
    refs = (params_ref, up_ref, down_ref, up_sum, down_sum, vector_sum, up_b_sum)
    clear(refs[3:])
    saved_refs = (standard_ref, inv_std_ref, normed_ref, activated_ref, slope_ref, branch_ref)

    def chunk(index, carry):
        at = pl.ds(pl.multiple_of(index * CHUNK, CHUNK), CHUNK)
        grad_ref[at, :] = backward_chunk(0, [ref[at, :] for ref in saved_refs], upstream_ref[at, :], refs)
        return carry

    lax.fori_loop(0, CELLS // CHUNK, chunk, 0)
    fill_grown(grown_ref, grad_ref[...])
    send_rims(here_ref[0], grown_ref, (params_ref, 0), rim_ref, sent_ref)
    pack_sums(refs, weights_ref, sums_ref)


def last_kernel(upstream_ref, inner_ref, c_ref, d_ref, a_ref, b_ref, scatter_ref, out_ref):
    returned = jnp.concatenate([c_ref[...], d_ref[...], a_ref[...], b_ref[...]], axis=0)
    out_ref[...] = (upstream_ref[...] + inner_ref[...] + matmul(scatter_ref[...], returned)).astype(BF)


def make_inner_kernel(block):
    def inner_kernel(grad_ref, params_ref, inner_ref, grown_ref):
        fill_grown(grown_ref, grad_ref[...])
        convolve(grown_ref, 13, (params_ref, block), True, jnp.zeros((1, WIDTH), F32), inner_ref)

    return inner_kernel


def taps_and_out_kernel(padded_ref, grad_ref, inside_ref, edges_ref, taps_ref, out_ref, sums_ref):
    join_rows(out_ref, inside_ref[...], edges_ref[...])
    taps_kernel(padded_ref, grad_ref, taps_ref, sums_ref)


def taps_kernel(padded_ref, grad_ref, taps_ref, sums_ref):
    kernel_sums(padded_ref, grad_ref, sums_ref)
    taps_ref[...] = jnp.sum(sums_ref[...].reshape(64, 8, WIDTH), axis=1).astype(BF)


def halves_kernel(
    core_ref, padded_ref, grad_ref, weights_0_ref, sums_0_ref, weights_1_ref, sums_1_ref, taps_1_ref,
    kept_ref, given_ref, taps_ref, partial_ref,
):
    taps_kernel(padded_ref, grad_ref, taps_ref, partial_ref)

    def fill(half_ref, *parts):
        at = 0
        for part in parts:
            half_ref[at : at + part.shape[0], :] = part[...]
            at += part.shape[0]
        half_ref[at:, :] = jnp.zeros((HALF_ROWS - at, WIDTH), BF)

    first = (weights_0_ref, sums_0_ref, taps_ref)
    second = (weights_1_ref, sums_1_ref, taps_1_ref)
    for core, kept, given in ((0, first, second), (1, second, first)):

        @pl.when(core_ref[0] == core)
        def _(kept=kept, given=given):
            fill(kept_ref, *kept)
            fill(given_ref, *given)


def swapped_tiles(value, step, odd):
    starts = [tile for tile in range(TILES) if (tile // step) % 2 == odd]
    pairs = [(tile, (tile + step) % TILES) for tile in starts]
    return lax.ppermute(value, TILE_AXES, pairs + [(target, source) for source, target in pairs])


def beside(sent):
    return swapped_tiles(sent[2], 1, 0), swapped_tiles(sent[3], 1, 1)


def beyond(sent, by_a, by_b):
    by_c = swapped_tiles(jnp.concatenate([sent[0, :96], by_a[96:112], by_b[96:112]]), 4, 0)
    by_d = swapped_tiles(jnp.concatenate([sent[1, :96], by_a[112:], by_b[112:]]), 4, 1)
    return by_c, by_d


def after(values, *others):
    return lax.optimization_barrier((values, others))[0]


HALF_ROWS = 1152


def swapped(value, axis):
    return lax.ppermute(value, axis, [(0, 1), (1, 0)])


def joined(value, axis):
    other = swapped(value, axis)
    return jnp.where(
        lax.axis_index(axis) == 0, jnp.concatenate([value, other]), jnp.concatenate([other, value])
    )


def summed_apart(value, axes):
    count = lax.axis_size(axes)
    parts = lax.all_to_all(value, axes, 0, 0, tiled=True).reshape(count, -1, WIDTH)
    return jnp.sum(parts.astype(F32), axis=0).astype(BF)


def gathered(value, axes):
    count = lax.axis_size(axes)
    copies = jnp.broadcast_to(value[None], (count,) + value.shape).reshape(-1, WIDTH)
    return lax.all_to_all(copies, axes, 0, 0, tiled=True)


ACROSS = ("far", "y", "member")


def summed_along(value, axis):
    count = lax.axis_size(axis)
    return jnp.sum(gathered(value, axis).reshape(count, -1, WIDTH).astype(F32), axis=0).astype(BF)


def make_unpack_kernel(factor):
    def unpack_kernel(sum_ref, taps, conv_b, gain, offset, up, up_b, down, down_b, scale):
        for block in range(BLOCKS):
            base = block * HALF_ROWS
            for part in range(HID // WIDTH):
                rows = slice(base + part * WIDTH, base + (part + 1) * WIDTH)
                up[block, :, part * WIDTH : (part + 1) * WIDTH] = sum_ref[rows, :].astype(F32) * factor
                rows = slice(base + HID + part * WIDTH, base + HID + (part + 1) * WIDTH)
                down[block, part * WIDTH : (part + 1) * WIDTH, :] = (sum_ref[rows, :].astype(F32) * factor).T
            base += 2 * HID
            vectors = sum_ref[base : base + 16, :].astype(F32) * factor
            for row, ref in enumerate((conv_b, gain, offset, down_b, scale)):
                ref[block : block + 1, :] = vectors[row : row + 1]
            for part in range(HID // WIDTH):
                up_b[block : block + 1, part * WIDTH : (part + 1) * WIDTH] = vectors[8 + part : 9 + part]
            base += 16
            kernel_sum = sum_ref[base : base + 64, :].astype(F32) * factor
            for row in range(TAPS * TAPS):
                taps[row, block : block + 1, :] = kernel_sum[row : row + 1]

    return unpack_kernel


def laid_down(items):
    rows = sum(item.shape[0] for item in items)
    total, at = None, 0
    for item in items:
        edges = [(at, rows - at - item.shape[0], 0)] + [(0, 0, 0)] * (item.ndim - 1)
        part = lax.pad(item, jnp.zeros((), item.dtype), edges)
        total = part if total is None else total + part
        at += item.shape[0]
    return total


def shaped(*shapes):
    return [jax.ShapeDtypeStruct(shape, dtype) for shape, dtype in shapes]


def call(kernel, shapes, inputs, scratch=(), scalars=0, cost=None):
    specs = [pl.BlockSpec(memory_space=pltpu.SMEM)] * scalars + whole(len(inputs) - scalars)
    return pl.pallas_call(
        kernel,
        out_shape=shaped(*shapes),
        in_specs=specs,
        out_specs=whole(len(shapes)),
        scratch_shapes=list(scratch),
        compiler_params=kernel_params(),
        cost_estimate=cost,
    )(*inputs)


def body(
    states, cotangent, seam_codes, corner_codes, dw_kernel, dw_bias, norm_gain, norm_bias, up_weight, up_bias,
    down_weight, down_bias, layer_scale,
):
    count = lax.axis_size(TILE_AXES) * lax.axis_size("member")
    here = lax.axis_index(TILE_AXES).astype(jnp.int32).reshape(1)
    codes = jnp.concatenate([seam_codes.T, corner_codes.T])
    field = states.reshape(CELLS, WIDTH)
    upstream = cotangent.reshape(CELLS, WIDTH)
    message = ((4, MESSAGE, WIDTH), BF)
    padded_shape = ((PAD_ROWS, PAD_COLS, WIDTH), F32)
    weights_shape = ((2 * HID, WIDTH), BF)
    sums_shape = ((16, WIDTH), BF)
    cells = (CELLS, WIDTH)
    inside, edges = (INSIDE, WIDTH), (2 * EDGE, WIDTH)
    wide_sums = [((WIDTH, HID), F32), ((WIDTH, HID), F32), ((16, WIDTH), F32), ((1, HID), F32)]
    padded_scratch = pltpu.VMEM((PAD_ROWS, PAD_COLS, WIDTH), F32)
    grown_scratch = pltpu.VMEM((PAD_ROWS, GROWN_COLS, WIDTH), F32)
    cells_scratch = pltpu.VMEM(cells, F32)
    sums = [grown_scratch, *(pltpu.VMEM(*item) for item in wide_sums), pltpu.VMEM((SIZE * 8, WIDTH), F32)]
    tap_scratch = [pltpu.VMEM((64 * 8, WIDTH), F32)]
    vpu = pl.CostEstimate(flops=2 * 49 * CELLS * WIDTH, bytes_accessed=3 << 20, transcendentals=0)

    sent, gather, owners = call(
        select_kernel,
        [message, ((4 * MESSAGE, CELLS), BF), ((4, 8, MESSAGE), jnp.int32)],
        [here, codes, field],
        scalars=2,
    )
    near = beside(sent)
    packed = laid_down(
        [dw_kernel.transpose(1, 2, 0, 3).reshape(TAPS * TAPS, BLOCKS, WIDTH)]
        + [item[None] for item in (dw_bias, norm_gain, norm_bias, down_bias, layer_scale)]
        + [up_bias.reshape(BLOCKS, HID // WIDTH, WIDTH).transpose(1, 0, 2)]
    )
    near, packed = lax.optimization_barrier((near, packed))
    params = (packed, up_weight, down_weight)
    far = beyond(sent, *near)
    part, conv_part = call(
        first_inside_kernel,
        [(inside, BF), (inside, F32)],
        [here, field, *near, *params],
        [padded_scratch, cells_scratch],
        scalars=1,
        cost=vpu,
    )
    middle, conv_edges, padded_0, sent = call(
        first_kernel,
        [(cells, BF), (edges, F32), padded_shape, message],
        [here, field, *far, *near, part, gather, *params],
        [cells_scratch],
        scalars=1,
    )
    near = beside(sent)
    (scatter,) = call(scatter_kernel, [((CELLS, 4 * MESSAGE), BF)], [owners], cost=vpu)
    near, scatter = lax.optimization_barrier((near, scatter))
    far = beyond(sent, *near)
    out_part, *partial = call(
        second_inside_kernel,
        [(inside, BF), (inside, F32), *wide_sums],
        [here, middle, *near, upstream, *params],
        [padded_scratch, cells_scratch],
        scalars=1,
        cost=vpu,
    )
    out_edges, padded_1, grad_1, sent, weights_1, sums_1 = call(
        second_kernel,
        [(edges, BF), padded_shape, (cells, F32), message, weights_shape, sums_shape],
        [here, middle, *far, *near, *partial, upstream, *params],
        [cells_scratch, *sums],
        scalars=1,
    )
    near = beside(sent)
    taps_1, out = call(
        taps_and_out_kernel,
        [((64, WIDTH), BF), (cells, BF)],
        [padded_1, grad_1, out_part, out_edges],
        tap_scratch,
        cost=vpu,
    )
    near, taps_1 = lax.optimization_barrier((near, taps_1))
    far = beyond(sent, *near)
    (inner_1,) = call(make_inner_kernel(1), [(cells, F32)], [grad_1, packed], [grown_scratch], cost=vpu)
    saved = call(
        third_again_kernel,
        [(cells, F32), (cells, F32), (cells, BF), ((CELLS, HID), BF), ((CELLS, HID), F32), (cells, F32)],
        [conv_part, conv_edges, *params],
        [cells_scratch],
        cost=vpu,
    )
    far, inner_1, saved = lax.optimization_barrier((far, inner_1, saved))
    upstream_0, grad_0, sent, weights_0, sums_0 = call(
        third_kernel,
        [(cells, F32), (cells, F32), message, weights_shape, sums_shape],
        [here, *saved, upstream, inner_1, *far, *near, scatter, *params],
        sums,
        scalars=1,
    )
    near = beside(sent)
    core = lax.axis_index("core").astype(jnp.int32).reshape(1)
    kept, given = call(
        halves_kernel,
        [((HALF_ROWS, WIDTH), BF), ((HALF_ROWS, WIDTH), BF)],
        [core, padded_0, grad_0, weights_0, sums_0, weights_1, sums_1, taps_1],
        [pltpu.VMEM((64, WIDTH), BF), *tap_scratch],
        scalars=1,
    )
    total = (kept.astype(F32) + swapped(given, "core").astype(F32)).astype(BF)
    total = summed_apart(total, ACROSS)
    total, near = lax.optimization_barrier((total, near))
    far = beyond(sent, *near)
    (inner_0,) = call(make_inner_kernel(0), [(cells, F32)], [grad_0, packed], [grown_scratch], cost=vpu)
    total = gathered(summed_along(total, "z"), ACROSS)
    total, far, inner_0 = lax.optimization_barrier((total, far, inner_0))
    (grad_field,) = call(last_kernel, [(cells, BF)], [upstream_0, inner_0, *far, *near, scatter])
    total = joined(total, "core")
    row, wide = ((BLOCKS, WIDTH), F32), ((BLOCKS, HID), F32)
    grads = call(
        make_unpack_kernel(1.0 / math.sqrt(count * CELLS)),
        [
            ((TAPS * TAPS, BLOCKS, WIDTH), F32), row, row, row, ((BLOCKS, WIDTH, HID), F32), wide,
            ((BLOCKS, HID, WIDTH), F32), row, row,
        ],
        [total],
    )
    kernel_grad = grads[0].reshape(TAPS, TAPS, BLOCKS, WIDTH).transpose(2, 0, 1, 3)
    shape = states.shape
    return (out.reshape(shape), grad_field.reshape(shape), kernel_grad, *grads[1:])


def solution(mesh):
    split = Mesh(mesh.devices.reshape(2, 4, 8, 2, 2), (*TILE_AXES, "member"))
    field = P("member", TILE_AXES, None, None, None)
    return jax.shard_map(
        body,
        mesh=split,
        in_specs=(field, field) + (P(),) * 11,
        out_specs=(field, field) + (P(),) * 9,
        check_vma=False,
    )
```

time: 180 us -> 128 us (0.71)
  blocking collectives: 26.5 us -> 0 us
  starting transfers between devices: 66.6 us -> 52.1 us
  local copies, waits for them, and re-layouts: 14.6 us -> 2.46 us
  waiting for transfers between devices: 26.7 us -> 34.6 us
  Pallas kernels: 39.9 us -> 33.7 us
    all_to_all x1 -> x0, blocking collectives: 26.5 us -> none  [summed_apart(): lax.all_to_all(value, axes, 0, 0, tiled=True).reshape(count, -1, WIDTH)]
    ppermute x16, starting transfers between devices: 59.5 us -> 38.8 us  [swapped_tiles(): lax.ppermute(value, TILE_AXES, pairs + [(target, source) for source, targ...]
    unnamed x69 -> x10, local copies, waits for them, and re-layouts: 10.2 us -> 0.97 us
    all_to_all x1 -> x2, waiting for transfers between devices: 0.53 us -> 9.14 us  [gathered(): return lax.all_to_all(copies, axes, 0, 0, tiled=True)]
    pallas_call x11 -> x14, Pallas kernels: 39.9 us -> 33.7 us  [call(): pl.pallas_call(kernel, out_shape=shaped(*shapes), in_specs=specs, out_spe...]
    all_to_all x0 -> x1, starting transfers between devices: none -> 4.76 us  [summed_apart(): lax.all_to_all(value, axes, 0, 0, tiled=True).reshape(count, -1, WIDTH)]
    all_to_all x1 -> x2, starting transfers between devices: 5.45 us -> 8.29 us  [gathered(): return lax.all_to_all(copies, axes, 0, 0, tiled=True)]
    all_to_all x2 -> x0, local copies, waits for them, and re-layouts: 2.64 us -> none  [the longest x1 1.8 us: gathered(): return lax.all_to_all(copies, axes, 0, 0, tiled=True)]
  transfers between devices with their start and end apart: 20 -> 21, of which waited for: 12 -> 12; matrix products, arithmetic and copies ran while one was open for 1% -> 1% of each run, Pallas kernels for 7% -> 16%
where the time goes in v2:
time: 128 us; the launch traced here: 127 us
  starting transfers between devices  52.1 us (41%)
  waiting for transfers between devices  34.6 us (27%)
  Pallas kernels  33.7 us (26%)
  other arithmetic  2.74 us (2%)
  local copies, waits for them, and re-layouts  2.46 us (2%)
    ppermute x16, starting transfers between devices, swapped_tiles(): lax.ppermute(value, TILE_AXES, pairs + [(target, source) for source, targ...  38.8 us
    pallas_call x14, Pallas kernels, call(): pl.pallas_call(kernel, out_shape=shaped(*shapes), in_specs=specs, out_spe...  33.7 us
    ppermute x16, waiting for transfers between devices, swapped_tiles(): lax.ppermute(value, TILE_AXES, pairs + [(target, source) for source, targ...  21.7 us
    all_to_all x2, waiting for transfers between devices, gathered(): return lax.all_to_all(copies, axes, 0, 0, tiled=True)  9.14 us
    all_to_all x2, starting transfers between devices, gathered(): return lax.all_to_all(copies, axes, 0, 0, tiled=True)  8.29 us
    all_to_all x1, starting transfers between devices, summed_apart(): lax.all_to_all(value, axes, 0, 0, tiled=True).reshape(count, -1, WIDTH)  4.76 us
  transfers between devices with their start and end apart: 21, of which 12 were waited for; matrix products, arithmetic and copies ran while one was open for 1% of the time, Pallas kernels for 16%

profile of v2, /device:TPU:2, one launch (start us, length us, event | category | flops | bytes accessed | tf_op | source)
XLA Modules:
  0.0 126.6 jit_solution(5655248649741960672)
XLA Ops:
  0.7 0.8 pad_add_fusion.1.codes_ref
  1.4 0.9 copy-done.3
  2.4 1.2 shard_map.212
  3.7 10.0 %collective-permute-start.1 = (bf16[128,128]{1,0:T(8,128)(2,1)S(1)}, bf16[128,128]{1,0:T(8,128)(2,1)S(1)}, u32[]{:S(2)}, u32[]{:S(2)}) collective-permute-start(bf16[128,128]{1,0:T(8,128)(2,1)S(1)} %get-tuple-element.165), channel_id=1, source_target_pairs={{2,4},{6,8},{10,12},{14,16},{18,20},{22,24},{26,28},{30,32},{34,36... | collective-permute-start | bytes 98312 | tf_op jit(solution)/shard_map/ppermute | solution.py:552
  13.7 0.9 pad_add_fusion.params_ref
  14.6 0.7 collective-permute-done.1.b_ref
  15.3 4.8 %collective-permute-start.3 = (bf16[128,128]{1,0:T(8,128)(2,1)S(1)}, bf16[128,128]{1,0:T(8,128)(2,1)S(1)}, u32[]{:S(2)}, u32[]{:S(2)}) collective-permute-start(bf16[128,128]{1,0:T(8,128)(2,1)S(1)} %pad_maximum_fusion.1), channel_id=1, source_target_pairs={{8,16},{10,18},{12,20},{14,22},{24,32},{26,34},{28,36},{30,38},{40... | collective-permute-start | bytes 98312 | tf_op jit(solution)/shard_map/ppermute | solution.py:552
  20.1 0.3 shard_map.215.scatter_ref
  20.4 3.7 %shard_map.213 = (bf16[768,128]{1,0:T(8,128)(2,1)S(1)}, f32[768,128]{1,0:T(8,128)S(1)}) custom-call(s32[1]{0:T(128)} %bitcast.here_ref, bf16[1024,128]{1,0:T(8,128)(2,1)S(1)} %bitcast.60, bf16[128,128]{1,0:T(8,128)(2,1)S(1)} %collective-permute-done.a_ref, bf16[128,128]{1,0:T(8,128)(2,1)S(1)} %collective-permute-done.1.b_ref, ...), custom_call_target="tpu_custom_call" | custom-call | flops 12845056 | bytes 3145728 | tf_op jit(solution)/shard_map/pallas_call | solution.py:643
  24.1 1.8 %collective-permute-done.3.d_ref = bf16[128,128]{1,0:T(8,128)(2,1)S(1)} collective-permute-done((bf16[128,128]{1,0:T(8,128)(2,1)S(1)}, bf16[128,128]{1,0:T(8,128)(2,1)S(1)}, u32[]{:S(2)}, u32[]{:S(2)}) %collective-permute-start.3) | collective-permute-done | bytes 32800 | tf_op jit(solution)/shard_map/ppermute | solution.py:552
  25.9 1.7 %shard_map.214 = (bf16[1024,128]{1,0:T(8,128)(2,1)S(1)}, f32[256,128]{1,0:T(8,128)S(1)}, f32[38,48,128]{2,1,0:T(8,128)S(1)}, bf16[4,128,128]{2,1,0:T(8,128)(2,1)S(1)}) custom-call(s32[1]{0:T(128)} %bitcast.here_ref, bf16[1024,128]{1,0:T(8,128)(2,1)S(1)} %bitcast.61, bf16[128,128]{1,0:T(8,128)(2,1)S(1)} %collective-permute-done.2.c_ref, ...), custom_call_target="tpu_custom_call" | custom-call | tf_op jit(solution)/shard_map/pallas_call | solution.py:643
  27.7 6.4 %collective-permute-start.5 = (bf16[128,128]{1,0:T(8,128)(2,1)S(1)}, bf16[128,128]{1,0:T(8,128)(2,1)S(1)}, u32[]{:S(2)}, u32[]{:S(2)}) collective-permute-start(bf16[128,128]{1,0:T(8,128)(2,1)S(1)} %get-tuple-element.161), channel_id=1, source_target_pairs={{2,4},{6,8},{10,12},{14,16},{18,20},{22,24},{26,28},{30,32},{34,36... | collective-permute-start | bytes 98312 | tf_op jit(solution)/shard_map/ppermute | solution.py:552
  34.1 2.7 %collective-permute-done.5.b_ref = bf16[128,128]{1,0:T(8,128)(2,1)S(1)} collective-permute-done((bf16[128,128]{1,0:T(8,128)(2,1)S(1)}, bf16[128,128]{1,0:T(8,128)(2,1)S(1)}, u32[]{:S(2)}, u32[]{:S(2)}) %collective-permute-start.5) | collective-permute-done | bytes 32800 | tf_op jit(solution)/shard_map/ppermute | solution.py:552
  36.8 0.1 collective-permute-start.6
  37.0 0.1 collective-permute-start.7
  37.1 5.0 %shard_map.216 = (bf16[768,128]{1,0:T(8,128)(2,1)S(1)}, f32[768,128]{1,0:T(8,128)S(1)}, f32[128,512]{1,0:T(8,128)S(1)}, f32[128,512]{1,0:T(8,128)S(1)}, f32[16,128]{1,0:T(8,128)S(1)}, /*index=5*/f32[1,512]{1,0:T(1,128)S(1)}) custom-call(s32[1]{0:T(128)} %bitcast.here_ref, bf16[1024,128]{1,0:T(8,128)(2,1)S(1)} %get-tuple-element.87.field_ref, ...), custom_call_target="tpu_custom_call" | custom-call | flops 12845056 | bytes 3145728 | tf_op jit(solution)/shard_map/pallas_call | solution.py:643
  42.1 5.5 %collective-permute-done.7.d_ref = bf16[128,128]{1,0:T(8,128)(2,1)S(1)} collective-permute-done((bf16[128,128]{1,0:T(8,128)(2,1)S(1)}, bf16[128,128]{1,0:T(8,128)(2,1)S(1)}, u32[]{:S(2)}, u32[]{:S(2)}) %collective-permute-start.7) | collective-permute-done | bytes 32800 | tf_op jit(solution)/shard_map/ppermute | solution.py:552
  47.6 3.1 %shard_map.217 = (bf16[256,128]{1,0:T(8,128)(2,1)S(1)}, f32[38,48,128]{2,1,0:T(8,128)S(1)}, f32[1024,128]{1,0:T(8,128)S(1)}, bf16[4,128,128]{2,1,0:T(8,128)(2,1)...) custom-call(s32[1]{0:T(128)} %bitcast.here_ref, bf16[1024,128]{1,0:T(8,128)(2,1)S(1)} %get-tuple-element.87.field_ref, ...), custom_call_target="tpu_custom_call" | custom-call | tf_op jit(solution)/shard_map/pallas_call | solution.py:643
  50.8 5.4 %collective-permute-start.9 = (bf16[128,128]{1,0:T(8,128)(2,1)S(1)}, bf16[128,128]{1,0:T(8,128)(2,1)S(1)}, u32[]{:S(2)}, u32[]{:S(2)}) collective-permute-start(bf16[128,128]{1,0:T(8,128)(2,1)S(1)} %get-tuple-element.157), channel_id=1, source_target_pairs={{2,4},{6,8},{10,12},{14,16},{18,20},{22,24},{26,28},{30,32},{34,36... | collective-permute-start | bytes 98312 | tf_op jit(solution)/shard_map/ppermute | solution.py:552
  56.2 2.3 %shard_map.218 = (bf16[64,128]{1,0:T(8,128)(2,1)S(1)}, bf16[1024,128]{1,0:T(8,128)(2,1)}) custom-call(f32[38,48,128]{2,1,0:T(8,128)S(1)} %get-tuple-element.97.padded_ref, f32[1024,128]{1,0:T(8,128)S(1)} %get-tuple-element.98.grad_ref, bf16[768,128]{1,0:T(8,128)(2,1)S(1)} %get-tuple-element.99.inside_ref, bf16[256,128]{1,0:T(8,128)(2,1)S(1)} %get-tuple-element.100.edges_ref), custom_call_target="tpu_custom_call" | custom-call | flops 12845056 | bytes 3145728 | tf_op jit(solution)/shard_map/pallas_call | solution.py:643
  58.5 1.6 %collective-permute-done.9.b_ref = bf16[128,128]{1,0:T(8,128)(2,1)S(1)} collective-permute-done((bf16[128,128]{1,0:T(8,128)(2,1)S(1)}, bf16[128,128]{1,0:T(8,128)(2,1)S(1)}, u32[]{:S(2)}, u32[]{:S(2)}) %collective-permute-start.9) | collective-permute-done | bytes 32800 | tf_op jit(solution)/shard_map/ppermute | solution.py:552
  60.1 0.1 collective-permute-start.10
  60.2 0.4 collective-permute-start.11
  60.6 3.0 %shard_map.220 = (f32[1024,128]{1,0:T(8,128)S(1)}, f32[1024,128]{1,0:T(8,128)S(1)}, bf16[1024,128]{1,0:T(8,128)(2,1)S(1)}, bf16[1024,512]{1,0:T(8,128)(2,1)S(1)}...) custom-call(f32[768,128]{1,0:T(8,128)S(1)} %get-tuple-element.106.conv_ref, ...), custom_call_target="tpu_custom_call" | custom-call | flops 12845056 | bytes 3145728 | tf_op jit(solution)/shard_map/pallas_call | solution.py:643
  63.6 2.5 %shard_map.219.inner_ref = f32[1024,128]{1,0:T(8,128)S(1)} custom-call(f32[1024,128]{1,0:T(8,128)S(1)} %get-tuple-element.98.grad_ref, f32[58,2,128]{2,1,0:T(2,128)S(1)} %pad_add_fusion.params_ref), custom_call_target="tpu_custom_call" | custom-call | flops 12845056 | bytes 3145728 | tf_op jit(solution)/shard_map/pallas_call | solution.py:643
  66.1 4.7 %collective-permute-done.11.d_ref = bf16[128,128]{1,0:T(8,128)(2,1)S(1)} collective-permute-done((bf16[128,128]{1,0:T(8,128)(2,1)S(1)}, bf16[128,128]{1,0:T(8,128)(2,1)S(1)}, u32[]{:S(2)}, u32[]{:S(2)}) %collective-permute-start.11) | collective-permute-done | bytes 32800 | tf_op jit(solution)/shard_map/ppermute | solution.py:552
  70.8 4.4 %shard_map.221 = (f32[1024,128]{1,0:T(8,128)S(1)}, f32[1024,128]{1,0:T(8,128)S(1)}, bf16[4,128,128]{2,1,0:T(8,128)(2,1)S(1)}, bf16[1024,128]{1,0:T(8,128)(2,1)S(1)}, bf16[16,128]{1,0:T(8,128)(2,1)S(1)}) custom-call(s32[1]{0:T(128)} %bitcast.here_ref, f32[1024,128]{1,0:T(8,128)S(1)} %get-tuple-element.114.standard_ref, ...), custom_call_target="tpu_custom_call" | custom-call | tf_op jit(solution)/shard_map/pallas_call | solution.py:643
  75.3 1.9 %shard_map.222 = (bf16[1152,128]{1,0:T(8,128)(2,1)S(1)}, bf16[1152,128]{1,0:T(8,128)(2,1)S(1)}) custom-call(s32[1]{0:T(128)} %bitcast.27.core_ref, f32[38,48,128]{2,1,0:T(8,128)S(1)} %get-tuple-element.125.padded_ref, f32[1024,128]{1,0:T(8,128)S(1)} %get-tuple-element.126.grad_ref, bf16[1024,128]{1,0:T(8,128)(2,1)S(1)} %get-tuple-element.127.weights_0_ref, ...), custom_call_target="tpu_custom_call" | custom-call | tf_op jit(solution)/shard_map/pallas_call | solution.py:643
  77.3 1.6 %collective-permute-done.12 = bf16[1152,128]{1,0:T(8,128)(2,1)S(1)} collective-permute-done((bf16[1152,128]{1,0:T(8,128)(2,1)S(1)}, bf16[1152,128]{1,0:T(8,128)(2,1)S(1)}, u32[]{:S(2)}, u32[]{:S(2)}) %collective-permute-start.12) | collective-permute-done | bytes 294944 | tf_op jit(solution)/shard_map/ppermute | solution.py:573
  78.9 0.8 add_convert_fusion
  79.6 4.8 %all-to-all-start = ((bf16[16,72,128]{2,1,0:T(8,128)(2,1)}), bf16[16,72,128]{2,1,0:T(8,128)(2,1)S(1)}, u32[]{:S(2)}, u32[]{:S(2)}) async-start(bf16[16,72,128]{2,1,0:T(8,128)(2,1)} %bitcast.28), calls=%async_computation | async-start | bytes 589824 | tf_op jit(solution)/shard_map/all_to_all | solution.py:585
  84.5 6.3 %collective-permute-start.14 = (bf16[128,128]{1,0:T(8,128)(2,1)S(1)}, bf16[128,128]{1,0:T(8,128)(2,1)S(1)}, u32[]{:S(2)}, u32[]{:S(2)}) collective-permute-start(bf16[128,128]{1,0:T(8,128)(2,1)S(1)} %get-tuple-element.153), channel_id=1, source_target_pairs={{2,4},{6,8},{10,12},{14,16},{18,20},{22,24},{26,28},{30,32},{34,36... | collective-permute-start | bytes 98312 | tf_op jit(solution)/shard_map/ppermute | solution.py:552
  90.8 1.9 %all-to-all-done = bf16[16,72,128]{2,1,0:T(8,128)(2,1)S(1)} async-done(((bf16[16,72,128]{2,1,0:T(8,128)(2,1)}), bf16[16,72,128]{2,1,0:T(8,128)(2,1)S(1)}, u32[]{:S(2)}, u32[]{:S(2)}) %all-to-all-start) | async-done | bytes 294944 | tf_op jit(solution)/shard_map/all_to_all | solution.py:585
  92.8 0.9 collective-permute-done.14.b_ref
  93.7 0.7 broadcast_in_dim.32
  94.3 3.4 %all-to-all-start.1 = ((bf16[8,72,128]{2,1,0:T(8,128)(2,1)}), bf16[8,72,128]{2,1,0:T(8,128)(2,1)S(1)}, u32[]{:S(2)}, u32[]{:S(2)}) async-start(bf16[8,72,128]{2,1,0:T(8,128)(2,1)} %broadcast_in_dim.32), calls=%async_computation.1 | async-start | bytes 294912 | tf_op jit(solution)/shard_map/all_to_all | solution.py:592
  97.8 9.1 %all-to-all-done.1 = bf16[8,72,128]{2,1,0:T(8,128)(2,1)S(1)} async-done(((bf16[8,72,128]{2,1,0:T(8,128)(2,1)}), bf16[8,72,128]{2,1,0:T(8,128)(2,1)S(1)}, u32[]{:S(2)}, u32[]{:S(2)}) %all-to-all-start.1) | async-done | bytes 147488 | tf_op jit(solution)/shard_map/all_to_all | solution.py:592
  106.9 0.8 broadcast_in_dim.33
  107.7 4.9 %all-to-all-start.2 = ((bf16[16,72,128]{2,1,0:T(8,128)(2,1)}), bf16[16,72,128]{2,1,0:T(8,128)(2,1)S(1)}, u32[]{:S(2)}, u32[]{:S(2)}) async-start(bf16[16,72,128]{2,1,0:T(8,128)(2,1)} %broadcast_in_dim.33), calls=%async_computation.2 | async-start | bytes 589824 | tf_op jit(solution)/shard_map/all_to_all | solution.py:592
  112.6 0.1 collective-permute-start.15
  112.7 4.7 %collective-permute-start.16 = (bf16[128,128]{1,0:T(8,128)(2,1)S(1)}, bf16[128,128]{1,0:T(8,128)(2,1)S(1)}, u32[]{:S(2)}, u32[]{:S(2)}) collective-permute-start(bf16[128,128]{1,0:T(8,128)(2,1)S(1)} %pad_maximum_fusion.7), channel_id=1, source_target_pairs={{8,16},{10,18},{12,20},{14,22},{24,32},{26,34},{28,36},{30,38},{40... | collective-permute-start | bytes 98312 | tf_op jit(solution)/shard_map/ppermute | solution.py:552
  117.4 2.5 %shard_map.223.inner_ref = f32[1024,128]{1,0:T(8,128)S(1)} custom-call(f32[1024,128]{1,0:T(8,128)S(1)} %get-tuple-element.126.grad_ref, f32[58,2,128]{2,1,0:T(2,128)S(1)} %pad_add_fusion.params_ref), custom_call_target="tpu_custom_call" | custom-call | flops 12845056 | bytes 3145728 | tf_op jit(solution)/shard_map/pallas_call | solution.py:643
  119.9 3.7 %collective-permute-done.16.d_ref = bf16[128,128]{1,0:T(8,128)(2,1)S(1)} collective-permute-done((bf16[128,128]{1,0:T(8,128)(2,1)S(1)}, bf16[128,128]{1,0:T(8,128)(2,1)S(1)}, u32[]{:S(2)}, u32[]{:S(2)}) %collective-permute-start.16) | collective-permute-done | bytes 32800 | tf_op jit(solution)/shard_map/ppermute | solution.py:552
  123.7 0.1 collective-permute-start.17
  123.8 1.2 shard_map.224
  124.9 0.3 collective-permute-done.17
  125.2 0.2 maximum_select_fusion.sum_ref
  125.4 1.2 shard_map.225
  (49 shorter events, 0.7 us)
Async XLA Ops:
  0.6 19.7 %copy-start = (bf16[2,128,512]{2,1,0:T(8,128)(2,1)S(1)}, bf16[2,128,512]{2,1,0:T(8,128)(2,1)}, u32[]{:S(2)}) copy-start(bf16[2,128,512]{2,1,0:T(8,128)(2,1)} %up_ref.11) | copy-start | bytes 786436
  0.7 19.7 %copy-start.1 = (bf16[2,512,128]{2,1,0:T(8,128)(2,1)S(1)}, bf16[2,512,128]{2,1,0:T(8,128)(2,1)}, u32[]{:S(2)}) copy-start(bf16[2,512,128]{2,1,0:T(8,128)(2,1)} %down_ref.11) | copy-start | bytes 786436
  1.4 0.9 copy-start.3
  2.4 18.0 %copy-start.4 = (bf16[1,1,32,32,128]{4,3,2,1,0:T(8,128)(2,1)S(1)}, bf16[1,1,32,32,128]{4,3,2,1,0:T(8,128)(2,1)}, u32[]{:S(2)}) copy-start(bf16[1,1,32,32,128]{4,3,2,1,0:T(8,128)(2,1)} %param.13) | copy-start | bytes 786436
  3.6 11.0 %collective-permute-start = (bf16[128,128]{1,0:T(8,128)(2,1)S(1)}, bf16[128,128]{1,0:T(8,128)(2,1)S(1)}, u32[]{:S(2)}, u32[]{:S(2)}) collective-permute-start(bf16[128,128]{1,0:T(8,128)(2,1)S(1)} %get-tuple-element.166), channel_id=1, source_target_pairs={{0,2},{4,6},{8,10},{12,14},{16,18},{20,22},{24,26},{28,30},{32,34}... | collective-permute-start | bytes 98312 | tf_op jit(solution)/shard_map/ppermute | solution.py:552
  3.7 11.6 %collective-permute-start.1 = (bf16[128,128]{1,0:T(8,128)(2,1)S(1)}, bf16[128,128]{1,0:T(8,128)(2,1)S(1)}, u32[]{:S(2)}, u32[]{:S(2)}) collective-permute-start(bf16[128,128]{1,0:T(8,128)(2,1)S(1)} %get-tuple-element.165), channel_id=1, source_target_pairs={{2,4},{6,8},{10,12},{14,16},{18,20},{22,24},{26,28},{30,32},{34,36... | collective-permute-start | bytes 98312 | tf_op jit(solution)/shard_map/ppermute | solution.py:552
  15.3 8.8 %collective-permute-start.2 = (bf16[128,128]{1,0:T(8,128)(2,1)S(1)}, bf16[128,128]{1,0:T(8,128)(2,1)S(1)}, u32[]{:S(2)}, u32[]{:S(2)}) collective-permute-start(bf16[128,128]{1,0:T(8,128)(2,1)S(1)} %pad_maximum_fusion), channel_id=1, source_target_pairs={{0,8},{2,10},{4,12},{6,14},{16,24},{18,26},{20,28},{22,30},{32,40}... | collective-permute-start | bytes 98312 | tf_op jit(solution)/shard_map/ppermute | solution.py:552
  15.3 10.6 %collective-permute-start.3 = (bf16[128,128]{1,0:T(8,128)(2,1)S(1)}, bf16[128,128]{1,0:T(8,128)(2,1)S(1)}, u32[]{:S(2)}, u32[]{:S(2)}) collective-permute-start(bf16[128,128]{1,0:T(8,128)(2,1)S(1)} %pad_maximum_fusion.1), channel_id=1, source_target_pairs={{8,16},{10,18},{12,20},{14,22},{24,32},{26,34},{28,36},{30,38},{40... | collective-permute-start | bytes 98312 | tf_op jit(solution)/shard_map/ppermute | solution.py:552
  25.9 11.2 %copy-start.2 = (bf16[1,1,32,32,128]{4,3,2,1,0:T(8,128)(2,1)S(1)}, bf16[1,1,32,32,128]{4,3,2,1,0:T(8,128)(2,1)}, u32[]{:S(2)}) copy-start(bf16[1,1,32,32,128]{4,3,2,1,0:T(8,128)(2,1)} %param.14) | copy-start | bytes 786436
  27.6 6.5 %collective-permute-start.4 = (bf16[128,128]{1,0:T(8,128)(2,1)S(1)}, bf16[128,128]{1,0:T(8,128)(2,1)S(1)}, u32[]{:S(2)}, u32[]{:S(2)}) collective-permute-start(bf16[128,128]{1,0:T(8,128)(2,1)S(1)} %get-tuple-element.162), channel_id=1, source_target_pairs={{0,2},{4,6},{8,10},{12,14},{16,18},{20,22},{24,26},{28,30},{32,34}... | collective-permute-start | bytes 98312 | tf_op jit(solution)/shard_map/ppermute | solution.py:552
  27.7 9.2 %collective-permute-start.5 = (bf16[128,128]{1,0:T(8,128)(2,1)S(1)}, bf16[128,128]{1,0:T(8,128)(2,1)S(1)}, u32[]{:S(2)}, u32[]{:S(2)}) collective-permute-start(bf16[128,128]{1,0:T(8,128)(2,1)S(1)} %get-tuple-element.161), channel_id=1, source_target_pairs={{2,4},{6,8},{10,12},{14,16},{18,20},{22,24},{26,28},{30,32},{34,36... | collective-permute-start | bytes 98312 | tf_op jit(solution)/shard_map/ppermute | solution.py:552
  36.8 5.2 %collective-permute-start.6 = (bf16[128,128]{1,0:T(8,128)(2,1)S(1)}, bf16[128,128]{1,0:T(8,128)(2,1)S(1)}, u32[]{:S(2)}, u32[]{:S(2)}) collective-permute-start(bf16[128,128]{1,0:T(8,128)(2,1)S(1)} %pad_maximum_fusion.2), channel_id=1, source_target_pairs={{0,8},{2,10},{4,12},{6,14},{16,24},{18,26},{20,28},{22,30},{32,40}... | collective-permute-start | bytes 98312 | tf_op jit(solution)/shard_map/ppermute | solution.py:552
  37.0 10.6 %collective-permute-start.7 = (bf16[128,128]{1,0:T(8,128)(2,1)S(1)}, bf16[128,128]{1,0:T(8,128)(2,1)S(1)}, u32[]{:S(2)}, u32[]{:S(2)}) collective-permute-start(bf16[128,128]{1,0:T(8,128)(2,1)S(1)} %pad_maximum_fusion.3), channel_id=1, source_target_pairs={{8,16},{10,18},{12,20},{14,22},{24,32},{26,34},{28,36},{30,38},{40... | collective-permute-start | bytes 98312 | tf_op jit(solution)/shard_map/ppermute | solution.py:552
  50.7 7.8 %collective-permute-start.8 = (bf16[128,128]{1,0:T(8,128)(2,1)S(1)}, bf16[128,128]{1,0:T(8,128)(2,1)S(1)}, u32[]{:S(2)}, u32[]{:S(2)}) collective-permute-start(bf16[128,128]{1,0:T(8,128)(2,1)S(1)} %get-tuple-element.158), channel_id=1, source_target_pairs={{0,2},{4,6},{8,10},{12,14},{16,18},{20,22},{24,26},{28,30},{32,34}... | collective-permute-start | bytes 98312 | tf_op jit(solution)/shard_map/ppermute | solution.py:552
  50.8 9.3 %collective-permute-start.9 = (bf16[128,128]{1,0:T(8,128)(2,1)S(1)}, bf16[128,128]{1,0:T(8,128)(2,1)S(1)}, u32[]{:S(2)}, u32[]{:S(2)}) collective-permute-start(bf16[128,128]{1,0:T(8,128)(2,1)S(1)} %get-tuple-element.157), channel_id=1, source_target_pairs={{2,4},{6,8},{10,12},{14,16},{18,20},{22,24},{26,28},{30,32},{34,36... | collective-permute-start | bytes 98312 | tf_op jit(solution)/shard_map/ppermute | solution.py:552
  60.1 6.0 %collective-permute-start.10 = (bf16[128,128]{1,0:T(8,128)(2,1)S(1)}, bf16[128,128]{1,0:T(8,128)(2,1)S(1)}, u32[]{:S(2)}, u32[]{:S(2)}) collective-permute-start(bf16[128,128]{1,0:T(8,128)(2,1)S(1)} %pad_maximum_fusion.4), channel_id=1, source_target_pairs={{0,8},{2,10},{4,12},{6,14},{16,24},{18,26},{20,28},{22,30},{32,40}... | collective-permute-start | bytes 98312 | tf_op jit(solution)/shard_map/ppermute | solution.py:552
  60.2 10.6 %collective-permute-start.11 = (bf16[128,128]{1,0:T(8,128)(2,1)S(1)}, bf16[128,128]{1,0:T(8,128)(2,1)S(1)}, u32[]{:S(2)}, u32[]{:S(2)}) collective-permute-start(bf16[128,128]{1,0:T(8,128)(2,1)S(1)} %pad_maximum_fusion.5), channel_id=1, source_target_pairs={{8,16},{10,18},{12,20},{14,22},{24,32},{26,34},{28,36},{30,38},{40... | collective-permute-start | bytes 98312 | tf_op jit(solution)/shard_map/ppermute | solution.py:552
  77.2 1.7 %collective-permute-start.12 = (bf16[1152,128]{1,0:T(8,128)(2,1)S(1)}, bf16[1152,128]{1,0:T(8,128)(2,1)S(1)}, u32[]{:S(2)}, u32[]{:S(2)}) collective-permute-start(bf16[1152,128]{1,0:T(8,128)(2,1)S(1)} %get-tuple-element.133), channel_id=1, source_target_pairs={{0,2},{2,0},{1,3},{3,1},{4,6},{6,4},{5,7},{7,5},{8,10},{10,8},{9,1... | collective-permute-start | bytes 884744 | tf_op jit(solution)/shard_map/ppermute | solution.py:573
  79.6 13.1 %all-to-all-start = ((bf16[16,72,128]{2,1,0:T(8,128)(2,1)}), bf16[16,72,128]{2,1,0:T(8,128)(2,1)S(1)}, u32[]{:S(2)}, u32[]{:S(2)}) async-start(bf16[16,72,128]{2,1,0:T(8,128)(2,1)} %bitcast.28), calls=%async_computation | async-start | bytes 589824 | tf_op jit(solution)/shard_map/all_to_all | solution.py:585
  84.4 8.4 %collective-permute-start.13 = (bf16[128,128]{1,0:T(8,128)(2,1)S(1)}, bf16[128,128]{1,0:T(8,128)(2,1)S(1)}, u32[]{:S(2)}, u32[]{:S(2)}) collective-permute-start(bf16[128,128]{1,0:T(8,128)(2,1)S(1)} %get-tuple-element.154), channel_id=1, source_target_pairs={{0,2},{4,6},{8,10},{12,14},{16,18},{20,22},{24,26},{28,30},{32,34}... | collective-permute-start | bytes 98312 | tf_op jit(solution)/shard_map/ppermute | solution.py:552
  84.5 9.2 %collective-permute-start.14 = (bf16[128,128]{1,0:T(8,128)(2,1)S(1)}, bf16[128,128]{1,0:T(8,128)(2,1)S(1)}, u32[]{:S(2)}, u32[]{:S(2)}) collective-permute-start(bf16[128,128]{1,0:T(8,128)(2,1)S(1)} %get-tuple-element.153), channel_id=1, source_target_pairs={{2,4},{6,8},{10,12},{14,16},{18,20},{22,24},{26,28},{30,32},{34,36... | collective-permute-start | bytes 98312 | tf_op jit(solution)/shard_map/ppermute | solution.py:552
  94.3 12.5 %all-to-all-start.1 = ((bf16[8,72,128]{2,1,0:T(8,128)(2,1)}), bf16[8,72,128]{2,1,0:T(8,128)(2,1)S(1)}, u32[]{:S(2)}, u32[]{:S(2)}) async-start(bf16[8,72,128]{2,1,0:T(8,128)(2,1)} %broadcast_in_dim.32), calls=%async_computation.1 | async-start | bytes 294912 | tf_op jit(solution)/shard_map/all_to_all | solution.py:592
  107.7 16.0 %all-to-all-start.2 = ((bf16[16,72,128]{2,1,0:T(8,128)(2,1)}), bf16[16,72,128]{2,1,0:T(8,128)(2,1)S(1)}, u32[]{:S(2)}, u32[]{:S(2)}) async-start(bf16[16,72,128]{2,1,0:T(8,128)(2,1)} %broadcast_in_dim.33), calls=%async_computation.2 | async-start | bytes 589824 | tf_op jit(solution)/shard_map/all_to_all | solution.py:592
  112.6 7.3 %collective-permute-start.15 = (bf16[128,128]{1,0:T(8,128)(2,1)S(1)}, bf16[128,128]{1,0:T(8,128)(2,1)S(1)}, u32[]{:S(2)}, u32[]{:S(2)}) collective-permute-start(bf16[128,128]{1,0:T(8,128)(2,1)S(1)} %pad_maximum_fusion.6), channel_id=1, source_target_pairs={{0,8},{2,10},{4,12},{6,14},{16,24},{18,26},{20,28},{22,30},{32,40}... | collective-permute-start | bytes 98312 | tf_op jit(solution)/shard_map/ppermute | solution.py:552
  112.7 10.9 %collective-permute-start.16 = (bf16[128,128]{1,0:T(8,128)(2,1)S(1)}, bf16[128,128]{1,0:T(8,128)(2,1)S(1)}, u32[]{:S(2)}, u32[]{:S(2)}) collective-permute-start(bf16[128,128]{1,0:T(8,128)(2,1)S(1)} %pad_maximum_fusion.7), channel_id=1, source_target_pairs={{8,16},{10,18},{12,20},{14,22},{24,32},{26,34},{28,36},{30,38},{40... | collective-permute-start | bytes 98312 | tf_op jit(solution)/shard_map/ppermute | solution.py:552
  123.7 1.6 %collective-permute-start.17 = (bf16[1152,128]{1,0:T(8,128)(2,1)S(1)}, bf16[1152,128]{1,0:T(8,128)(2,1)S(1)}, u32[]{:S(2)}, u32[]{:S(2)}) collective-permute-start(bf16[1152,128]{1,0:T(8,128)(2,1)S(1)} %bitcast.62), channel_id=1, source_target_pairs={{0,2},{2,0},{1,3},{3,1},{4,6},{6,4},{5,7},{7,5},{8,10},{10,8},{9,1... | collective-permute-start | bytes 884744 | tf_op jit(solution)/shard_map/ppermute | solution.py:573

commit v3 on v2

--- a/solution.py
+++ b/solution.py
@@ -118,10 +118,10 @@
         for part in range(CELLS // WIDTH):
             chosen = onehot(cells == lane + part * WIDTH)
             gather_ref[facing * MESSAGE : (facing + 1) * MESSAGE, part * WIDTH : (part + 1) * WIDTH] = chosen
-    send_cells(here, gather_ref[...], field_ref[...], sent_ref)
     slot = iota((8, MESSAGE), 1)
     for facing in range(4):
         owners_ref[slot_of_facing(here, facing)] = scattered_cells(codes_ref, here, facing, slot)
+    send_cells(here, gather_ref[...], field_ref[...], sent_ref)
 
 
 def send_cells(here, gather, field, sent_ref):
@@ -159,25 +159,34 @@
     return lax.broadcasted_iota(jnp.int32, shape, dim)
 
 
-def fill_inside(padded_ref, here, field, by_a, by_b):
+def fill_inside(inside_ref, here, field, by_a, by_b):
     side = side_of(here, 0)
     west, east = jnp.where(side == 0, by_b, by_a), jnp.where(side == 0, by_a, by_b)
     cols = (SIZE * 8, MESSAGE)
     place = onehot(col_rim_slots(iota(cols, 0), 5) == iota(cols, 1))
-    padded_ref[3:35, 0:8] = matmul(place, west).reshape(SIZE, 8, WIDTH)
+    inside_ref[:, 0:8] = matmul(place, west).reshape(SIZE, 8, WIDTH)
     place = onehot(col_rim_slots(iota(cols, 0), 0) == iota(cols, 1))
-    padded_ref[3:35, 40:48] = matmul(place, east).reshape(SIZE, 8, WIDTH)
-    padded_ref[3:35, 8:40] = field.astype(F32).reshape(SIZE, SIZE, WIDTH)
-
-
-def fill_rims(padded_ref, here, by_c, by_d):
+    inside_ref[:, 40:48] = matmul(place, east).reshape(SIZE, 8, WIDTH)
+    inside_ref[:, 8:40] = field.astype(F32).reshape(SIZE, SIZE, WIDTH)
+
+
+def fill_ends(ends_ref, rims_ref, here, inside_ref, by_c, by_d):
     row_side, col_side = side_of(here, 2), side_of(here, 0)
     north, south = jnp.where(row_side == 0, by_d, by_c), jnp.where(row_side == 0, by_c, by_d)
     rows = (3 * PAD_COLS, MESSAGE)
     slots = row_rim_slots(iota(rows, 0), True, 112 - 16 * col_side, 96 + 16 * col_side)
     place = onehot(slots == iota(rows, 1))
-    padded_ref[0:3] = matmul(place, north).reshape(3, PAD_COLS, WIDTH)
-    padded_ref[35:38] = matmul(place, south).reshape(3, PAD_COLS, WIDTH)
+    rims_ref[0:3] = matmul(place, north).reshape(3, PAD_COLS, WIDTH)
+    rims_ref[3:6] = matmul(place, south).reshape(3, PAD_COLS, WIDTH)
+    ends_ref[0:3] = rims_ref[0:3]
+    ends_ref[3:10] = inside_ref[0:7]
+    ends_ref[10:17] = inside_ref[25:32]
+    ends_ref[17:20] = rims_ref[3:6]
+
+
+def convolve_ends(ends_ref, params, bias, conv_ref):
+    convolve(ends_ref, 5, params, False, bias, conv_ref, 0, 1)
+    convolve(ends_ref, 5, params, False, bias, conv_ref, 7, 8, 18)
 
 
 def tap(kernel, row_tap, col_tap):
@@ -185,12 +194,12 @@
     return ref[row_tap * TAPS + col_tap, block : block + 1, :]
 
 
-def convolve(source_ref, first_col, kernel_ref, flipped, start, out_ref, first=0, last=SIZE // 4):
+def convolve(source_ref, first_col, kernel_ref, flipped, start, out_ref, first=0, last=SIZE // 4, shift=0):
     def group(index, carry):
         totals = [jnp.broadcast_to(start, (SIZE, WIDTH)) for _ in range(4)]
         for col_tap in range(TAPS):
             for row in range(4 + TAPS - 1):
-                values = source_ref[index * 4 + row, first_col + col_tap : first_col + col_tap + SIZE, :]
+                values = source_ref[index * 4 + row - shift, first_col + col_tap : first_col + col_tap + SIZE, :]
                 for out in range(max(0, row - TAPS + 1), min(4, row + 1)):
                     a, e = row - out, col_tap
                     if flipped:
@@ -306,11 +315,11 @@
 
 def first_inside_kernel(
     here_ref, field_ref, a_ref, b_ref, params_ref, up_ref, down_ref,
-    out_ref, conv_ref, padded_ref, full_ref,
+    out_ref, conv_ref, inside_ref, full_ref,
 ):
-    fill_inside(padded_ref, here_ref[0], field_ref[...], a_ref[...], b_ref[...])
+    fill_inside(inside_ref, here_ref[0], field_ref[...], a_ref[...], b_ref[...])
     bias, gain, offset, down_b, scale, up_b = block_rows(params_ref, 0)
-    convolve(padded_ref, 5, (params_ref, 0), False, bias, full_ref, 1, 7)
+    convolve(inside_ref, 5, (params_ref, 0), False, bias, full_ref, 1, 7, 3)
 
     def chunk(index, carry):
         at = pl.ds(pl.multiple_of(index * CHUNK, CHUNK), CHUNK)
@@ -322,7 +331,7 @@
         )
         return carry
 
-    lax.fori_loop(0, INSIDE // CHUNK, chunk, 0)
+    lax.fori_loop(0, INSIDE // CHUNK, chunk, 0, unroll=True)
 
 
 def ends(ref):
@@ -336,15 +345,13 @@
 
 
 def first_kernel(
-    here_ref, field_ref, c_ref, d_ref, a_ref, b_ref, out_in_ref, gather_ref, params_ref, up_ref, down_ref,
-    out_ref, conv_ref, padded_ref, sent_ref, full_ref,
+    here_ref, field_ref, c_ref, d_ref, inside_ref, out_in_ref, gather_ref, params_ref, up_ref, down_ref,
+    out_ref, conv_ref, rims_ref, sent_ref, ends_ref, full_ref,
 ):
     here = here_ref[0]
-    fill_inside(padded_ref, here, field_ref[...], a_ref[...], b_ref[...])
-    fill_rims(padded_ref, here, c_ref[...], d_ref[...])
+    fill_ends(ends_ref, rims_ref, here, inside_ref, c_ref[...], d_ref[...])
     bias, gain, offset, down_b, scale, up_b = block_rows(params_ref, 0)
-    for index in (0, 7):
-        convolve(padded_ref, 5, (params_ref, 0), False, bias, full_ref, index, index + 1)
+    convolve_ends(ends_ref, (params_ref, 0), bias, full_ref)
     conv = ends(full_ref)
     conv_ref[...] = conv
     out = forward_chunk(conv, ends(field_ref), (gain, offset, down_b, scale), up_ref[0], up_b, down_ref[0])
@@ -422,10 +429,10 @@
 
 def second_inside_kernel(
     here_ref, field_ref, a_ref, b_ref, cotangent_ref, params_ref, up_ref, down_ref,
-    out_ref, grad_ref, up_sum, down_sum, vector_sum, up_b_sum, padded_ref, conv_ref,
+    out_ref, inside_ref, grad_ref, up_sum, down_sum, vector_sum, up_b_sum, conv_ref,
 ):
-    fill_inside(padded_ref, here_ref[0], field_ref[...], a_ref[...], b_ref[...])
-    convolve(padded_ref, 5, (params_ref, 1), False, block_rows(params_ref, 1)[0], conv_ref, 1, 7)
+    fill_inside(inside_ref, here_ref[0], field_ref[...], a_ref[...], b_ref[...])
+    convolve(inside_ref, 5, (params_ref, 1), False, block_rows(params_ref, 1)[0], conv_ref, 1, 7, 3)
     refs = (params_ref, up_ref, down_ref, up_sum, down_sum, vector_sum, up_b_sum)
     clear(refs[3:])
 
@@ -437,20 +444,18 @@
         )
         return carry
 
-    lax.fori_loop(0, INSIDE // CHUNK, chunk, 0)
+    lax.fori_loop(0, INSIDE // CHUNK, chunk, 0, unroll=True)
 
 
 def second_kernel(
-    here_ref, field_ref, c_ref, d_ref, a_ref, b_ref, grad_in_ref, up_in, down_in, vector_in, up_b_in,
+    here_ref, field_ref, c_ref, d_ref, inside_ref, grad_in_ref, up_in, down_in, vector_in, up_b_in,
     cotangent_ref, params_ref, up_ref, down_ref,
-    out_ref, padded_ref, grad_ref, sent_ref, weights_ref, sums_ref,
-    conv_ref, grown_ref, up_sum, down_sum, vector_sum, up_b_sum, rim_ref,
+    out_ref, rims_ref, grad_ref, sent_ref, weights_ref, sums_ref,
+    ends_ref, conv_ref, grown_ref, up_sum, down_sum, vector_sum, up_b_sum, rim_ref,
 ):
     here = here_ref[0]
-    fill_inside(padded_ref, here, field_ref[...], a_ref[...], b_ref[...])
-    fill_rims(padded_ref, here, c_ref[...], d_ref[...])
-    for index in (0, 7):
-        convolve(padded_ref, 5, (params_ref, 1), False, block_rows(params_ref, 1)[0], conv_ref, index, index + 1)
+    fill_ends(ends_ref, rims_ref, here, inside_ref, c_ref[...], d_ref[...])
+    convolve_ends(ends_ref, (params_ref, 1), block_rows(params_ref, 1)[0], conv_ref)
     refs = (params_ref, up_ref, down_ref, up_sum, down_sum, vector_sum, up_b_sum)
     for ref, start in zip(refs[3:], (up_in, down_in, vector_in, up_b_in)):
         ref[...] = start[...]
@@ -474,17 +479,16 @@
         inv_std_ref[at, :] = jnp.broadcast_to(saved[1], (CHUNK, WIDTH))
         return carry
 
-    lax.fori_loop(0, CELLS // CHUNK, chunk, 0)
+    lax.fori_loop(0, CELLS // CHUNK, chunk, 0, unroll=True)
 
 
 def third_kernel(
-    here_ref, standard_ref, inv_std_ref, normed_ref, activated_ref, slope_ref, branch_ref, cotangent_ref, inner_ref,
-    c_ref, d_ref, a_ref, b_ref, scatter_ref, params_ref, up_ref, down_ref,
+    here_ref, standard_ref, inv_std_ref, normed_ref, activated_ref, slope_ref, branch_ref, base_ref, c_ref, d_ref,
+    scatter_ref, params_ref, up_ref, down_ref,
     upstream_ref, grad_ref, sent_ref, weights_ref, sums_ref,
     grown_ref, up_sum, down_sum, vector_sum, up_b_sum, rim_ref,
 ):
-    returned = jnp.concatenate([c_ref[...], d_ref[...], a_ref[...], b_ref[...]], axis=0)
-    upstream_ref[...] = cotangent_ref[...].astype(F32) + inner_ref[...] + matmul(scatter_ref[...], returned)
+    upstream_ref[...] = base_ref[...] + owned(scatter_ref, 0, c_ref, d_ref)
     refs = (params_ref, up_ref, down_ref, up_sum, down_sum, vector_sum, up_b_sum)
     clear(refs[3:])
     saved_refs = (standard_ref, inv_std_ref, normed_ref, activated_ref, slope_ref, branch_ref)
@@ -494,27 +498,41 @@
         grad_ref[at, :] = backward_chunk(0, [ref[at, :] for ref in saved_refs], upstream_ref[at, :], refs)
         return carry
 
-    lax.fori_loop(0, CELLS // CHUNK, chunk, 0)
+    lax.fori_loop(0, CELLS // CHUNK, chunk, 0, unroll=True)
     fill_grown(grown_ref, grad_ref[...])
     send_rims(here_ref[0], grown_ref, (params_ref, 0), rim_ref, sent_ref)
     pack_sums(refs, weights_ref, sums_ref)
 
 
-def last_kernel(upstream_ref, inner_ref, c_ref, d_ref, a_ref, b_ref, scatter_ref, out_ref):
-    returned = jnp.concatenate([c_ref[...], d_ref[...], a_ref[...], b_ref[...]], axis=0)
-    out_ref[...] = (upstream_ref[...] + inner_ref[...] + matmul(scatter_ref[...], returned)).astype(BF)
+def owned(scatter_ref, first, *refs):
+    lanes = slice(first * MESSAGE, (first + len(refs)) * MESSAGE)
+    return matmul(scatter_ref[:, lanes], jnp.concatenate([ref[...] for ref in refs], axis=0))
+
+
+def last_kernel(base_ref, c_ref, d_ref, scatter_ref, out_ref):
+    out_ref[...] = (base_ref[...] + owned(scatter_ref, 0, c_ref, d_ref)).astype(BF)
 
 
 def make_inner_kernel(block):
-    def inner_kernel(grad_ref, params_ref, inner_ref, grown_ref):
+    def inner_kernel(grad_ref, upstream_ref, a_ref, b_ref, scatter_ref, params_ref, base_ref, grown_ref):
         fill_grown(grown_ref, grad_ref[...])
-        convolve(grown_ref, 13, (params_ref, block), True, jnp.zeros((1, WIDTH), F32), inner_ref)
+        convolve(grown_ref, 13, (params_ref, block), True, jnp.zeros((1, WIDTH), F32), base_ref)
+        base_ref[...] += upstream_ref[...].astype(F32) + owned(scatter_ref, 2, a_ref, b_ref)
 
     return inner_kernel
 
 
-def taps_and_out_kernel(padded_ref, grad_ref, inside_ref, edges_ref, taps_ref, out_ref, sums_ref):
+def fill_padded(padded_ref, inside_ref, rims_ref):
+    padded_ref[0:3] = rims_ref[0:3]
+    padded_ref[3:35] = inside_ref[...]
+    padded_ref[35:38] = rims_ref[3:6]
+
+
+def taps_and_out_kernel(
+    pad_inside_ref, pad_rims_ref, grad_ref, inside_ref, edges_ref, taps_ref, out_ref, padded_ref, sums_ref
+):
     join_rows(out_ref, inside_ref[...], edges_ref[...])
+    fill_padded(padded_ref, pad_inside_ref, pad_rims_ref)
     taps_kernel(padded_ref, grad_ref, taps_ref, sums_ref)
 
 
@@ -524,9 +542,10 @@
 
 
 def halves_kernel(
-    core_ref, padded_ref, grad_ref, weights_0_ref, sums_0_ref, weights_1_ref, sums_1_ref, taps_1_ref,
-    kept_ref, given_ref, taps_ref, partial_ref,
+    core_ref, pad_inside_ref, pad_rims_ref, grad_ref, weights_0_ref, sums_0_ref, weights_1_ref, sums_1_ref, taps_1_ref,
+    kept_ref, given_ref, taps_ref, padded_ref, partial_ref,
 ):
+    fill_padded(padded_ref, pad_inside_ref, pad_rims_ref)
     taps_kernel(padded_ref, grad_ref, taps_ref, partial_ref)
 
     def fill(half_ref, *parts):
@@ -553,7 +572,8 @@
 
 
 def beside(sent):
-    return swapped_tiles(sent[2], 1, 0), swapped_tiles(sent[3], 1, 1)
+    by_b = swapped_tiles(sent[3], 1, 1)
+    return swapped_tiles(sent[2], 1, 0), by_b
 
 
 def beyond(sent, by_a, by_b):
@@ -562,22 +582,11 @@
     return by_c, by_d
 
 
-def after(values, *others):
-    return lax.optimization_barrier((values, others))[0]
-
-
 HALF_ROWS = 1152
 
 
 def swapped(value, axis):
     return lax.ppermute(value, axis, [(0, 1), (1, 0)])
-
-
-def joined(value, axis):
-    other = swapped(value, axis)
-    return jnp.where(
-        lax.axis_index(axis) == 0, jnp.concatenate([value, other]), jnp.concatenate([other, value])
-    )
 
 
 def summed_apart(value, axes):
@@ -601,15 +610,14 @@
 
 
 def make_unpack_kernel(factor):
-    def unpack_kernel(sum_ref, taps, conv_b, gain, offset, up, up_b, down, down_b, scale):
-        for block in range(BLOCKS):
-            base = block * HALF_ROWS
+    def unpack_kernel(core_ref, mine_ref, other_ref, taps, conv_b, gain, offset, up, up_b, down, down_b, scale):
+        def unpack(sum_ref, block):
             for part in range(HID // WIDTH):
-                rows = slice(base + part * WIDTH, base + (part + 1) * WIDTH)
+                rows = slice(part * WIDTH, (part + 1) * WIDTH)
                 up[block, :, part * WIDTH : (part + 1) * WIDTH] = sum_ref[rows, :].astype(F32) * factor
-                rows = slice(base + HID + part * WIDTH, base + HID + (part + 1) * WIDTH)
+                rows = slice(HID + part * WIDTH, HID + (part + 1) * WIDTH)
                 down[block, part * WIDTH : (part + 1) * WIDTH, :] = (sum_ref[rows, :].astype(F32) * factor).T
-            base += 2 * HID
+            base = 2 * HID
             vectors = sum_ref[base : base + 16, :].astype(F32) * factor
             for row, ref in enumerate((conv_b, gain, offset, down_b, scale)):
                 ref[block : block + 1, :] = vectors[row : row + 1]
@@ -619,6 +627,13 @@
             kernel_sum = sum_ref[base : base + 64, :].astype(F32) * factor
             for row in range(TAPS * TAPS):
                 taps[row, block : block + 1, :] = kernel_sum[row : row + 1]
+
+        for core in range(2):
+
+            @pl.when(core_ref[0] == core)
+            def _(core=core):
+                unpack(mine_ref, core)
+                unpack(other_ref, 1 - core)
 
     return unpack_kernel
 
@@ -657,11 +672,12 @@
 ):
     count = lax.axis_size(TILE_AXES) * lax.axis_size("member")
     here = lax.axis_index(TILE_AXES).astype(jnp.int32).reshape(1)
-    codes = jnp.concatenate([seam_codes.T, corner_codes.T])
     field = states.reshape(CELLS, WIDTH)
     upstream = cotangent.reshape(CELLS, WIDTH)
     message = ((4, MESSAGE, WIDTH), BF)
-    padded_shape = ((PAD_ROWS, PAD_COLS, WIDTH), F32)
+    inside_shape = ((SIZE, PAD_COLS, WIDTH), F32)
+    rims_shape = ((6, PAD_COLS, WIDTH), F32)
+    ends_scratch = pltpu.VMEM((20, PAD_COLS, WIDTH), F32)
     weights_shape = ((2 * HID, WIDTH), BF)
     sums_shape = ((16, WIDTH), BF)
     cells = (CELLS, WIDTH)
@@ -674,6 +690,7 @@
     tap_scratch = [pltpu.VMEM((64 * 8, WIDTH), F32)]
     vpu = pl.CostEstimate(flops=2 * 49 * CELLS * WIDTH, bytes_accessed=3 << 20, transcendentals=0)
 
+    codes = jnp.concatenate([seam_codes.T, corner_codes.T])
     sent, gather, owners = call(
         select_kernel,
         [message, ((4 * MESSAGE, CELLS), BF), ((4, 8, MESSAGE), jnp.int32)],
@@ -689,51 +706,57 @@
     near, packed = lax.optimization_barrier((near, packed))
     params = (packed, up_weight, down_weight)
     far = beyond(sent, *near)
-    part, conv_part = call(
+    part, conv_part, pad_inside_0 = call(
         first_inside_kernel,
-        [(inside, BF), (inside, F32)],
+        [(inside, BF), (inside, F32), inside_shape],
         [here, field, *near, *params],
-        [padded_scratch, cells_scratch],
+        [cells_scratch],
         scalars=1,
         cost=vpu,
     )
-    middle, conv_edges, padded_0, sent = call(
+    middle, conv_edges, pad_rims_0, sent = call(
         first_kernel,
-        [(cells, BF), (edges, F32), padded_shape, message],
-        [here, field, *far, *near, part, gather, *params],
-        [cells_scratch],
+        [(cells, BF), (edges, F32), rims_shape, message],
+        [here, field, *far, pad_inside_0, part, gather, *params],
+        [ends_scratch, cells_scratch],
         scalars=1,
     )
     near = beside(sent)
     (scatter,) = call(scatter_kernel, [((CELLS, 4 * MESSAGE), BF)], [owners], cost=vpu)
     near, scatter = lax.optimization_barrier((near, scatter))
     far = beyond(sent, *near)
-    out_part, *partial = call(
+    out_part, pad_inside_1, *partial = call(
         second_inside_kernel,
-        [(inside, BF), (inside, F32), *wide_sums],
+        [(inside, BF), inside_shape, (inside, F32), *wide_sums],
         [here, middle, *near, upstream, *params],
-        [padded_scratch, cells_scratch],
+        [cells_scratch],
         scalars=1,
         cost=vpu,
     )
-    out_edges, padded_1, grad_1, sent, weights_1, sums_1 = call(
+    out_edges, pad_rims_1, grad_1, sent, weights_1, sums_1 = call(
         second_kernel,
-        [(edges, BF), padded_shape, (cells, F32), message, weights_shape, sums_shape],
-        [here, middle, *far, *near, *partial, upstream, *params],
-        [cells_scratch, *sums],
+        [(edges, BF), rims_shape, (cells, F32), message, weights_shape, sums_shape],
+        [here, middle, *far, pad_inside_1, *partial, upstream, *params],
+        [ends_scratch, cells_scratch, *sums],
         scalars=1,
     )
     near = beside(sent)
     taps_1, out = call(
         taps_and_out_kernel,
         [((64, WIDTH), BF), (cells, BF)],
-        [padded_1, grad_1, out_part, out_edges],
-        tap_scratch,
+        [pad_inside_1, pad_rims_1, grad_1, out_part, out_edges],
+        [padded_scratch, *tap_scratch],
         cost=vpu,
     )
     near, taps_1 = lax.optimization_barrier((near, taps_1))
     far = beyond(sent, *near)
-    (inner_1,) = call(make_inner_kernel(1), [(cells, F32)], [grad_1, packed], [grown_scratch], cost=vpu)
+    (base_1,) = call(
+        make_inner_kernel(1),
+        [(cells, F32)],
+        [grad_1, upstream, *near, scatter, packed],
+        [grown_scratch],
+        cost=vpu,
+    )
     saved = call(
         third_again_kernel,
         [(cells, F32), (cells, F32), (cells, BF), ((CELLS, HID), BF), ((CELLS, HID), F32), (cells, F32)],
@@ -741,11 +764,11 @@
         [cells_scratch],
         cost=vpu,
     )
-    far, inner_1, saved = lax.optimization_barrier((far, inner_1, saved))
+    far, base_1, saved = lax.optimization_barrier((far, base_1, saved))
     upstream_0, grad_0, sent, weights_0, sums_0 = call(
         third_kernel,
         [(cells, F32), (cells, F32), message, weights_shape, sums_shape],
-        [here, *saved, upstream, inner_1, *far, *near, scatter, *params],
+        [here, *saved, base_1, *far, scatter, *params],
         sums,
         scalars=1,
     )
@@ -754,19 +777,28 @@
     kept, given = call(
         halves_kernel,
         [((HALF_ROWS, WIDTH), BF), ((HALF_ROWS, WIDTH), BF)],
-        [core, padded_0, grad_0, weights_0, sums_0, weights_1, sums_1, taps_1],
-        [pltpu.VMEM((64, WIDTH), BF), *tap_scratch],
+        [core, pad_inside_0, pad_rims_0, grad_0, weights_0, sums_0, weights_1, sums_1, taps_1],
+        [pltpu.VMEM((64, WIDTH), BF), padded_scratch, *tap_scratch],
         scalars=1,
     )
     total = (kept.astype(F32) + swapped(given, "core").astype(F32)).astype(BF)
     total = summed_apart(total, ACROSS)
     total, near = lax.optimization_barrier((total, near))
     far = beyond(sent, *near)
-    (inner_0,) = call(make_inner_kernel(0), [(cells, F32)], [grad_0, packed], [grown_scratch], cost=vpu)
-    total = gathered(summed_along(total, "z"), ACROSS)
-    total, far, inner_0 = lax.optimization_barrier((total, far, inner_0))
-    (grad_field,) = call(last_kernel, [(cells, BF)], [upstream_0, inner_0, *far, *near, scatter])
-    total = joined(total, "core")
+    (base_0,) = call(
+        make_inner_kernel(0),
+        [(cells, F32)],
+        [grad_0, upstream_0, *near, scatter, packed],
+        [grown_scratch],
+        cost=vpu,
+    )
+    total = summed_along(total, "z")
+    (by_c, by_d), (total, by_c) = far, lax.optimization_barrier((total, far[0]))
+    far = (by_c, by_d)
+    total = gathered(total, ACROSS)
+    total, far, base_0 = lax.optimization_barrier((total, far, base_0))
+    (grad_field,) = call(last_kernel, [(cells, BF)], [base_0, *far, scatter])
+    halves = (total, swapped(total, "core"))
     row, wide = ((BLOCKS, WIDTH), F32), ((BLOCKS, HID), F32)
     grads = call(
         make_unpack_kernel(1.0 / math.sqrt(count * CELLS)),
@@ -774,7 +806,8 @@
             ((TAPS * TAPS, BLOCKS, WIDTH), F32), row, row, row, ((BLOCKS, WIDTH, HID), F32), wide,
             ((BLOCKS, HID, WIDTH), F32), row, row,
         ],
-        [total],
+        [core, *halves],
+        scalars=1,
     )
     kernel_grad = grads[0].reshape(TAPS, TAPS, BLOCKS, WIDTH).transpose(2, 0, 1, 3)
     shape = states.shape

time: 128 us -> 126 us (0.984)
  waiting for transfers between devices: 34.6 us -> 31.4 us
  Pallas kernels: 33.7 us -> 30.7 us
  starting transfers between devices: 52.1 us -> 54.8 us
    all_to_all x2, waiting for transfers between devices: 9.14 us -> 6.05 us  [gathered(): return lax.all_to_all(copies, axes, 0, 0, tiled=True)]
    pallas_call x14, Pallas kernels: 33.7 us -> 30.7 us  [call(): pl.pallas_call(kernel, out_shape=shaped(*shapes), in_specs=specs, out_spe...]
    ppermute x16, starting transfers between devices: 38.8 us -> 41.4 us  [swapped_tiles(): lax.ppermute(value, TILE_AXES, pairs + [(target, source) for source, targ...]
  transfers between devices with their start and end apart: 21 -> 21, of which waited for: 12 -> 12; matrix products, arithmetic and copies ran while one was open for 1% -> 1% of each run, Pallas kernels for 16% -> 15%
where the time goes in v3:
time: 126 us; the launch traced here: 124 us
  starting transfers between devices  54.8 us (43%)
  waiting for transfers between devices  31.4 us (25%)
  Pallas kernels  30.7 us (24%)
  local copies, waits for them, and re-layouts  3.4 us (3%)
  other arithmetic  2.57 us (2%)
    ppermute x16, starting transfers between devices, swapped_tiles(): lax.ppermute(value, TILE_AXES, pairs + [(target, source) for source, targ...  41.4 us
    pallas_call x14, Pallas kernels, call(): pl.pallas_call(kernel, out_shape=shaped(*shapes), in_specs=specs, out_spe...  30.7 us
    ppermute x16, waiting for transfers between devices, swapped_tiles(): lax.ppermute(value, TILE_AXES, pairs + [(target, source) for source, targ...  20.6 us
    all_to_all x2, starting transfers between devices, gathered(): return lax.all_to_all(copies, axes, 0, 0, tiled=True)  8.59 us
    all_to_all x2, waiting for transfers between devices, gathered(): return lax.all_to_all(copies, axes, 0, 0, tiled=True)  6.05 us
    all_to_all x1, starting transfers between devices, summed_apart(): lax.all_to_all(value, axes, 0, 0, tiled=True).reshape(count, -1, WIDTH)  4.76 us
    all_to_all x1, waiting for transfers between devices, summed_apart(): lax.all_to_all(value, axes, 0, 0, tiled=True).reshape(count, -1, WIDTH)  2.64 us
  transfers between devices with their start and end apart: 21, of which 12 were waited for; matrix products, arithmetic and copies ran while one was open for 1% of the time, Pallas kernels for 15%

profile of v3, /device:TPU:2, one launch (start us, length us, event | category | flops | bytes accessed | tf_op | source)
XLA Modules:
  0.0 123.9 jit_solution(2041565190348546097)
XLA Ops:
  0.7 0.8 pad_add_fusion.1.codes_ref
  1.4 0.9 copy-done.2
  2.4 1.2 shard_map.212
  3.6 9.4 %collective-permute-start.1 = (bf16[128,128]{1,0:T(8,128)(2,1)S(1)}, bf16[128,128]{1,0:T(8,128)(2,1)S(1)}, u32[]{:S(2)}, u32[]{:S(2)}) collective-permute-start(bf16[128,128]{1,0:T(8,128)(2,1)S(1)} %get-tuple-element.173), channel_id=1, source_target_pairs={{2,4},{6,8},{10,12},{14,16},{18,20},{22,24},{26,28},{30,32},{34,36... | collective-permute-start | bytes 98312 | tf_op jit(solution)/shard_map/ppermute | solution.py:571
  13.0 0.9 pad_add_fusion.params_ref
  13.9 0.7 collective-permute-done.1.b_ref
  14.6 0.1 collective-permute-start.2
  14.7 5.4 %collective-permute-start.3 = (bf16[128,128]{1,0:T(8,128)(2,1)S(1)}, bf16[128,128]{1,0:T(8,128)(2,1)S(1)}, u32[]{:S(2)}, u32[]{:S(2)}) collective-permute-start(bf16[128,128]{1,0:T(8,128)(2,1)S(1)} %pad_maximum_fusion.1), channel_id=1, source_target_pairs={{8,16},{10,18},{12,20},{14,22},{24,32},{26,34},{28,36},{30,38},{40... | collective-permute-start | bytes 98312 | tf_op jit(solution)/shard_map/ppermute | solution.py:571
  20.1 0.3 shard_map.215.scatter_ref
  20.4 0.9 copy-done.3
  21.3 3.6 %shard_map.213 = (bf16[768,128]{1,0:T(8,128)(2,1)S(1)}, f32[768,128]{1,0:T(8,128)S(1)}, f32[32,48,128]{2,1,0:T(8,128)S(1)}) custom-call(s32[1]{0:T(128)} %bitcast.here_ref, bf16[1024,128]{1,0:T(8,128)(2,1)S(1)} %bitcast.57, bf16[128,128]{1,0:T(8,128)(2,1)S(1)} %collective-permute-done.a_ref, bf16[128,128]{1,0:T(8,128)(2,1)S(1)} %collective-permute-done.1.b_ref, ...), custom_call_target="tpu_custom_call" | custom-call | flops 12845056 | bytes 3145728 | tf_op jit(solution)/shard_map/pallas_call | solution.py:658
  24.9 0.4 collective-permute-done.3.d_ref
  25.3 1.6 %shard_map.214 = (bf16[1024,128]{1,0:T(8,128)(2,1)S(1)}, f32[256,128]{1,0:T(8,128)S(1)}, f32[6,48,128]{2,1,0:T(8,128)S(1)}, bf16[4,128,128]{2,1,0:T(8,128)(2,1)S(1)}) custom-call(s32[1]{0:T(128)} %bitcast.here_ref, bf16[1024,128]{1,0:T(8,128)(2,1)S(1)} %bitcast.58, bf16[128,128]{1,0:T(8,128)(2,1)S(1)} %collective-permute-done.2.c_ref, ...), custom_call_target="tpu_custom_call" | custom-call | tf_op jit(solution)/shard_map/pallas_call | solution.py:658
  26.9 6.4 %collective-permute-start.5 = (bf16[128,128]{1,0:T(8,128)(2,1)S(1)}, bf16[128,128]{1,0:T(8,128)(2,1)S(1)}, u32[]{:S(2)}, u32[]{:S(2)}) collective-permute-start(bf16[128,128]{1,0:T(8,128)(2,1)S(1)} %get-tuple-element.169), channel_id=1, source_target_pairs={{2,4},{6,8},{10,12},{14,16},{18,20},{22,24},{26,28},{30,32},{34,36... | collective-permute-start | bytes 98312 | tf_op jit(solution)/shard_map/ppermute | solution.py:571
  33.3 2.7 %collective-permute-done.5.b_ref = bf16[128,128]{1,0:T(8,128)(2,1)S(1)} collective-permute-done((bf16[128,128]{1,0:T(8,128)(2,1)S(1)}, bf16[128,128]{1,0:T(8,128)(2,1)S(1)}, u32[]{:S(2)}, u32[]{:S(2)}) %collective-permute-start.5) | collective-permute-done | bytes 32800 | tf_op jit(solution)/shard_map/ppermute | solution.py:571
  36.1 0.1 collective-permute-start.6
  36.2 0.7 collective-permute-start.7
  36.9 4.2 %shard_map.216 = (bf16[768,128]{1,0:T(8,128)(2,1)S(1)}, f32[32,48,128]{2,1,0:T(8,128)S(1)}, f32[768,128]{1,0:T(8,128)S(1)}, f32[128,512]{1,0:T(8,128)S(1)}, f32[...) custom-call(s32[1]{0:T(128)} %bitcast.here_ref, ...), custom_call_target="tpu_custom_call" | custom-call | flops 12845056 | bytes 3145728 | tf_op jit(solution)/shard_map/pallas_call | solution.py:658
  41.1 5.9 %collective-permute-done.7.d_ref = bf16[128,128]{1,0:T(8,128)(2,1)S(1)} collective-permute-done((bf16[128,128]{1,0:T(8,128)(2,1)S(1)}, bf16[128,128]{1,0:T(8,128)(2,1)S(1)}, u32[]{:S(2)}, u32[]{:S(2)}) %collective-permute-start.7) | collective-permute-done | bytes 32800 | tf_op jit(solution)/shard_map/ppermute | solution.py:571
  47.0 2.8 %shard_map.217 = (bf16[256,128]{1,0:T(8,128)(2,1)S(1)}, f32[6,48,128]{2,1,0:T(8,128)S(1)}, f32[1024,128]{1,0:T(8,128)S(1)}, bf16[4,128,128]{2,1,0:T(8,128)(2,1)S...) custom-call(s32[1]{0:T(128)} %bitcast.here_ref, bf16[1024,128]{1,0:T(8,128)(2,1)S(1)} %get-tuple-element.92.field_ref, ...), custom_call_target="tpu_custom_call" | custom-call | tf_op jit(solution)/shard_map/pallas_call | solution.py:658
  49.9 5.2 %collective-permute-start.9 = (bf16[128,128]{1,0:T(8,128)(2,1)S(1)}, bf16[128,128]{1,0:T(8,128)(2,1)S(1)}, u32[]{:S(2)}, u32[]{:S(2)}) collective-permute-start(bf16[128,128]{1,0:T(8,128)(2,1)S(1)} %get-tuple-element.165), channel_id=1, source_target_pairs={{2,4},{6,8},{10,12},{14,16},{18,20},{22,24},{26,28},{30,32},{34,36... | collective-permute-start | bytes 98312 | tf_op jit(solution)/shard_map/ppermute | solution.py:571
  55.1 2.3 %shard_map.218 = (bf16[64,128]{1,0:T(8,128)(2,1)S(1)}, bf16[1024,128]{1,0:T(8,128)(2,1)}) custom-call(f32[32,48,128]{2,1,0:T(8,128)S(1)} %get-tuple-element.97.inside_ref.pad_inside_ref, f32[6,48,128]{2,1,0:T(8,128)S(1)} %get-tuple-element.103.pad_rims_ref, f32[1024,128]{1,0:T(8,128)S(1)} %get-tuple-element.104.grad_ref, ...), custom_call_target="tpu_custom_call" | custom-call | flops 12845056 | bytes 3145728 | tf_op jit(solution)/shard_map/pallas_call | solution.py:658
  57.4 1.6 %collective-permute-done.9.b_ref = bf16[128,128]{1,0:T(8,128)(2,1)S(1)} collective-permute-done((bf16[128,128]{1,0:T(8,128)(2,1)S(1)}, bf16[128,128]{1,0:T(8,128)(2,1)S(1)}, u32[]{:S(2)}, u32[]{:S(2)}) %collective-permute-start.9) | collective-permute-done | bytes 32800 | tf_op jit(solution)/shard_map/ppermute | solution.py:571
  59.0 0.1 collective-permute-start.10
  59.1 0.3 collective-permute-start.11
  59.5 2.1 %shard_map.220 = (f32[1024,128]{1,0:T(8,128)S(1)}, f32[1024,128]{1,0:T(8,128)S(1)}, bf16[1024,128]{1,0:T(8,128)(2,1)S(1)}, bf16[1024,512]{1,0:T(8,128)(2,1)S(1)}...) custom-call(f32[768,128]{1,0:T(8,128)S(1)} %get-tuple-element.114.conv_ref, ...), custom_call_target="tpu_custom_call" | custom-call | flops 12845056 | bytes 3145728 | tf_op jit(solution)/shard_map/pallas_call | solution.py:658
  61.5 2.8 %shard_map.219.base_ref = f32[1024,128]{1,0:T(8,128)S(1)} custom-call(f32[1024,128]{1,0:T(8,128)S(1)} %get-tuple-element.104.grad_ref, bf16[1024,128]{1,0:T(8,128)(2,1)S(1)} %bitcast.61, bf16[128,128]{1,0:T(8,128)(2,1)S(1)} %collective-permute-done.8.a_ref, bf16[128,128]{1,0:T(8,128)(2,1)S(1)} %collective-permute-done.9.b_ref, ...), custom_call_target="tpu_custom_call" | custom-call | flops 12845056 | bytes 3145728 | tf_op jit(solution)/shard_map/pallas_call | solution.py:658
  64.3 5.7 %collective-permute-done.11.d_ref = bf16[128,128]{1,0:T(8,128)(2,1)S(1)} collective-permute-done((bf16[128,128]{1,0:T(8,128)(2,1)S(1)}, bf16[128,128]{1,0:T(8,128)(2,1)S(1)}, u32[]{:S(2)}, u32[]{:S(2)}) %collective-permute-start.11) | collective-permute-done | bytes 32800 | tf_op jit(solution)/shard_map/ppermute | solution.py:571
  70.0 3.1 %shard_map.221 = (f32[1024,128]{1,0:T(8,128)S(1)}, f32[1024,128]{1,0:T(8,128)S(1)}, bf16[4,128,128]{2,1,0:T(8,128)(2,1)S(1)}, bf16[1024,128]{1,0:T(8,128)(2,1)S(1)}, bf16[16,128]{1,0:T(8,128)(2,1)S(1)}) custom-call(s32[1]{0:T(128)} %bitcast.here_ref, f32[1024,128]{1,0:T(8,128)S(1)} %get-tuple-element.122.standard_ref, ...), custom_call_target="tpu_custom_call" | custom-call | tf_op jit(solution)/shard_map/pallas_call | solution.py:658
  73.1 2.0 %shard_map.222 = (bf16[1152,128]{1,0:T(8,128)(2,1)S(1)}, bf16[1152,128]{1,0:T(8,128)(2,1)S(1)}) custom-call(s32[1]{0:T(128)} %bitcast.23.core_ref, f32[32,48,128]{2,1,0:T(8,128)S(1)} %get-tuple-element.89.inside_ref.pad_inside_ref, f32[6,48,128]{2,1,0:T(8,128)S(1)} %get-tuple-element.108.pad_rims_ref, f32[1024,128]{1,0:T(8,128)S(1)} %get-tuple-element.131.grad_ref, ...), custom_call_target="tpu_custom_call" | custom-call | tf_op jit(solution)/shard_map/pallas_call | solution.py:658
  75.1 1.6 %collective-permute-done.12 = bf16[1152,128]{1,0:T(8,128)(2,1)S(1)} collective-permute-done((bf16[1152,128]{1,0:T(8,128)(2,1)S(1)}, bf16[1152,128]{1,0:T(8,128)(2,1)S(1)}, u32[]{:S(2)}, u32[]{:S(2)}) %collective-permute-start.12) | collective-permute-done | bytes 294944 | tf_op jit(solution)/shard_map/ppermute | solution.py:589
  76.7 0.8 add_convert_fusion
  77.5 4.8 %all-to-all-start = ((bf16[16,72,128]{2,1,0:T(8,128)(2,1)}), bf16[16,72,128]{2,1,0:T(8,128)(2,1)S(1)}, u32[]{:S(2)}, u32[]{:S(2)}) async-start(bf16[16,72,128]{2,1,0:T(8,128)(2,1)} %bitcast.28), calls=%async_computation | async-start | bytes 589824 | tf_op jit(solution)/shard_map/all_to_all | solution.py:594
  82.2 5.7 %collective-permute-start.14 = (bf16[128,128]{1,0:T(8,128)(2,1)S(1)}, bf16[128,128]{1,0:T(8,128)(2,1)S(1)}, u32[]{:S(2)}, u32[]{:S(2)}) collective-permute-start(bf16[128,128]{1,0:T(8,128)(2,1)S(1)} %get-tuple-element.161), channel_id=1, source_target_pairs={{2,4},{6,8},{10,12},{14,16},{18,20},{22,24},{26,28},{30,32},{34,36... | collective-permute-start | bytes 98312 | tf_op jit(solution)/shard_map/ppermute | solution.py:571
  87.9 2.6 %all-to-all-done = bf16[16,72,128]{2,1,0:T(8,128)(2,1)S(1)} async-done(((bf16[16,72,128]{2,1,0:T(8,128)(2,1)}), bf16[16,72,128]{2,1,0:T(8,128)(2,1)S(1)}, u32[]{:S(2)}, u32[]{:S(2)}) %all-to-all-start) | async-done | bytes 294944 | tf_op jit(solution)/shard_map/all_to_all | solution.py:594
  90.6 0.8 collective-permute-done.14.b_ref
  91.4 0.7 broadcast_in_dim.32
  92.1 3.4 %all-to-all-start.1 = ((bf16[8,72,128]{2,1,0:T(8,128)(2,1)}), bf16[8,72,128]{2,1,0:T(8,128)(2,1)S(1)}, u32[]{:S(2)}, u32[]{:S(2)}) async-start(bf16[8,72,128]{2,1,0:T(8,128)(2,1)} %broadcast_in_dim.32), calls=%async_computation.1 | async-start | bytes 294912 | tf_op jit(solution)/shard_map/all_to_all | solution.py:601
  95.5 2.9 %collective-permute-start.15 = (bf16[128,128]{1,0:T(8,128)(2,1)S(1)}, bf16[128,128]{1,0:T(8,128)(2,1)S(1)}, u32[]{:S(2)}, u32[]{:S(2)}) collective-permute-start(bf16[128,128]{1,0:T(8,128)(2,1)S(1)} %pad_maximum_fusion.6), channel_id=1, source_target_pairs={{0,8},{2,10},{4,12},{6,14},{16,24},{18,26},{20,28},{22,30},{32,40}... | collective-permute-start | bytes 98312 | tf_op jit(solution)/shard_map/ppermute | solution.py:571
  98.4 6.0 %all-to-all-done.1 = bf16[8,72,128]{2,1,0:T(8,128)(2,1)S(1)} async-done(((bf16[8,72,128]{2,1,0:T(8,128)(2,1)}), bf16[8,72,128]{2,1,0:T(8,128)(2,1)S(1)}, u32[]{:S(2)}, u32[]{:S(2)}) %all-to-all-start.1) | async-done | bytes 147488 | tf_op jit(solution)/shard_map/all_to_all | solution.py:601
  104.5 0.8 broadcast_in_dim.33
  105.2 5.2 %all-to-all-start.2 = ((bf16[16,72,128]{2,1,0:T(8,128)(2,1)}), bf16[16,72,128]{2,1,0:T(8,128)(2,1)S(1)}, u32[]{:S(2)}, u32[]{:S(2)}) async-start(bf16[16,72,128]{2,1,0:T(8,128)(2,1)} %broadcast_in_dim.33), calls=%async_computation.2 | async-start | bytes 589824 | tf_op jit(solution)/shard_map/all_to_all | solution.py:601
  110.4 5.1 %collective-permute-start.16 = (bf16[128,128]{1,0:T(8,128)(2,1)S(1)}, bf16[128,128]{1,0:T(8,128)(2,1)S(1)}, u32[]{:S(2)}, u32[]{:S(2)}) collective-permute-start(bf16[128,128]{1,0:T(8,128)(2,1)S(1)} %pad_maximum_fusion.7), channel_id=1, source_target_pairs={{8,16},{10,18},{12,20},{14,22},{24,32},{26,34},{28,36},{30,38},{40... | collective-permute-start | bytes 98312 | tf_op jit(solution)/shard_map/ppermute | solution.py:571
  115.5 2.7 %shard_map.223.base_ref = f32[1024,128]{1,0:T(8,128)S(1)} custom-call(f32[1024,128]{1,0:T(8,128)S(1)} %get-tuple-element.131.grad_ref, f32[1024,128]{1,0:T(8,128)S(1)} %get-tuple-element.145.upstream_ref, bf16[128,128]{1,0:T(8,128)(2,1)S(1)} %collective-permute-done.13.a_ref, bf16[128,128]{1,0:T(8,128)(2,1)S(1)} %collective-permute-done.14.b_ref, ...), custom_call_target="tpu_custom_call" | custom-call | flops 12845056 | bytes 3145728 | tf_op jit(solution)/shard_map/pallas_call | solution.py:658
  118.3 2.8 %collective-permute-done.16.d_ref = bf16[128,128]{1,0:T(8,128)(2,1)S(1)} collective-permute-done((bf16[128,128]{1,0:T(8,128)(2,1)S(1)}, bf16[128,128]{1,0:T(8,128)(2,1)S(1)}, u32[]{:S(2)}, u32[]{:S(2)}) %collective-permute-start.16) | collective-permute-done | bytes 32800 | tf_op jit(solution)/shard_map/ppermute | solution.py:571
  121.1 1.0 shard_map.224
  122.1 0.6 collective-permute-done.17.other_ref
  122.7 1.2 shard_map.225
  (48 shorter events, 0.3 us)
Async XLA Ops:
  0.6 19.7 %copy-start.1 = (bf16[2,512,128]{2,1,0:T(8,128)(2,1)S(1)}, bf16[2,512,128]{2,1,0:T(8,128)(2,1)}, u32[]{:S(2)}) copy-start(bf16[2,512,128]{2,1,0:T(8,128)(2,1)} %down_ref.11) | copy-start | bytes 786436
  0.7 19.7 %copy-start = (bf16[2,128,512]{2,1,0:T(8,128)(2,1)S(1)}, bf16[2,128,512]{2,1,0:T(8,128)(2,1)}, u32[]{:S(2)}) copy-start(bf16[2,128,512]{2,1,0:T(8,128)(2,1)} %up_ref.11) | copy-start | bytes 786436
  1.4 0.9 copy-start.2
  3.6 11.0 %collective-permute-start.1 = (bf16[128,128]{1,0:T(8,128)(2,1)S(1)}, bf16[128,128]{1,0:T(8,128)(2,1)S(1)}, u32[]{:S(2)}, u32[]{:S(2)}) collective-permute-start(bf16[128,128]{1,0:T(8,128)(2,1)S(1)} %get-tuple-element.173), channel_id=1, source_target_pairs={{2,4},{6,8},{10,12},{14,16},{18,20},{22,24},{26,28},{30,32},{34,36... | collective-permute-start | bytes 98312 | tf_op jit(solution)/shard_map/ppermute | solution.py:571
  13.0 1.6 %collective-permute-start = (bf16[128,128]{1,0:T(8,128)(2,1)S(1)}, bf16[128,128]{1,0:T(8,128)(2,1)S(1)}, u32[]{:S(2)}, u32[]{:S(2)}) collective-permute-start(bf16[128,128]{1,0:T(8,128)(2,1)S(1)} %get-tuple-element.174), channel_id=1, source_target_pairs={{0,2},{4,6},{8,10},{12,14},{16,18},{20,22},{24,26},{28,30},{32,34}... | collective-permute-start | bytes 98312 | tf_op jit(solution)/shard_map/ppermute | solution.py:571
  14.6 10.3 %collective-permute-start.2 = (bf16[128,128]{1,0:T(8,128)(2,1)S(1)}, bf16[128,128]{1,0:T(8,128)(2,1)S(1)}, u32[]{:S(2)}, u32[]{:S(2)}) collective-permute-start(bf16[128,128]{1,0:T(8,128)(2,1)S(1)} %pad_maximum_fusion), channel_id=1, source_target_pairs={{0,8},{2,10},{4,12},{6,14},{16,24},{18,26},{20,28},{22,30},{32,40}... | collective-permute-start | bytes 98312 | tf_op jit(solution)/shard_map/ppermute | solution.py:571
  14.7 10.6 %collective-permute-start.3 = (bf16[128,128]{1,0:T(8,128)(2,1)S(1)}, bf16[128,128]{1,0:T(8,128)(2,1)S(1)}, u32[]{:S(2)}, u32[]{:S(2)}) collective-permute-start(bf16[128,128]{1,0:T(8,128)(2,1)S(1)} %pad_maximum_fusion.1), channel_id=1, source_target_pairs={{8,16},{10,18},{12,20},{14,22},{24,32},{26,34},{28,36},{30,38},{40... | collective-permute-start | bytes 98312 | tf_op jit(solution)/shard_map/ppermute | solution.py:571
  20.4 1.0 copy-start.3
  21.3 15.5 %copy-start.4 = (bf16[1,1,32,32,128]{4,3,2,1,0:T(8,128)(2,1)S(1)}, bf16[1,1,32,32,128]{4,3,2,1,0:T(8,128)(2,1)}, u32[]{:S(2)}) copy-start(bf16[1,1,32,32,128]{4,3,2,1,0:T(8,128)(2,1)} %param.14) | copy-start | bytes 786436
  26.9 9.2 %collective-permute-start.5 = (bf16[128,128]{1,0:T(8,128)(2,1)S(1)}, bf16[128,128]{1,0:T(8,128)(2,1)S(1)}, u32[]{:S(2)}, u32[]{:S(2)}) collective-permute-start(bf16[128,128]{1,0:T(8,128)(2,1)S(1)} %get-tuple-element.169), channel_id=1, source_target_pairs={{2,4},{6,8},{10,12},{14,16},{18,20},{22,24},{26,28},{30,32},{34,36... | collective-permute-start | bytes 98312 | tf_op jit(solution)/shard_map/ppermute | solution.py:571
  33.3 2.8 %collective-permute-start.4 = (bf16[128,128]{1,0:T(8,128)(2,1)S(1)}, bf16[128,128]{1,0:T(8,128)(2,1)S(1)}, u32[]{:S(2)}, u32[]{:S(2)}) collective-permute-start(bf16[128,128]{1,0:T(8,128)(2,1)S(1)} %get-tuple-element.170), channel_id=1, source_target_pairs={{0,2},{4,6},{8,10},{12,14},{16,18},{20,22},{24,26},{28,30},{32,34}... | collective-permute-start | bytes 98312 | tf_op jit(solution)/shard_map/ppermute | solution.py:571
  36.1 5.0 %collective-permute-start.6 = (bf16[128,128]{1,0:T(8,128)(2,1)S(1)}, bf16[128,128]{1,0:T(8,128)(2,1)S(1)}, u32[]{:S(2)}, u32[]{:S(2)}) collective-permute-start(bf16[128,128]{1,0:T(8,128)(2,1)S(1)} %pad_maximum_fusion.2), channel_id=1, source_target_pairs={{0,8},{2,10},{4,12},{6,14},{16,24},{18,26},{20,28},{22,30},{32,40}... | collective-permute-start | bytes 98312 | tf_op jit(solution)/shard_map/ppermute | solution.py:571
  36.2 10.8 %collective-permute-start.7 = (bf16[128,128]{1,0:T(8,128)(2,1)S(1)}, bf16[128,128]{1,0:T(8,128)(2,1)S(1)}, u32[]{:S(2)}, u32[]{:S(2)}) collective-permute-start(bf16[128,128]{1,0:T(8,128)(2,1)S(1)} %pad_maximum_fusion.3), channel_id=1, source_target_pairs={{8,16},{10,18},{12,20},{14,22},{24,32},{26,34},{28,36},{30,38},{40... | collective-permute-start | bytes 98312 | tf_op jit(solution)/shard_map/ppermute | solution.py:571
  49.9 9.2 %collective-permute-start.9 = (bf16[128,128]{1,0:T(8,128)(2,1)S(1)}, bf16[128,128]{1,0:T(8,128)(2,1)S(1)}, u32[]{:S(2)}, u32[]{:S(2)}) collective-permute-start(bf16[128,128]{1,0:T(8,128)(2,1)S(1)} %get-tuple-element.165), channel_id=1, source_target_pairs={{2,4},{6,8},{10,12},{14,16},{18,20},{22,24},{26,28},{30,32},{34,36... | collective-permute-start | bytes 98312 | tf_op jit(solution)/shard_map/ppermute | solution.py:571
  55.1 3.9 %collective-permute-start.8 = (bf16[128,128]{1,0:T(8,128)(2,1)S(1)}, bf16[128,128]{1,0:T(8,128)(2,1)S(1)}, u32[]{:S(2)}, u32[]{:S(2)}) collective-permute-start(bf16[128,128]{1,0:T(8,128)(2,1)S(1)} %get-tuple-element.166), channel_id=1, source_target_pairs={{0,2},{4,6},{8,10},{12,14},{16,18},{20,22},{24,26},{28,30},{32,34}... | collective-permute-start | bytes 98312 | tf_op jit(solution)/shard_map/ppermute | solution.py:571
  59.0 5.3 %collective-permute-start.10 = (bf16[128,128]{1,0:T(8,128)(2,1)S(1)}, bf16[128,128]{1,0:T(8,128)(2,1)S(1)}, u32[]{:S(2)}, u32[]{:S(2)}) collective-permute-start(bf16[128,128]{1,0:T(8,128)(2,1)S(1)} %pad_maximum_fusion.4), channel_id=1, source_target_pairs={{0,8},{2,10},{4,12},{6,14},{16,24},{18,26},{20,28},{22,30},{32,40}... | collective-permute-start | bytes 98312 | tf_op jit(solution)/shard_map/ppermute | solution.py:571
  59.1 10.8 %collective-permute-start.11 = (bf16[128,128]{1,0:T(8,128)(2,1)S(1)}, bf16[128,128]{1,0:T(8,128)(2,1)S(1)}, u32[]{:S(2)}, u32[]{:S(2)}) collective-permute-start(bf16[128,128]{1,0:T(8,128)(2,1)S(1)} %pad_maximum_fusion.5), channel_id=1, source_target_pairs={{8,16},{10,18},{12,20},{14,22},{24,32},{26,34},{28,36},{30,38},{40... | collective-permute-start | bytes 98312 | tf_op jit(solution)/shard_map/ppermute | solution.py:571
  75.0 1.7 %collective-permute-start.12 = (bf16[1152,128]{1,0:T(8,128)(2,1)S(1)}, bf16[1152,128]{1,0:T(8,128)(2,1)S(1)}, u32[]{:S(2)}, u32[]{:S(2)}) collective-permute-start(bf16[1152,128]{1,0:T(8,128)(2,1)S(1)} %get-tuple-element.138), channel_id=1, source_target_pairs={{0,2},{2,0},{1,3},{3,1},{4,6},{6,4},{5,7},{7,5},{8,10},{10,8},{9,1... | collective-permute-start | bytes 884744 | tf_op jit(solution)/shard_map/ppermute | solution.py:589
  77.5 13.1 %all-to-all-start = ((bf16[16,72,128]{2,1,0:T(8,128)(2,1)}), bf16[16,72,128]{2,1,0:T(8,128)(2,1)S(1)}, u32[]{:S(2)}, u32[]{:S(2)}) async-start(bf16[16,72,128]{2,1,0:T(8,128)(2,1)} %bitcast.28), calls=%async_computation | async-start | bytes 589824 | tf_op jit(solution)/shard_map/all_to_all | solution.py:594
  82.2 9.2 %collective-permute-start.14 = (bf16[128,128]{1,0:T(8,128)(2,1)S(1)}, bf16[128,128]{1,0:T(8,128)(2,1)S(1)}, u32[]{:S(2)}, u32[]{:S(2)}) collective-permute-start(bf16[128,128]{1,0:T(8,128)(2,1)S(1)} %get-tuple-element.161), channel_id=1, source_target_pairs={{2,4},{6,8},{10,12},{14,16},{18,20},{22,24},{26,28},{30,32},{34,36... | collective-permute-start | bytes 98312 | tf_op jit(solution)/shard_map/ppermute | solution.py:571
  87.9 3.5 %collective-permute-start.13 = (bf16[128,128]{1,0:T(8,128)(2,1)S(1)}, bf16[128,128]{1,0:T(8,128)(2,1)S(1)}, u32[]{:S(2)}, u32[]{:S(2)}) collective-permute-start(bf16[128,128]{1,0:T(8,128)(2,1)S(1)} %get-tuple-element.162), channel_id=1, source_target_pairs={{0,2},{4,6},{8,10},{12,14},{16,18},{20,22},{24,26},{28,30},{32,34}... | collective-permute-start | bytes 98312 | tf_op jit(solution)/shard_map/ppermute | solution.py:571
  92.1 12.4 %all-to-all-start.1 = ((bf16[8,72,128]{2,1,0:T(8,128)(2,1)}), bf16[8,72,128]{2,1,0:T(8,128)(2,1)S(1)}, u32[]{:S(2)}, u32[]{:S(2)}) async-start(bf16[8,72,128]{2,1,0:T(8,128)(2,1)} %broadcast_in_dim.32), calls=%async_computation.1 | async-start | bytes 294912 | tf_op jit(solution)/shard_map/all_to_all | solution.py:601
  95.5 9.0 %collective-permute-start.15 = (bf16[128,128]{1,0:T(8,128)(2,1)S(1)}, bf16[128,128]{1,0:T(8,128)(2,1)S(1)}, u32[]{:S(2)}, u32[]{:S(2)}) collective-permute-start(bf16[128,128]{1,0:T(8,128)(2,1)S(1)} %pad_maximum_fusion.6), channel_id=1, source_target_pairs={{0,8},{2,10},{4,12},{6,14},{16,24},{18,26},{20,28},{22,30},{32,40}... | collective-permute-start | bytes 98312 | tf_op jit(solution)/shard_map/ppermute | solution.py:571
  105.2 15.8 %all-to-all-start.2 = ((bf16[16,72,128]{2,1,0:T(8,128)(2,1)}), bf16[16,72,128]{2,1,0:T(8,128)(2,1)S(1)}, u32[]{:S(2)}, u32[]{:S(2)}) async-start(bf16[16,72,128]{2,1,0:T(8,128)(2,1)} %broadcast_in_dim.33), calls=%async_computation.2 | async-start | bytes 589824 | tf_op jit(solution)/shard_map/all_to_all | solution.py:601
  110.4 10.6 %collective-permute-start.16 = (bf16[128,128]{1,0:T(8,128)(2,1)S(1)}, bf16[128,128]{1,0:T(8,128)(2,1)S(1)}, u32[]{:S(2)}, u32[]{:S(2)}) collective-permute-start(bf16[128,128]{1,0:T(8,128)(2,1)S(1)} %pad_maximum_fusion.7), channel_id=1, source_target_pairs={{8,16},{10,18},{12,20},{14,22},{24,32},{26,34},{28,36},{30,38},{40... | collective-permute-start | bytes 98312 | tf_op jit(solution)/shard_map/ppermute | solution.py:571
  121.1 1.6 %collective-permute-start.17 = (bf16[1152,128]{1,0:T(8,128)(2,1)S(1)}, bf16[1152,128]{1,0:T(8,128)(2,1)S(1)}, u32[]{:S(2)}, u32[]{:S(2)}) collective-permute-start(bf16[1152,128]{1,0:T(8,128)(2,1)S(1)} %bitcast.62), channel_id=1, source_target_pairs={{0,2},{2,0},{1,3},{3,1},{4,6},{6,4},{5,7},{7,5},{8,10},{10,8},{9,1... | collective-permute-start | bytes 884744 | tf_op jit(solution)/shard_map/ppermute | solution.py:589

commit v4 on v3

--- a/solution.py
+++ b/solution.py
@@ -209,7 +209,7 @@
             out_ref[pl.ds(pl.multiple_of(index * 128 + out * SIZE, SIZE), SIZE), :] = totals[out]
         return carry
 
-    lax.fori_loop(first, last, group, 0)
+    lax.fori_loop(first, last, group, 0, unroll=2 if last - first > 1 else True)
 
 
 def kernel_sums(padded_ref, grad_ref, sums_ref):
@@ -233,7 +233,7 @@
                 sums_ref[at : at + 8, :] += totals[row_tap]
         return carry
 
-    lax.fori_loop(0, SIZE // 4, group, 0)
+    lax.fori_loop(0, SIZE // 4, group, 0, unroll=2)
 
 
 def row_rim(grown_ref, kernel_ref, top):
@@ -263,7 +263,7 @@
             out_ref[pl.ds(pl.multiple_of(index * 64 + out * 8, 8), 8), :] = totals[out]
         return carry
 
-    lax.fori_loop(0, SIZE // 8, group, 0)
+    lax.fori_loop(0, SIZE // 8, group, 0, unroll=True)
 
 
 def send_rims(here, grown_ref, kernel, rim_ref, sent_ref):

time: 126 us -> 125 us (level)
  Pallas kernels: 30.7 us -> 28.8 us
  waiting for transfers between devices: 31.4 us -> 32.8 us
    pallas_call x14, Pallas kernels: 30.7 us -> 28.8 us  [call(): pl.pallas_call(kernel, out_shape=shaped(*shapes), in_specs=specs, out_spe...]
    ppermute x16, waiting for transfers between devices: 20.6 us -> 22 us  [swapped_tiles(): lax.ppermute(value, TILE_AXES, pairs + [(target, source) for source, targ...]
  transfers between devices with their start and end apart: 21 -> 21, of which waited for: 12 -> 13; matrix products, arithmetic and copies ran while one was open for 1% -> 1% of each run, Pallas kernels for 15% -> 14%
where the time goes in v4:
time: 125 us; the launch traced here: 123 us
  starting transfers between devices  54.6 us (44%)
  waiting for transfers between devices  32.8 us (26%)
  Pallas kernels  28.8 us (23%)
  local copies, waits for them, and re-layouts  3.4 us (3%)
  other arithmetic  2.57 us (2%)
    ppermute x16, starting transfers between devices, swapped_tiles(): lax.ppermute(value, TILE_AXES, pairs + [(target, source) for source, targ...  41.2 us
    pallas_call x14, Pallas kernels, call(): pl.pallas_call(kernel, out_shape=shaped(*shapes), in_specs=specs, out_spe...  28.8 us
    ppermute x16, waiting for transfers between devices, swapped_tiles(): lax.ppermute(value, TILE_AXES, pairs + [(target, source) for source, targ...  22 us
    all_to_all x2, starting transfers between devices, gathered(): return lax.all_to_all(copies, axes, 0, 0, tiled=True)  8.6 us
    all_to_all x2, waiting for transfers between devices, gathered(): return lax.all_to_all(copies, axes, 0, 0, tiled=True)  6.04 us
    all_to_all x1, starting transfers between devices, summed_apart(): lax.all_to_all(value, axes, 0, 0, tiled=True).reshape(count, -1, WIDTH)  4.76 us
    all_to_all x1, waiting for transfers between devices, summed_apart(): lax.all_to_all(value, axes, 0, 0, tiled=True).reshape(count, -1, WIDTH)  2.63 us
  transfers between devices with their start and end apart: 21, of which 13 were waited for; matrix products, arithmetic and copies ran while one was open for 1% of the time, Pallas kernels for 14%

profile of v4, /device:TPU:2, one launch (start us, length us, event | category | flops | bytes accessed | tf_op | source)
XLA Modules:
  0.0 123.1 jit_solution(13124180152021057705)
XLA Ops:
  0.7 0.8 pad_add_fusion.1.codes_ref
  1.4 0.9 copy-done.2
  2.4 1.2 shard_map.212
  3.6 9.4 %collective-permute-start.1 = (bf16[128,128]{1,0:T(8,128)(2,1)S(1)}, bf16[128,128]{1,0:T(8,128)(2,1)S(1)}, u32[]{:S(2)}, u32[]{:S(2)}) collective-permute-start(bf16[128,128]{1,0:T(8,128)(2,1)S(1)} %get-tuple-element.173), channel_id=1, source_target_pairs={{2,4},{6,8},{10,12},{14,16},{18,20},{22,24},{26,28},{30,32},{34,36... | collective-permute-start | bytes 98312 | tf_op jit(solution)/shard_map/ppermute | solution.py:571
  13.0 0.9 pad_add_fusion.params_ref
  13.9 0.7 collective-permute-done.1.b_ref
  14.6 0.1 collective-permute-start.2
  14.7 5.4 %collective-permute-start.3 = (bf16[128,128]{1,0:T(8,128)(2,1)S(1)}, bf16[128,128]{1,0:T(8,128)(2,1)S(1)}, u32[]{:S(2)}, u32[]{:S(2)}) collective-permute-start(bf16[128,128]{1,0:T(8,128)(2,1)S(1)} %pad_maximum_fusion.1), channel_id=1, source_target_pairs={{8,16},{10,18},{12,20},{14,22},{24,32},{26,34},{28,36},{30,38},{40... | collective-permute-start | bytes 98312 | tf_op jit(solution)/shard_map/ppermute | solution.py:571
  20.1 0.3 shard_map.215.scatter_ref
  20.4 0.9 copy-done.3
  21.3 3.4 %shard_map.213 = (bf16[768,128]{1,0:T(8,128)(2,1)S(1)}, f32[768,128]{1,0:T(8,128)S(1)}, f32[32,48,128]{2,1,0:T(8,128)S(1)}) custom-call(s32[1]{0:T(128)} %bitcast.here_ref, bf16[1024,128]{1,0:T(8,128)(2,1)S(1)} %bitcast.57, bf16[128,128]{1,0:T(8,128)(2,1)S(1)} %collective-permute-done.a_ref, bf16[128,128]{1,0:T(8,128)(2,1)S(1)} %collective-permute-done.1.b_ref, ...), custom_call_target="tpu_custom_call" | custom-call | flops 12845056 | bytes 3145728 | tf_op jit(solution)/shard_map/pallas_call | solution.py:658
  24.7 0.6 collective-permute-done.3.d_ref
  25.3 1.6 %shard_map.214 = (bf16[1024,128]{1,0:T(8,128)(2,1)S(1)}, f32[256,128]{1,0:T(8,128)S(1)}, f32[6,48,128]{2,1,0:T(8,128)S(1)}, bf16[4,128,128]{2,1,0:T(8,128)(2,1)S(1)}) custom-call(s32[1]{0:T(128)} %bitcast.here_ref, bf16[1024,128]{1,0:T(8,128)(2,1)S(1)} %bitcast.58, bf16[128,128]{1,0:T(8,128)(2,1)S(1)} %collective-permute-done.2.c_ref, ...), custom_call_target="tpu_custom_call" | custom-call | tf_op jit(solution)/shard_map/pallas_call | solution.py:658
  26.9 6.4 %collective-permute-start.5 = (bf16[128,128]{1,0:T(8,128)(2,1)S(1)}, bf16[128,128]{1,0:T(8,128)(2,1)S(1)}, u32[]{:S(2)}, u32[]{:S(2)}) collective-permute-start(bf16[128,128]{1,0:T(8,128)(2,1)S(1)} %get-tuple-element.169), channel_id=1, source_target_pairs={{2,4},{6,8},{10,12},{14,16},{18,20},{22,24},{26,28},{30,32},{34,36... | collective-permute-start | bytes 98312 | tf_op jit(solution)/shard_map/ppermute | solution.py:571
  33.3 2.7 %collective-permute-done.5.b_ref = bf16[128,128]{1,0:T(8,128)(2,1)S(1)} collective-permute-done((bf16[128,128]{1,0:T(8,128)(2,1)S(1)}, bf16[128,128]{1,0:T(8,128)(2,1)S(1)}, u32[]{:S(2)}, u32[]{:S(2)}) %collective-permute-start.5) | collective-permute-done | bytes 32800 | tf_op jit(solution)/shard_map/ppermute | solution.py:571
  36.1 0.1 collective-permute-start.6
  36.2 0.5 collective-permute-start.7
  36.7 4.0 %shard_map.216 = (bf16[768,128]{1,0:T(8,128)(2,1)S(1)}, f32[32,48,128]{2,1,0:T(8,128)S(1)}, f32[768,128]{1,0:T(8,128)S(1)}, f32[128,512]{1,0:T(8,128)S(1)}, f32[...) custom-call(s32[1]{0:T(128)} %bitcast.here_ref, ...), custom_call_target="tpu_custom_call" | custom-call | flops 12845056 | bytes 3145728 | tf_op jit(solution)/shard_map/pallas_call | solution.py:658
  40.7 0.3 collective-permute-done.6.c_ref
  41.0 6.0 %collective-permute-done.7.d_ref = bf16[128,128]{1,0:T(8,128)(2,1)S(1)} collective-permute-done((bf16[128,128]{1,0:T(8,128)(2,1)S(1)}, bf16[128,128]{1,0:T(8,128)(2,1)S(1)}, u32[]{:S(2)}, u32[]{:S(2)}) %collective-permute-start.7) | collective-permute-done | bytes 32800 | tf_op jit(solution)/shard_map/ppermute | solution.py:571
  47.0 2.4 %shard_map.217 = (bf16[256,128]{1,0:T(8,128)(2,1)S(1)}, f32[6,48,128]{2,1,0:T(8,128)S(1)}, f32[1024,128]{1,0:T(8,128)S(1)}, bf16[4,128,128]{2,1,0:T(8,128)(2,1)S...) custom-call(s32[1]{0:T(128)} %bitcast.here_ref, bf16[1024,128]{1,0:T(8,128)(2,1)S(1)} %get-tuple-element.92.field_ref, ...), custom_call_target="tpu_custom_call" | custom-call | tf_op jit(solution)/shard_map/pallas_call | solution.py:658
  49.4 5.2 %collective-permute-start.9 = (bf16[128,128]{1,0:T(8,128)(2,1)S(1)}, bf16[128,128]{1,0:T(8,128)(2,1)S(1)}, u32[]{:S(2)}, u32[]{:S(2)}) collective-permute-start(bf16[128,128]{1,0:T(8,128)(2,1)S(1)} %get-tuple-element.165), channel_id=1, source_target_pairs={{2,4},{6,8},{10,12},{14,16},{18,20},{22,24},{26,28},{30,32},{34,36... | collective-permute-start | bytes 98312 | tf_op jit(solution)/shard_map/ppermute | solution.py:571
  54.7 2.1 %shard_map.218 = (bf16[64,128]{1,0:T(8,128)(2,1)S(1)}, bf16[1024,128]{1,0:T(8,128)(2,1)}) custom-call(f32[32,48,128]{2,1,0:T(8,128)S(1)} %get-tuple-element.97.inside_ref.pad_inside_ref, f32[6,48,128]{2,1,0:T(8,128)S(1)} %get-tuple-element.103.pad_rims_ref, f32[1024,128]{1,0:T(8,128)S(1)} %get-tuple-element.104.grad_ref, ...), custom_call_target="tpu_custom_call" | custom-call | flops 12845056 | bytes 3145728 | tf_op jit(solution)/shard_map/pallas_call | solution.py:658
  56.7 1.8 %collective-permute-done.9.b_ref = bf16[128,128]{1,0:T(8,128)(2,1)S(1)} collective-permute-done((bf16[128,128]{1,0:T(8,128)(2,1)S(1)}, bf16[128,128]{1,0:T(8,128)(2,1)S(1)}, u32[]{:S(2)}, u32[]{:S(2)}) %collective-permute-start.9) | collective-permute-done | bytes 32800 | tf_op jit(solution)/shard_map/ppermute | solution.py:571
  58.7 0.3 collective-permute-start.11
  59.0 2.1 %shard_map.220 = (f32[1024,128]{1,0:T(8,128)S(1)}, f32[1024,128]{1,0:T(8,128)S(1)}, bf16[1024,128]{1,0:T(8,128)(2,1)S(1)}, bf16[1024,512]{1,0:T(8,128)(2,1)S(1)}...) custom-call(f32[768,128]{1,0:T(8,128)S(1)} %get-tuple-element.114.conv_ref, ...), custom_call_target="tpu_custom_call" | custom-call | flops 12845056 | bytes 3145728 | tf_op jit(solution)/shard_map/pallas_call | solution.py:658
  61.1 2.5 %shard_map.219.base_ref = f32[1024,128]{1,0:T(8,128)S(1)} custom-call(f32[1024,128]{1,0:T(8,128)S(1)} %get-tuple-element.104.grad_ref, bf16[1024,128]{1,0:T(8,128)(2,1)S(1)} %bitcast.61, bf16[128,128]{1,0:T(8,128)(2,1)S(1)} %collective-permute-done.8.a_ref, bf16[128,128]{1,0:T(8,128)(2,1)S(1)} %collective-permute-done.9.b_ref, ...), custom_call_target="tpu_custom_call" | custom-call | flops 12845056 | bytes 3145728 | tf_op jit(solution)/shard_map/pallas_call | solution.py:658
  63.6 6.0 %collective-permute-done.11.d_ref = bf16[128,128]{1,0:T(8,128)(2,1)S(1)} collective-permute-done((bf16[128,128]{1,0:T(8,128)(2,1)S(1)}, bf16[128,128]{1,0:T(8,128)(2,1)S(1)}, u32[]{:S(2)}, u32[]{:S(2)}) %collective-permute-start.11) | collective-permute-done | bytes 32800 | tf_op jit(solution)/shard_map/ppermute | solution.py:571
  69.5 2.7 %shard_map.221 = (f32[1024,128]{1,0:T(8,128)S(1)}, f32[1024,128]{1,0:T(8,128)S(1)}, bf16[4,128,128]{2,1,0:T(8,128)(2,1)S(1)}, bf16[1024,128]{1,0:T(8,128)(2,1)S(1)}, bf16[16,128]{1,0:T(8,128)(2,1)S(1)}) custom-call(s32[1]{0:T(128)} %bitcast.here_ref, f32[1024,128]{1,0:T(8,128)S(1)} %get-tuple-element.122.standard_ref, ...), custom_call_target="tpu_custom_call" | custom-call | tf_op jit(solution)/shard_map/pallas_call | solution.py:658
  72.3 1.9 %shard_map.222 = (bf16[1152,128]{1,0:T(8,128)(2,1)S(1)}, bf16[1152,128]{1,0:T(8,128)(2,1)S(1)}) custom-call(s32[1]{0:T(128)} %bitcast.23.core_ref, f32[32,48,128]{2,1,0:T(8,128)S(1)} %get-tuple-element.89.inside_ref.pad_inside_ref, f32[6,48,128]{2,1,0:T(8,128)S(1)} %get-tuple-element.108.pad_rims_ref, f32[1024,128]{1,0:T(8,128)S(1)} %get-tuple-element.131.grad_ref, ...), custom_call_target="tpu_custom_call" | custom-call | tf_op jit(solution)/shard_map/pallas_call | solution.py:658
  74.3 1.6 %collective-permute-done.12 = bf16[1152,128]{1,0:T(8,128)(2,1)S(1)} collective-permute-done((bf16[1152,128]{1,0:T(8,128)(2,1)S(1)}, bf16[1152,128]{1,0:T(8,128)(2,1)S(1)}, u32[]{:S(2)}, u32[]{:S(2)}) %collective-permute-start.12) | collective-permute-done | bytes 294944 | tf_op jit(solution)/shard_map/ppermute | solution.py:589
  75.9 0.8 add_convert_fusion
  76.7 4.8 %all-to-all-start = ((bf16[16,72,128]{2,1,0:T(8,128)(2,1)}), bf16[16,72,128]{2,1,0:T(8,128)(2,1)S(1)}, u32[]{:S(2)}, u32[]{:S(2)}) async-start(bf16[16,72,128]{2,1,0:T(8,128)(2,1)} %bitcast.28), calls=%async_computation | async-start | bytes 589824 | tf_op jit(solution)/shard_map/all_to_all | solution.py:594
  81.4 5.7 %collective-permute-start.14 = (bf16[128,128]{1,0:T(8,128)(2,1)S(1)}, bf16[128,128]{1,0:T(8,128)(2,1)S(1)}, u32[]{:S(2)}, u32[]{:S(2)}) collective-permute-start(bf16[128,128]{1,0:T(8,128)(2,1)S(1)} %get-tuple-element.161), channel_id=1, source_target_pairs={{2,4},{6,8},{10,12},{14,16},{18,20},{22,24},{26,28},{30,32},{34,36... | collective-permute-start | bytes 98312 | tf_op jit(solution)/shard_map/ppermute | solution.py:571
  87.1 2.6 %all-to-all-done = bf16[16,72,128]{2,1,0:T(8,128)(2,1)S(1)} async-done(((bf16[16,72,128]{2,1,0:T(8,128)(2,1)}), bf16[16,72,128]{2,1,0:T(8,128)(2,1)S(1)}, u32[]{:S(2)}, u32[]{:S(2)}) %all-to-all-start) | async-done | bytes 294944 | tf_op jit(solution)/shard_map/all_to_all | solution.py:594
  89.8 0.8 collective-permute-done.14.b_ref
  90.6 0.7 broadcast_in_dim.32
  91.3 3.4 %all-to-all-start.1 = ((bf16[8,72,128]{2,1,0:T(8,128)(2,1)}), bf16[8,72,128]{2,1,0:T(8,128)(2,1)S(1)}, u32[]{:S(2)}, u32[]{:S(2)}) async-start(bf16[8,72,128]{2,1,0:T(8,128)(2,1)} %broadcast_in_dim.32), calls=%async_computation.1 | async-start | bytes 294912 | tf_op jit(solution)/shard_map/all_to_all | solution.py:601
  94.7 2.9 %collective-permute-start.15 = (bf16[128,128]{1,0:T(8,128)(2,1)S(1)}, bf16[128,128]{1,0:T(8,128)(2,1)S(1)}, u32[]{:S(2)}, u32[]{:S(2)}) collective-permute-start(bf16[128,128]{1,0:T(8,128)(2,1)S(1)} %pad_maximum_fusion.6), channel_id=1, source_target_pairs={{0,8},{2,10},{4,12},{6,14},{16,24},{18,26},{20,28},{22,30},{32,40}... | collective-permute-start | bytes 98312 | tf_op jit(solution)/shard_map/ppermute | solution.py:571
  97.6 6.0 %all-to-all-done.1 = bf16[8,72,128]{2,1,0:T(8,128)(2,1)S(1)} async-done(((bf16[8,72,128]{2,1,0:T(8,128)(2,1)}), bf16[8,72,128]{2,1,0:T(8,128)(2,1)S(1)}, u32[]{:S(2)}, u32[]{:S(2)}) %all-to-all-start.1) | async-done | bytes 147488 | tf_op jit(solution)/shard_map/all_to_all | solution.py:601
  103.7 0.8 broadcast_in_dim.33
  104.4 5.2 %all-to-all-start.2 = ((bf16[16,72,128]{2,1,0:T(8,128)(2,1)}), bf16[16,72,128]{2,1,0:T(8,128)(2,1)S(1)}, u32[]{:S(2)}, u32[]{:S(2)}) async-start(bf16[16,72,128]{2,1,0:T(8,128)(2,1)} %broadcast_in_dim.33), calls=%async_computation.2 | async-start | bytes 589824 | tf_op jit(solution)/shard_map/all_to_all | solution.py:601
  109.6 5.1 %collective-permute-start.16 = (bf16[128,128]{1,0:T(8,128)(2,1)S(1)}, bf16[128,128]{1,0:T(8,128)(2,1)S(1)}, u32[]{:S(2)}, u32[]{:S(2)}) collective-permute-start(bf16[128,128]{1,0:T(8,128)(2,1)S(1)} %pad_maximum_fusion.7), channel_id=1, source_target_pairs={{8,16},{10,18},{12,20},{14,22},{24,32},{26,34},{28,36},{30,38},{40... | collective-permute-start | bytes 98312 | tf_op jit(solution)/shard_map/ppermute | solution.py:571
  114.7 2.5 %shard_map.223.base_ref = f32[1024,128]{1,0:T(8,128)S(1)} custom-call(f32[1024,128]{1,0:T(8,128)S(1)} %get-tuple-element.131.grad_ref, f32[1024,128]{1,0:T(8,128)S(1)} %get-tuple-element.145.upstream_ref, bf16[128,128]{1,0:T(8,128)(2,1)S(1)} %collective-permute-done.13.a_ref, bf16[128,128]{1,0:T(8,128)(2,1)S(1)} %collective-permute-done.14.b_ref, ...), custom_call_target="tpu_custom_call" | custom-call | flops 12845056 | bytes 3145728 | tf_op jit(solution)/shard_map/pallas_call | solution.py:658
  117.2 3.1 %collective-permute-done.16.d_ref = bf16[128,128]{1,0:T(8,128)(2,1)S(1)} collective-permute-done((bf16[128,128]{1,0:T(8,128)(2,1)S(1)}, bf16[128,128]{1,0:T(8,128)(2,1)S(1)}, u32[]{:S(2)}, u32[]{:S(2)}) %collective-permute-start.16) | collective-permute-done | bytes 32800 | tf_op jit(solution)/shard_map/ppermute | solution.py:571
  120.3 1.0 shard_map.224
  121.3 0.6 collective-permute-done.17.other_ref
  121.8 1.2 shard_map.225
  (48 shorter events, 0.4 us)
Async XLA Ops:
  0.6 19.7 %copy-start.1 = (bf16[2,512,128]{2,1,0:T(8,128)(2,1)S(1)}, bf16[2,512,128]{2,1,0:T(8,128)(2,1)}, u32[]{:S(2)}) copy-start(bf16[2,512,128]{2,1,0:T(8,128)(2,1)} %down_ref.11) | copy-start | bytes 786436
  0.7 19.7 %copy-start = (bf16[2,128,512]{2,1,0:T(8,128)(2,1)S(1)}, bf16[2,128,512]{2,1,0:T(8,128)(2,1)}, u32[]{:S(2)}) copy-start(bf16[2,128,512]{2,1,0:T(8,128)(2,1)} %up_ref.11) | copy-start | bytes 786436
  1.4 0.9 copy-start.2
  3.6 11.0 %collective-permute-start.1 = (bf16[128,128]{1,0:T(8,128)(2,1)S(1)}, bf16[128,128]{1,0:T(8,128)(2,1)S(1)}, u32[]{:S(2)}, u32[]{:S(2)}) collective-permute-start(bf16[128,128]{1,0:T(8,128)(2,1)S(1)} %get-tuple-element.173), channel_id=1, source_target_pairs={{2,4},{6,8},{10,12},{14,16},{18,20},{22,24},{26,28},{30,32},{34,36... | collective-permute-start | bytes 98312 | tf_op jit(solution)/shard_map/ppermute | solution.py:571
  13.0 1.6 %collective-permute-start = (bf16[128,128]{1,0:T(8,128)(2,1)S(1)}, bf16[128,128]{1,0:T(8,128)(2,1)S(1)}, u32[]{:S(2)}, u32[]{:S(2)}) collective-permute-start(bf16[128,128]{1,0:T(8,128)(2,1)S(1)} %get-tuple-element.174), channel_id=1, source_target_pairs={{0,2},{4,6},{8,10},{12,14},{16,18},{20,22},{24,26},{28,30},{32,34}... | collective-permute-start | bytes 98312 | tf_op jit(solution)/shard_map/ppermute | solution.py:571
  14.6 10.1 %collective-permute-start.2 = (bf16[128,128]{1,0:T(8,128)(2,1)S(1)}, bf16[128,128]{1,0:T(8,128)(2,1)S(1)}, u32[]{:S(2)}, u32[]{:S(2)}) collective-permute-start(bf16[128,128]{1,0:T(8,128)(2,1)S(1)} %pad_maximum_fusion), channel_id=1, source_target_pairs={{0,8},{2,10},{4,12},{6,14},{16,24},{18,26},{20,28},{22,30},{32,40}... | collective-permute-start | bytes 98312 | tf_op jit(solution)/shard_map/ppermute | solution.py:571
  14.7 10.6 %collective-permute-start.3 = (bf16[128,128]{1,0:T(8,128)(2,1)S(1)}, bf16[128,128]{1,0:T(8,128)(2,1)S(1)}, u32[]{:S(2)}, u32[]{:S(2)}) collective-permute-start(bf16[128,128]{1,0:T(8,128)(2,1)S(1)} %pad_maximum_fusion.1), channel_id=1, source_target_pairs={{8,16},{10,18},{12,20},{14,22},{24,32},{26,34},{28,36},{30,38},{40... | collective-permute-start | bytes 98312 | tf_op jit(solution)/shard_map/ppermute | solution.py:571
  20.4 1.0 copy-start.3
  21.3 15.3 %copy-start.4 = (bf16[1,1,32,32,128]{4,3,2,1,0:T(8,128)(2,1)S(1)}, bf16[1,1,32,32,128]{4,3,2,1,0:T(8,128)(2,1)}, u32[]{:S(2)}) copy-start(bf16[1,1,32,32,128]{4,3,2,1,0:T(8,128)(2,1)} %param.14) | copy-start | bytes 786436
  26.9 9.2 %collective-permute-start.5 = (bf16[128,128]{1,0:T(8,128)(2,1)S(1)}, bf16[128,128]{1,0:T(8,128)(2,1)S(1)}, u32[]{:S(2)}, u32[]{:S(2)}) collective-permute-start(bf16[128,128]{1,0:T(8,128)(2,1)S(1)} %get-tuple-element.169), channel_id=1, source_target_pairs={{2,4},{6,8},{10,12},{14,16},{18,20},{22,24},{26,28},{30,32},{34,36... | collective-permute-start | bytes 98312 | tf_op jit(solution)/shard_map/ppermute | solution.py:571
  33.3 2.8 %collective-permute-start.4 = (bf16[128,128]{1,0:T(8,128)(2,1)S(1)}, bf16[128,128]{1,0:T(8,128)(2,1)S(1)}, u32[]{:S(2)}, u32[]{:S(2)}) collective-permute-start(bf16[128,128]{1,0:T(8,128)(2,1)S(1)} %get-tuple-element.170), channel_id=1, source_target_pairs={{0,2},{4,6},{8,10},{12,14},{16,18},{20,22},{24,26},{28,30},{32,34}... | collective-permute-start | bytes 98312 | tf_op jit(solution)/shard_map/ppermute | solution.py:571
  36.1 4.9 %collective-permute-start.6 = (bf16[128,128]{1,0:T(8,128)(2,1)S(1)}, bf16[128,128]{1,0:T(8,128)(2,1)S(1)}, u32[]{:S(2)}, u32[]{:S(2)}) collective-permute-start(bf16[128,128]{1,0:T(8,128)(2,1)S(1)} %pad_maximum_fusion.2), channel_id=1, source_target_pairs={{0,8},{2,10},{4,12},{6,14},{16,24},{18,26},{20,28},{22,30},{32,40}... | collective-permute-start | bytes 98312 | tf_op jit(solution)/shard_map/ppermute | solution.py:571
  36.2 10.8 %collective-permute-start.7 = (bf16[128,128]{1,0:T(8,128)(2,1)S(1)}, bf16[128,128]{1,0:T(8,128)(2,1)S(1)}, u32[]{:S(2)}, u32[]{:S(2)}) collective-permute-start(bf16[128,128]{1,0:T(8,128)(2,1)S(1)} %pad_maximum_fusion.3), channel_id=1, source_target_pairs={{8,16},{10,18},{12,20},{14,22},{24,32},{26,34},{28,36},{30,38},{40... | collective-permute-start | bytes 98312 | tf_op jit(solution)/shard_map/ppermute | solution.py:571
  49.4 9.2 %collective-permute-start.9 = (bf16[128,128]{1,0:T(8,128)(2,1)S(1)}, bf16[128,128]{1,0:T(8,128)(2,1)S(1)}, u32[]{:S(2)}, u32[]{:S(2)}) collective-permute-start(bf16[128,128]{1,0:T(8,128)(2,1)S(1)} %get-tuple-element.165), channel_id=1, source_target_pairs={{2,4},{6,8},{10,12},{14,16},{18,20},{22,24},{26,28},{30,32},{34,36... | collective-permute-start | bytes 98312 | tf_op jit(solution)/shard_map/ppermute | solution.py:571
  54.7 3.9 %collective-permute-start.8 = (bf16[128,128]{1,0:T(8,128)(2,1)S(1)}, bf16[128,128]{1,0:T(8,128)(2,1)S(1)}, u32[]{:S(2)}, u32[]{:S(2)}) collective-permute-start(bf16[128,128]{1,0:T(8,128)(2,1)S(1)} %get-tuple-element.166), channel_id=1, source_target_pairs={{0,2},{4,6},{8,10},{12,14},{16,18},{20,22},{24,26},{28,30},{32,34}... | collective-permute-start | bytes 98312 | tf_op jit(solution)/shard_map/ppermute | solution.py:571
  58.6 5.0 %collective-permute-start.10 = (bf16[128,128]{1,0:T(8,128)(2,1)S(1)}, bf16[128,128]{1,0:T(8,128)(2,1)S(1)}, u32[]{:S(2)}, u32[]{:S(2)}) collective-permute-start(bf16[128,128]{1,0:T(8,128)(2,1)S(1)} %pad_maximum_fusion.4), channel_id=1, source_target_pairs={{0,8},{2,10},{4,12},{6,14},{16,24},{18,26},{20,28},{22,30},{32,40}... | collective-permute-start | bytes 98312 | tf_op jit(solution)/shard_map/ppermute | solution.py:571
  58.7 10.8 %collective-permute-start.11 = (bf16[128,128]{1,0:T(8,128)(2,1)S(1)}, bf16[128,128]{1,0:T(8,128)(2,1)S(1)}, u32[]{:S(2)}, u32[]{:S(2)}) collective-permute-start(bf16[128,128]{1,0:T(8,128)(2,1)S(1)} %pad_maximum_fusion.5), channel_id=1, source_target_pairs={{8,16},{10,18},{12,20},{14,22},{24,32},{26,34},{28,36},{30,38},{40... | collective-permute-start | bytes 98312 | tf_op jit(solution)/shard_map/ppermute | solution.py:571
  74.2 1.7 %collective-permute-start.12 = (bf16[1152,128]{1,0:T(8,128)(2,1)S(1)}, bf16[1152,128]{1,0:T(8,128)(2,1)S(1)}, u32[]{:S(2)}, u32[]{:S(2)}) collective-permute-start(bf16[1152,128]{1,0:T(8,128)(2,1)S(1)} %get-tuple-element.138), channel_id=1, source_target_pairs={{0,2},{2,0},{1,3},{3,1},{4,6},{6,4},{5,7},{7,5},{8,10},{10,8},{9,1... | collective-permute-start | bytes 884744 | tf_op jit(solution)/shard_map/ppermute | solution.py:589
  76.7 13.1 %all-to-all-start = ((bf16[16,72,128]{2,1,0:T(8,128)(2,1)}), bf16[16,72,128]{2,1,0:T(8,128)(2,1)S(1)}, u32[]{:S(2)}, u32[]{:S(2)}) async-start(bf16[16,72,128]{2,1,0:T(8,128)(2,1)} %bitcast.28), calls=%async_computation | async-start | bytes 589824 | tf_op jit(solution)/shard_map/all_to_all | solution.py:594
  81.4 9.2 %collective-permute-start.14 = (bf16[128,128]{1,0:T(8,128)(2,1)S(1)}, bf16[128,128]{1,0:T(8,128)(2,1)S(1)}, u32[]{:S(2)}, u32[]{:S(2)}) collective-permute-start(bf16[128,128]{1,0:T(8,128)(2,1)S(1)} %get-tuple-element.161), channel_id=1, source_target_pairs={{2,4},{6,8},{10,12},{14,16},{18,20},{22,24},{26,28},{30,32},{34,36... | collective-permute-start | bytes 98312 | tf_op jit(solution)/shard_map/ppermute | solution.py:571
  87.1 3.5 %collective-permute-start.13 = (bf16[128,128]{1,0:T(8,128)(2,1)S(1)}, bf16[128,128]{1,0:T(8,128)(2,1)S(1)}, u32[]{:S(2)}, u32[]{:S(2)}) collective-permute-start(bf16[128,128]{1,0:T(8,128)(2,1)S(1)} %get-tuple-element.162), channel_id=1, source_target_pairs={{0,2},{4,6},{8,10},{12,14},{16,18},{20,22},{24,26},{28,30},{32,34}... | collective-permute-start | bytes 98312 | tf_op jit(solution)/shard_map/ppermute | solution.py:571
  91.3 12.3 %all-to-all-start.1 = ((bf16[8,72,128]{2,1,0:T(8,128)(2,1)}), bf16[8,72,128]{2,1,0:T(8,128)(2,1)S(1)}, u32[]{:S(2)}, u32[]{:S(2)}) async-start(bf16[8,72,128]{2,1,0:T(8,128)(2,1)} %broadcast_in_dim.32), calls=%async_computation.1 | async-start | bytes 294912 | tf_op jit(solution)/shard_map/all_to_all | solution.py:601
  94.7 9.0 %collective-permute-start.15 = (bf16[128,128]{1,0:T(8,128)(2,1)S(1)}, bf16[128,128]{1,0:T(8,128)(2,1)S(1)}, u32[]{:S(2)}, u32[]{:S(2)}) collective-permute-start(bf16[128,128]{1,0:T(8,128)(2,1)S(1)} %pad_maximum_fusion.6), channel_id=1, source_target_pairs={{0,8},{2,10},{4,12},{6,14},{16,24},{18,26},{20,28},{22,30},{32,40}... | collective-permute-start | bytes 98312 | tf_op jit(solution)/shard_map/ppermute | solution.py:571
  104.4 15.9 %all-to-all-start.2 = ((bf16[16,72,128]{2,1,0:T(8,128)(2,1)}), bf16[16,72,128]{2,1,0:T(8,128)(2,1)S(1)}, u32[]{:S(2)}, u32[]{:S(2)}) async-start(bf16[16,72,128]{2,1,0:T(8,128)(2,1)} %broadcast_in_dim.33), calls=%async_computation.2 | async-start | bytes 589824 | tf_op jit(solution)/shard_map/all_to_all | solution.py:601
  109.6 10.6 %collective-permute-start.16 = (bf16[128,128]{1,0:T(8,128)(2,1)S(1)}, bf16[128,128]{1,0:T(8,128)(2,1)S(1)}, u32[]{:S(2)}, u32[]{:S(2)}) collective-permute-start(bf16[128,128]{1,0:T(8,128)(2,1)S(1)} %pad_maximum_fusion.7), channel_id=1, source_target_pairs={{8,16},{10,18},{12,20},{14,22},{24,32},{26,34},{28,36},{30,38},{40... | collective-permute-start | bytes 98312 | tf_op jit(solution)/shard_map/ppermute | solution.py:571
  120.3 1.6 %collective-permute-start.17 = (bf16[1152,128]{1,0:T(8,128)(2,1)S(1)}, bf16[1152,128]{1,0:T(8,128)(2,1)S(1)}, u32[]{:S(2)}, u32[]{:S(2)}) collective-permute-start(bf16[1152,128]{1,0:T(8,128)(2,1)S(1)} %bitcast.62), channel_id=1, source_target_pairs={{0,2},{2,0},{1,3},{3,1},{4,6},{6,4},{5,7},{7,5},{8,10},{10,8},{9,1... | collective-permute-start | bytes 884744 | tf_op jit(solution)/shard_map/ppermute | solution.py:589
